TPU v7x, 512 devices: a whole 4x4x16 slice. The times are simulated.
512 devices in a mesh: depth: 64 (over y_lo, z, core), grp: 8 (over y_hi, x).
Axes of the slice: x: 4, y: 4 (y_hi: 2, y_lo: 2; y = y_hi * 2 + y_lo), z: 16, core: 2. Of those that a mesh axis runs over, the one named last changes fastest.
Arguments:
- inputs: bfloat16 [16, 128, 128, 256], P(None, 'depth', 'grp'), may hold values from -6 to 6
- weight_two: bfloat16 [3, 3, 3, 32, 16], replicated, may hold values from -0.3125 to 0.3125
- weight_three: bfloat16 [3, 3, 3, 64, 32], P(None, None, None, 'grp'), may hold values from -0.21875 to 0.21875
- cotangent: bfloat16 [64, 64, 64, 128], P('grp', 'depth'), may hold values from -6 to 6
Outputs:
- input_grad: bfloat16 [16, 128, 128, 256], P(None, 'depth', 'grp')
- weight_grad_two: float32 [3, 3, 3, 32, 16], replicated
- weight_grad_three: float32 [3, 3, 3, 64, 32], P(None, None, None, 'grp')
All inputs are finite; a program needn't handle non-finite values.
Results may differ from a plain program's by a relative error of at most 0.02.
Values may be sent and summed in bfloat16 or wider, within the bound.
No kernel may reach another device: no remote copies, remote signals or barrier semaphores. Data moves between devices by JAX's collectives and lax.ppermute only.
A program may use at most 128 MiB of HBM per device.

v0:
```python
import math

import jax
import jax.numpy as jnp
from jax import lax
from jax.sharding import PartitionSpec as P


def extended(cells, sides, width):
    for axis, dim in sides:
        count = lax.axis_size(axis)
        ends = count - 1
        head = lax.slice_in_dim(cells, 0, width, axis=dim)
        tail = lax.slice_in_dim(cells, cells.shape[dim] - width, cells.shape[dim], axis=dim)
        cells = jnp.concatenate(
            [
                lax.ppermute(tail, axis, [(i, (i + 1) % count) for i in range(ends)]),
                cells,
                lax.ppermute(head, axis, [((i + 1) % count, i) for i in range(ends)]),
            ],
            axis=dim,
        )
    return cells


def activate(values):
    return 0.3 * values + 0.7 * jax.nn.softplus(values)


def derivative(values):
    return 0.3 + 0.7 * jax.nn.sigmoid(values)


def stack_taps(padded, depth_off, flipped):
    planes = padded.shape[1] - 2
    height = padded.shape[2] - 2
    breadth = padded.shape[3] - 2
    windows = []
    for row_off in range(3):
        for col_off in range(3):
            if flipped:
                start_d, start_h, start_w = (2 - depth_off, 2 - row_off, 2 - col_off)
            else:
                start_d, start_h, start_w = (depth_off, row_off, col_off)
            windows.append(
                padded[
                    :,
                    start_d : start_d + planes,
                    start_h : start_h + height,
                    start_w : start_w + breadth,
                ]
            )
    return jnp.concatenate(windows, axis=0)


def convolve(padded, weights):
    filters, chans = (weights.shape[3], weights.shape[4])
    summed = None
    for depth_off in range(3):
        taps = stack_taps(padded, depth_off, False)
        matrix = jnp.transpose(weights[depth_off], (2, 0, 1, 3)).reshape(filters, 9 * chans)
        term = jnp.einsum("fk,kdhw->fdhw", matrix, taps, preferred_element_type=jnp.float32)
        summed = term if summed is None else summed + term
    return summed


def convolve_back(padded, weights):
    filters, chans = (weights.shape[3], weights.shape[4])
    summed = None
    for depth_off in range(3):
        taps = stack_taps(padded, depth_off, True)
        matrix = jnp.transpose(weights[depth_off], (3, 0, 1, 2)).reshape(chans, 9 * filters)
        term = jnp.einsum("ck,kdhw->cdhw", matrix, taps, preferred_element_type=jnp.float32)
        summed = term if summed is None else summed + term
    return summed


def filter_grad(grads, padded):
    filters = grads.shape[0]
    chans = padded.shape[0]
    pieces = []
    for depth_off in range(3):
        taps = stack_taps(padded, depth_off, False)
        product = jnp.einsum("fdhw,kdhw->fk", grads, taps, preferred_element_type=jnp.float32)
        pieces.append(jnp.transpose(product.reshape(filters, 3, 3, chans), (1, 2, 0, 3)))
    return jnp.stack(pieces)


def on_device(inputs, weight_two, weight_three, cotangent):
    padded_in = extended(inputs, (("depth", 1), ("grp", 2)), 1)
    padded_in = jnp.pad(padded_in, ((0, 0), (0, 0), (0, 0), (1, 1)))
    pre_two = convolve(padded_in, weight_two)
    filters, planes, height, breadth = pre_two.shape
    cells = planes * lax.axis_size("depth") * height * lax.axis_size("grp") * breadth
    shaped = activate(pre_two).reshape(filters, planes // 2, 2, height // 2, 2, breadth // 2, 2)
    pooled = shaped.mean(axis=(2, 4, 6)).astype(jnp.bfloat16)
    scale_three = 1.0 / math.sqrt(cells / 8)
    columns = lax.all_gather(pooled, "grp", axis=2, tiled=True)
    padded_pool = extended(columns, (("depth", 1),), 1)
    padded_pool = jnp.pad(padded_pool, ((0, 0), (0, 0), (1, 1), (1, 1)))
    pre_three = convolve(padded_pool, weight_three)
    grad_three = (cotangent.astype(jnp.float32) * derivative(pre_three)).astype(jnp.bfloat16)
    local_three = filter_grad(grad_three, padded_pool)
    cot_pad = extended(grad_three, (("depth", 1),), 1)
    widened = jnp.pad(cot_pad, ((0, 0), (0, 0), (1, 1), (1, 1)))
    partial_terms = convolve_back(widened, weight_three)
    pooled_grad = lax.psum_scatter(
        partial_terms.astype(jnp.bfloat16), "grp", scatter_dimension=2, tiled=True
    ).astype(jnp.float32)
    weight_grad_three = lax.psum(local_three, "depth") * scale_three
    spread = jnp.broadcast_to(pooled_grad[:, :, None, :, None, :, None], shaped.shape).reshape(
        pre_two.shape
    )
    grad_two = (spread * 0.125 * derivative(pre_two)).astype(jnp.bfloat16)
    grad_pad = extended(grad_two, (("depth", 1), ("grp", 2)), 1)
    grad_pad = jnp.pad(grad_pad, ((0, 0), (0, 0), (0, 0), (1, 1)))
    input_grad = convolve_back(grad_pad, weight_two).astype(jnp.bfloat16)
    local_two = filter_grad(grad_two, padded_in)
    scale_two = 1.0 / math.sqrt(cells)
    weight_grad_two = lax.psum(local_two, ("depth", "grp")) * scale_two
    return (input_grad, weight_grad_two, weight_grad_three)


def solution(mesh):
    placed = (
        P(None, "depth", "grp", None),
        P(),
        P(None, None, None, "grp", None),
        P("grp", "depth", None, None),
    )
    return jax.shard_map(
        on_device,
        mesh=mesh,
        in_specs=placed,
        out_specs=(P(None, "depth", "grp", None), P(), P(None, None, None, "grp", None)),
        check_vma=False,
    )
```

profile of v0, /device:TPU:1, one launch (start us, length us, event | category | flops | bytes accessed | tf_op | source)
XLA Modules:
  0.0 489.2 jit_solution(16164769346820233200)
XLA Ops:
  7.2 1.1 copy.92
  8.3 4.9 %collective-permute-start = (bf16[16,1,16,256]{3,0,2,1:T(8,128)(2,1)S(1)}, bf16[16,1,16,256]{3,0,2,1:T(8,128)(2,1)S(1)}, u32[]{:S(2)}, u32[]{:S(2)}) collective-permute-start(bf16[16,1,16,256]{3,0,2,1:T(8,128)(2,1)S(1)} %get-tuple-element.120), channel_id=1, source_target_pairs={{0,8},{8,16},{16,24},{24,32},{32,40},{40,48},{48,56},{56,64},{64,7... | collective-permute-start | bytes 393224 | tf_op jit(solution)/shard_map/ppermute | solution.py:17
  13.3 5.1 %collective-permute-start.1 = (bf16[16,1,16,256]{3,0,2,1:T(8,128)(2,1)S(1)}, bf16[16,1,16,256]{3,0,2,1:T(8,128)(2,1)S(1)}, u32[]{:S(2)}, u32[]{:S(2)}) collective-permute-start(bf16[16,1,16,256]{3,0,2,1:T(8,128)(2,1)S(1)} %get-tuple-element.119), channel_id=1, source_target_pairs={{8,0},{16,8},{24,16},{32,24},{40,32},{48,40},{56,48},{64,56},{72,6... | collective-permute-start | bytes 393224 | tf_op jit(solution)/shard_map/ppermute | solution.py:19
  18.5 1.1 constant_dynamic-update-slice_fusion.1
  19.6 3.1 collective-permute-start.2
  22.7 1.3 collective-permute-start.3
  24.0 1.5 slice_bitcast_fusion.5
  25.5 1.9 collective-permute-done.3
  31.2 0.8 copy-done.4
  32.1 2.0 fusion.67
  34.1 1.9 copy.101
  36.0 3.4 reduce_sum.18
  39.7 29.8 %all-gather = bf16[32,64,128]{2,0,1:T(8,128)(2,1)S(1)} all-gather(bf16[32,8,128]{2,0,1:T(8,128)(2,1)S(1)} %copy.103), channel_id=2, replica_groups=mesh['depth'=64,'grp'=8] {'grp'}, dimensions={1}, use_global_device_ids=true | all-gather | bytes 589824 | tf_op jit(solution)/shard_map/all_gather | solution.py:98
  69.4 6.6 %collective-permute-start.5 = (bf16[32,1,64,128]{3,0,2,1:T(8,128)(2,1)S(1)}, bf16[32,1,64,128]{3,0,2,1:T(8,128)(2,1)S(1)}, u32[]{:S(2)}, u32[]{:S(2)}) collective-permute-start(bf16[32,1,64,128]{3,0,2,1:T(8,128)(2,1)S(1)} %bitcast.226), channel_id=1, source_target_pairs={{8,0},{16,8},{24,16},{32,24},{40,32},{48,40},{56,48},{64,56},{72,6... | collective-permute-start | bytes 1572872 | tf_op jit(solution)/shard_map/ppermute | solution.py:19
  76.0 4.4 collective-permute-start.4
  80.4 1.4 fusion.101
  82.5 0.7 copy.105
  84.6 0.8 copy.112
  86.3 3.2 select_maximum_fusion
  90.4 0.9 slice_dynamic-update-slice_fusion.45
  91.8 1.1 constant_dynamic-update-slice_fusion.4
  94.9 0.8 slice_dynamic-update-slice_fusion.40
  97.9 0.8 fusion.62
  99.4 1.9 collective-permute-start.7
  101.3 4.7 collective-permute-start.6
  106.0 2.9 convolution_bitcast_fusion.1
  111.8 1.2 fusion.24
  113.0 5.3 %convolution_bitcast_fusion = f32[1,3,3,8,32]{4,3,2,1,0:T(8,128)S(1)} fusion(bf16[3,3,32,64,128]{4,2,1,0,3:T(8,128)(2,1)} %bitcast.222, bf16[8,1,64,128]{3,0,2,1:T(8,128)(2,1)S(1)} %fusion.62), kind=kOutput, calls=%fused_computation.65 | convolution fusion | flops 37748736 | bytes 4858880 | tf_op jit(solution)/shard_map/fdhw,kdhw->fk/dot_general | solution.py:84
  118.2 5.3 %convolution_bitcast_fusion.2 = f32[1,3,3,8,32]{4,3,2,1,0:T(8,128)S(1)} fusion(bf16[3,3,32,64,128]{4,2,1,0,3:T(8,128)(2,1)} %bitcast.221, bf16[8,1,64,128]{3,0,2,1:T(8,128)(2,1)S(1)} %fusion.62), kind=kOutput, calls=%fused_computation.67 | convolution fusion | flops 37748736 | bytes 4858880 | tf_op jit(solution)/shard_map/fdhw,kdhw->fk/dot_general | solution.py:84
  123.6 210.9 %psum.15 = f32[3,3,3,8,32]{4,3,2,1,0:T(8,128)S(1)} all-reduce(f32[3,3,3,8,32]{4,3,2,1,0:T(8,128)S(1)} %pad_maximum_fusion.8), channel_id=1, replica_groups=mesh['depth'=64,'grp'=8] {'depth'}, use_global_device_ids=true, to_apply=%region_4.5 | all-reduce | flops 6912 | bytes 55296 | tf_op jit(solution)/shard_map/psum | solution.py:110
  335.1 0.9 multiply_bitcast_fusion
  336.2 2.2 broadcast_in_dim.8
  338.3 2.2 copy.111
  340.5 1.6 multiply_convert_fusion
  342.1 2.4 fusion.105
  344.5 0.7 fusion.104
  345.3 3.6 collective-permute-start.8
  348.9 4.0 collective-permute-start.9
  352.9 0.7 fusion.103
  353.7 112.2 %psum.14 = f32[3,3,3,32,16]{3,4,2,1,0:T(8,128)S(1)} all-reduce(f32[3,3,3,32,16]{3,4,2,1,0:T(8,128)S(1)} %pad_maximum_fusion.7), channel_id=1, replica_groups=mesh['depth'=64,'grp'=8] {'depth','grp'}, use_global_device_ids=true, to_apply=%region_3.4 | all-reduce | flops 13824 | bytes 110592 | tf_op jit(solution)/shard_map/psum | solution.py:120
  466.0 3.0 collective-permute-start.10
  469.0 1.6 collective-permute-start.11
  471.3 2.7 collective-permute-done.11
  474.0 1.6 select_maximum_fusion.2
  478.8 0.9 fusion.95
  479.7 0.9 fusion.93
  480.6 0.9 fusion.34
  481.6 0.8 copy.121
  (113 shorter events, 20.6 us)
Async XLA Ops:
  7.2 328.0 %reduce-scatter.2.cloned.1.call-start = ((), (), s32[]{:S(2)}) async-start(), calls=%async_computation.1 | async-start | bytes 589824 | tf_op jit(solution)/shard_map/reduce_scatter | solution.py:107
  8.3 10.1 %collective-permute-start = (bf16[16,1,16,256]{3,0,2,1:T(8,128)(2,1)S(1)}, bf16[16,1,16,256]{3,0,2,1:T(8,128)(2,1)S(1)}, u32[]{:S(2)}, u32[]{:S(2)}) collective-permute-start(bf16[16,1,16,256]{3,0,2,1:T(8,128)(2,1)S(1)} %get-tuple-element.120), channel_id=1, source_target_pairs={{0,8},{8,16},{16,24},{24,32},{32,40},{40,48},{48,56},{56,64},{64,7... | collective-permute-start | bytes 393224 | tf_op jit(solution)/shard_map/ppermute | solution.py:17
  13.3 6.3 %collective-permute-start.1 = (bf16[16,1,16,256]{3,0,2,1:T(8,128)(2,1)S(1)}, bf16[16,1,16,256]{3,0,2,1:T(8,128)(2,1)S(1)}, u32[]{:S(2)}, u32[]{:S(2)}) collective-permute-start(bf16[16,1,16,256]{3,0,2,1:T(8,128)(2,1)S(1)} %get-tuple-element.119), channel_id=1, source_target_pairs={{8,0},{16,8},{24,16},{32,24},{40,32},{48,40},{56,48},{64,56},{72,6... | collective-permute-start | bytes 393224 | tf_op jit(solution)/shard_map/ppermute | solution.py:19
  19.6 5.9 %collective-permute-start.2 = (bf16[16,4,1,256]{3,0,2,1:T(8,128)(2,1)S(1)}, bf16[16,4,1,256]{3,0,2,1:T(8,128)(2,1)S(1)}, u32[]{:S(2)}, u32[]{:S(2)}) collective-permute-start(bf16[16,4,1,256]{3,0,2,1:T(8,128)(2,1)S(1)} %get-tuple-element.115), channel_id=1, source_target_pairs={{0,1},{1,2},{2,3},{3,4},{4,5},{5,6},{6,7},{8,9},{9,10},{10,11},{11... | collective-permute-start | bytes 98312 | tf_op jit(solution)/shard_map/ppermute | solution.py:17
  22.7 4.7 collective-permute-start.3
  27.9 1.0 copy-start.5
  29.8 1.4 copy-start.2
  29.8 2.2 copy-start.4
  69.4 16.9 %collective-permute-start.5 = (bf16[32,1,64,128]{3,0,2,1:T(8,128)(2,1)S(1)}, bf16[32,1,64,128]{3,0,2,1:T(8,128)(2,1)S(1)}, u32[]{:S(2)}, u32[]{:S(2)}) collective-permute-start(bf16[32,1,64,128]{3,0,2,1:T(8,128)(2,1)S(1)} %bitcast.226), channel_id=1, source_target_pairs={{8,0},{16,8},{24,16},{32,24},{40,32},{48,40},{56,48},{64,56},{72,6... | collective-permute-start | bytes 1572872 | tf_op jit(solution)/shard_map/ppermute | solution.py:19
  76.0 10.3 %collective-permute-start.4 = (bf16[32,1,64,128]{3,0,2,1:T(8,128)(2,1)S(1)}, bf16[32,1,64,128]{3,0,2,1:T(8,128)(2,1)}, u32[]{:S(2)}, u32[]{:S(2)}) collective-permute-start(bf16[32,1,64,128]{3,0,2,1:T(8,128)(2,1)S(1)} %bitcast.227), channel_id=1, source_target_pairs={{0,8},{8,16},{16,24},{24,32},{32,40},{40,48},{48,56},{56,64},{64,7... | collective-permute-start | bytes 1572872 | tf_op jit(solution)/shard_map/ppermute | solution.py:17
  94.9 1.2 copy-start.12
  95.7 2.2 copy-start
  96.0 3.3 copy-start.1
  96.0 0.7 copy-start.11
  96.8 1.1 copy-start.6
  96.8 1.1 copy-start.10
  99.4 9.5 %collective-permute-start.7 = (bf16[8,1,64,128]{3,0,2,1:T(8,128)(2,1)S(1)}, bf16[8,1,64,128]{3,0,2,1:T(8,128)(2,1)S(1)}, u32[]{:S(2)}, u32[]{:S(2)}) collective-permute-start(bf16[8,1,64,128]{3,0,2,1:T(8,128)(2,1)S(1)} %fusion.62), channel_id=1, source_target_pairs={{8,0},{16,8},{24,16},{32,24},{40,32},{48,40},{56,48},{64,56},{72,6... | collective-permute-start | bytes 393224 | tf_op jit(solution)/shard_map/ppermute | solution.py:19
  101.3 7.6 %collective-permute-start.6 = (bf16[8,1,64,128]{3,0,2,1:T(8,128)(2,1)S(1)}, bf16[8,1,64,128]{3,0,2,1:T(8,128)(2,1)S(1)}, u32[]{:S(2)}, u32[]{:S(2)}) collective-permute-start(bf16[8,1,64,128]{3,0,2,1:T(8,128)(2,1)S(1)} %fusion.62), channel_id=1, source_target_pairs={{0,8},{8,16},{16,24},{24,32},{32,40},{40,48},{48,56},{56,64},{64,7... | collective-permute-start | bytes 393224 | tf_op jit(solution)/shard_map/ppermute | solution.py:17
  109.9 1.1 copy-start.7
  110.4 1.0 copy-start.8
  344.5 8.5 %copy-start.3 = (bf16[144,2,16,256]{3,0,2,1:T(8,128)(2,1)S(1)}, bf16[144,2,16,256]{3,0,2,1:T(8,128)(2,1)}, u32[]{:S(2)}) copy-start(bf16[144,2,16,256]{3,0,2,1:T(8,128)(2,1)} %copy-done.2) | copy-start | bytes 7077892
  345.3 120.7 %collective-permute-start.8 = (bf16[32,1,16,256]{3,0,2,1:T(8,128)(2,1)S(1)}, bf16[32,1,16,256]{3,0,2,1:T(8,128)(2,1)S(1)}, u32[]{:S(2)}, u32[]{:S(2)}) collective-permute-start(bf16[32,1,16,256]{3,0,2,1:T(8,128)(2,1)S(1)} %get-tuple-element.113), channel_id=1, source_target_pairs={{0,8},{8,16},{16,24},{24,32},{32,40},{40,48},{48,56},{56,64},{64,7... | collective-permute-start | bytes 786440 | tf_op jit(solution)/shard_map/ppermute | solution.py:17
  348.9 117.1 %collective-permute-start.9 = (bf16[32,1,16,256]{3,0,2,1:T(8,128)(2,1)S(1)}, bf16[32,1,16,256]{3,0,2,1:T(8,128)(2,1)S(1)}, u32[]{:S(2)}, u32[]{:S(2)}) collective-permute-start(bf16[32,1,16,256]{3,0,2,1:T(8,128)(2,1)S(1)} %get-tuple-element.114), channel_id=1, source_target_pairs={{8,0},{16,8},{24,16},{32,24},{40,32},{48,40},{56,48},{64,56},{72,6... | collective-permute-start | bytes 786440 | tf_op jit(solution)/shard_map/ppermute | solution.py:19
  466.0 5.3 %collective-permute-start.10 = (bf16[32,4,1,256]{3,0,2,1:T(8,128)(2,1)S(1)}, bf16[32,4,1,256]{3,0,2,1:T(8,128)(2,1)S(1)}, u32[]{:S(2)}, u32[]{:S(2)}) collective-permute-start(bf16[32,4,1,256]{3,0,2,1:T(8,128)(2,1)S(1)} %get-tuple-element.61), channel_id=1, source_target_pairs={{0,1},{1,2},{2,3},{3,4},{4,5},{5,6},{6,7},{8,9},{9,10},{10,11},{11... | collective-permute-start | bytes 196616 | tf_op jit(solution)/shard_map/ppermute | solution.py:17
  469.0 5.0 %collective-permute-start.11 = (bf16[32,4,1,256]{3,0,2,1:T(8,128)(2,1)S(1)}, bf16[32,4,1,256]{3,0,2,1:T(8,128)(2,1)S(1)}, u32[]{:S(2)}, u32[]{:S(2)}) collective-permute-start(bf16[32,4,1,256]{3,0,2,1:T(8,128)(2,1)S(1)} %get-tuple-element.62), channel_id=1, source_target_pairs={{1,0},{2,1},{3,2},{4,3},{5,4},{6,5},{7,6},{9,8},{10,9},{11,10},{12... | collective-permute-start | bytes 196616 | tf_op jit(solution)/shard_map/ppermute | solution.py:19
  479.7 0.9 copy-start.9
Sparse Core Ops, SparseCore 0:
  113.1 93.1 reduce-scatter.1
where the time goes:
time: 495 us; the launch traced here: 489 us
  blocking collectives  353 us (71%)
  starting transfers between devices  44.3 us (9%)
  local copies, waits for them, and re-layouts  31.7 us (6%)
  matrix products  27.2 us (5%)
  between operations  14.9 us (3%)
  other arithmetic  13.5 us (3%)
    psum x1, blocking collectives, on_device(): weight_grad_three = lax.psum(local_three, 'depth') * scale_three  211 us
    psum x1, blocking collectives, on_device(): weight_grad_two = lax.psum(local_two, ('depth', 'grp')) * scale_two  112 us
    all_gather x1, blocking collectives, on_device(): columns = lax.all_gather(pooled, 'grp', axis=2, tiled=True)  29.8 us
    ppermute x6, starting transfers between devices, extended(): lax.ppermute(tail, axis, [(i, (i + 1) % count) for i in range(ends)])  23.7 us
    ppermute x6, starting transfers between devices, extended(): lax.ppermute(head, axis, [((i + 1) % count, i) for i in range(ends)])  20.5 us
    dot_general x6, matrix products, filter_grad(): jnp.einsum('fdhw,kdhw->fk', grads, taps, preferred_element_type=jnp.float32)  17.4 us
    unnamed x64, local copies, waits for them, and re-layouts  15.7 us
  transfers between devices with their start and end apart: 13, of which 2 were waited for; matrix products, arithmetic and copies ran while one was open for 5% of the time, Pallas kernels for 0%

commit v1 on v0

v1 whole, which is shorter than its diff:
```python
import functools
import math

import jax
import jax.numpy as jnp
import numpy as np
from jax import lax
from jax.experimental import pallas as pl
from jax.experimental.pallas import tpu as pltpu
from jax.sharding import PartitionSpec as P


F32 = jnp.float32
BF16 = jnp.bfloat16
BREADTH = 128


def call(kernel, outs, scratch, args, flops, scalars=0):
    specs = [pl.BlockSpec(memory_space=pltpu.SMEM)] * scalars
    specs += [pl.BlockSpec(memory_space=pltpu.VMEM)] * (len(args) - scalars)
    moved = sum(math.prod(a.shape) * a.dtype.itemsize for a in list(args) + list(outs))
    return pl.pallas_call(
        kernel,
        out_shape=outs,
        in_specs=specs,
        out_specs=[pl.BlockSpec(memory_space=pltpu.VMEM)] * len(outs),
        scratch_shapes=scratch,
        compiler_params=pltpu.CompilerParams(vmem_limit_bytes=32 * 1024 * 1024),
        cost_estimate=pl.CostEstimate(flops=flops, bytes_accessed=moved, transcendentals=0),
    )(*args)


def dot(left, right):
    return jnp.dot(left, right, preferred_element_type=F32)


def dot_nt(left, right):
    return lax.dot_general(left, right, (((1,), (1,)), ((), ())), preferred_element_type=F32)


def indicator(shape, test):
    row = lax.broadcasted_iota(jnp.int32, shape, 0)
    col = lax.broadcasted_iota(jnp.int32, shape, 1)
    return jnp.where(test(row, col), 1.0, 0.0).astype(BF16)


def splitter():
    def test(row, col):
        part, at = col // BREADTH, col % BREADTH
        return row == 2 * at + part - 1

    return indicator((2 * BREADTH, 4 * BREADTH), test)


def shifter():
    def test(row, col):
        part, at = col // BREADTH, col % BREADTH
        return row == at + 2 * part - 1

    return indicator((BREADTH, 2 * BREADTH), test)


def joiner():
    def test(row, col):
        return col == 2 * (row % BREADTH) + row // BREADTH

    return indicator((2 * BREADTH, 2 * BREADTH), test)


def forward_two(first_ref, count_ref, own, below, above, top, bottom, weight, pooled, slope, parts, split):
    split[...] = splitter()
    edge = top.shape[0]
    height = own.shape[0]

    def place(row, block):
        cells = dot(block, split[...]).astype(BF16)
        for part in range(4):
            parts[row, part * 64 : part * 64 + 64, :] = cells[:, part * BREADTH : (part + 1) * BREADTH]

    def middle(row, carry):
        block = jnp.concatenate([below[row], own[row, 0], own[row, 1], above[row]], axis=0)
        place(row + edge, block)
        return carry

    lax.fori_loop(0, height, middle, 0, unroll=2)

    def ends(row, carry):
        place(row, top[row].reshape(64, 2 * BREADTH))
        place(row + edge + height, bottom[row].reshape(64, 2 * BREADTH))
        return carry

    lax.fori_loop(0, edge, ends, 0)

    def one(row, keep):
        cells = parts[pl.ds(2 * row, 4)].reshape(1024, BREADTH)
        pre = dot(weight[...], cells)
        small = jnp.exp(-jnp.abs(pre))
        whole = 1.0 + small
        value = 0.3 * pre + 0.7 * (jnp.maximum(pre, 0.0) + jnp.log(whole))
        summed = jnp.sum(value.reshape(8, 32, BREADTH), axis=0) * 0.125
        at = first_ref[0] + row
        inside = jnp.logical_and(at >= 0, at < count_ref[0])
        pooled[row] = jnp.where(inside, summed, 0.0).astype(BF16)
        if keep:
            slope[row - 2] = 0.3 + 0.7 * (jnp.where(pre >= 0.0, 1.0, small) / whole)

    rows = pooled.shape[0]
    for row in (0, 1, rows - 2, rows - 1):
        one(row, False)

    def inner(row, carry):
        one(row, True)
        return carry

    lax.fori_loop(2, rows - 2, inner, 0, unroll=2)


def forward_three(below, own, above, cot, weight, grads, parts, shift):
    shift[...] = shifter()
    rows = own.shape[0]
    for plane, ref in enumerate((below, own, above)):

        def place(row, carry, plane=plane, ref=ref):
            block = ref[row]
            moved = dot(block, shift[...]).astype(BF16)
            at = plane * 32
            parts[row, at : at + 32, :] = moved[:, :BREADTH]
            parts[row, 96 + at : 96 + at + 32, :] = block
            parts[row, 192 + at : 192 + at + 32, :] = moved[:, BREADTH:]
            return carry

        lax.fori_loop(0, rows, place, 0, unroll=2)

    def one(row, carry):
        pre = dot(weight[...], parts[pl.ds(row, 3)].reshape(864, BREADTH))
        small = jnp.exp(-jnp.abs(pre))
        slope = 0.3 + 0.7 * (jnp.where(pre >= 0.0, 1.0, small) / (1.0 + small))
        grads[row] = (cot[row].astype(F32) * slope).astype(BF16)
        return carry

    lax.fori_loop(0, rows - 2, one, 0, unroll=2)


def filters_three(grads, parts, out):
    left = jnp.concatenate([grads[row] for row in range(2, 10)], axis=1)
    for off in range(3):
        right = jnp.concatenate([parts[row + off] for row in range(2, 10)], axis=1)
        out[off] = dot_nt(left, right)


def backward_three(first_ref, count_ref, below, own, above, slope, weight, grads, parts, shift):
    shift[...] = shifter()
    rows = own.shape[0]
    for plane, ref in enumerate((below, own, above)):

        def place(row, carry, plane=plane, ref=ref):
            block = ref[row]
            moved = dot(block, shift[...]).astype(BF16)
            at = plane * 64
            parts[row, at : at + 64, :] = moved[:, :BREADTH]
            parts[row, 192 + at : 192 + at + 64, :] = block
            parts[row, 384 + at : 384 + at + 64, :] = moved[:, BREADTH:]
            return carry

        lax.fori_loop(0, rows, place, 0, unroll=2)

    def one(row, carry):
        pool = dot(weight[...], parts[pl.ds(row, 3)].reshape(1728, BREADTH))
        at = first_ref[0] + row
        inside = jnp.logical_and(at >= 0, at < count_ref[0])
        pool = jnp.where(inside, pool, 0.0) * 0.125
        full = pool[None] * slope[row].reshape(8, 32, BREADTH)
        grads[row] = full.astype(BF16).reshape(256, BREADTH)
        return carry

    lax.fori_loop(0, rows - 2, one, 0, unroll=2)


def filters_two(grads, parts, out):
    left = jnp.concatenate([grads[row] for row in range(1, 9)], axis=1)
    blocks = []
    for off in range(4):
        right = jnp.concatenate([parts[2 * row + 4 + off] for row in range(1, 9)], axis=1)
        blocks.append(dot_nt(left, right))
    total = jnp.concatenate(
        [jnp.zeros((32, 256), F32)] * 3, axis=1
    )
    for phase in range(8):
        deep, high, wide = phase // 4, (phase // 2) % 2, phase % 2
        part = jnp.concatenate(
            [block[phase * 32 : phase * 32 + 32] for block in blocks[high : high + 3]], axis=1
        )
        move = (wide * 4 + deep) * 16
        if move:
            part = pltpu.roll(part, 768 - move, 1)
        total = total + part
    out[...] = total


def backward_two(own, below, above, weight, out, parts, shift, join):
    shift[...] = shifter()
    join[...] = joiner()

    def place(row, carry):
        for high in range(2):
            for deep in range(4):
                ref, at = ((below, 0), (own, 0), (own, 128), (above, 0))[deep]
                at = at + high * 64
                even = ref[row, at : at + 32, :]
                odd = ref[row, at + 32 : at + 64, :]
                left = dot(odd, shift[:, :BREADTH]).astype(BF16)
                right = dot(even, shift[:, BREADTH:]).astype(BF16)
                for part, block in enumerate((left, even, odd, right)):
                    to = part * 128 + deep * 32
                    parts[2 * row + high, to : to + 32, :] = block
        return carry

    lax.fori_loop(0, own.shape[0], place, 0)

    def one(row, carry):
        cells = dot(weight[...], parts[pl.ds(2 * row + 1, 4)].reshape(2048, BREADTH)).astype(BF16)
        both = jnp.concatenate([cells[:64], cells[64:]], axis=1)
        out[row] = dot(both, join[...]).astype(BF16)
        return carry

    lax.fori_loop(0, out.shape[0], one, 0, unroll=2)


def tap_choice(back):
    chosen = np.full((8, 64), 27, np.int32)
    for phase in range(8):
        deep, high, wide = phase // 4, (phase // 2) % 2, phase % 2
        for place in range(64):
            b, e, a = place // 16 - high, (place // 4) % 4 - wide, place % 4 - deep
            if min(a, b, e) >= 0 and max(a, b, e) <= 2:
                if back:
                    a, b, e = 2 - a, 2 - b, 2 - e
                chosen[phase, place] = a * 9 + b * 3 + e
    return chosen


def taps_two(weight, back):
    taps = weight.reshape(27, 32, 16)
    if back:
        taps = jnp.transpose(taps, (0, 2, 1))
    outs, ins = taps.shape[1:]
    pick = jnp.asarray(np.eye(28)[tap_choice(back)][..., :27], BF16)
    full = jnp.einsum("pkt,tfc->pfkc", pick, taps, preferred_element_type=F32).astype(BF16)
    if back:
        full = jnp.transpose(full.reshape(2, 2, 2, outs, 64 * ins), (2, 0, 1, 3, 4))
    return full.reshape(8 * outs, 64 * ins)


def shifted(axis, step):
    count = lax.axis_size(axis)
    return [(i, i + step) for i in range(count) if 0 <= i + step < count]


def neighbours(first, last, axis):
    return (
        lax.ppermute(last, axis, shifted(axis, 1)),
        lax.ppermute(first, axis, shifted(axis, -1)),
    )


def exchange(blocks, axis):
    return lax.all_to_all(blocks, axis, 0, 0, tiled=True)


def summed_parts(total, axis):
    return jnp.sum(exchange(total, axis), axis=0)


def gathered(block, axis):
    count = lax.axis_size(axis)
    return exchange(jnp.broadcast_to(block[None], (count,) + block.shape), axis)


def on_device(inputs, weight_two, weight_three, cotangent):
    groups = lax.axis_size("grp")
    slabs = lax.axis_size("depth")
    group = lax.axis_index("grp")
    chans, planes, height, breadth = inputs.shape
    cells = planes * slabs * height * groups * breadth
    pool_rows = height // 2
    count = jnp.full((1,), pool_rows * groups, jnp.int32)
    share = weight_three.shape[3]
    filters = share * groups

    own = jnp.transpose(inputs, (2, 1, 0, 3))
    below, above = neighbours(own[:, 0], own[:, 1], "depth")

    def edge(lo):
        return jnp.concatenate(
            [below[lo : lo + 7, None], own[lo : lo + 7], above[lo : lo + 7, None]], axis=1
        )

    top, bottom = neighbours(edge(0), edge(height - 7), "grp")

    padded = jnp.pad(cotangent[:, 0], ((0, 0), (2, 2), (0, 0)))
    rows_out = jnp.stack(
        [
            padded[:, pool_rows * to : pool_rows * to + pool_rows + 4].reshape(-1, BREADTH)
            for to in range(groups)
        ]
    )
    weights_out = jnp.broadcast_to(
        weight_three.reshape(1, -1, BREADTH), (groups, weight_three.size // BREADTH, BREADTH)
    )
    arrived = exchange(jnp.concatenate([rows_out, weights_out], axis=1), "grp")
    cut = share * (pool_rows + 4)
    cot = jnp.transpose(arrived[:, :cut].reshape(filters, pool_rows + 4, BREADTH), (1, 0, 2))
    taps = arrived[:, cut:].reshape(groups, 3, 3, 3, share, 32)
    weight_fwd = jnp.transpose(taps, (0, 4, 2, 3, 1, 5)).reshape(filters, 864)
    weight_back = jnp.transpose(
        taps[:, ::-1, ::-1, ::-1], (5, 2, 3, 1, 0, 4)
    ).reshape(32, 27 * filters)

    first = (pool_rows * group - 3).astype(jnp.int32).reshape(1)
    pooled, slope, parts_two = call(
        forward_two,
        [
            jax.ShapeDtypeStruct((pool_rows + 6, 32, BREADTH), BF16),
            jax.ShapeDtypeStruct((pool_rows + 2, 256, BREADTH), F32),
            jax.ShapeDtypeStruct((height + 14, 256, BREADTH), BF16),
        ],
        [pltpu.VMEM((2 * BREADTH, 4 * BREADTH), BF16)],
        (first, count, own, below, above, top, bottom, taps_two(weight_two, False)),
        2 * 14 * 256 * 1024 * 128,
        scalars=2,
    )

    pool_below, pool_above = neighbours(pooled, pooled, "depth")
    shift = pltpu.VMEM((BREADTH, 2 * BREADTH), BF16)
    grads, parts_three = call(
        forward_three,
        [
            jax.ShapeDtypeStruct((pool_rows + 4, filters, BREADTH), BF16),
            jax.ShapeDtypeStruct((pool_rows + 6, 288, BREADTH), BF16),
        ],
        [shift],
        (pool_below, pooled, pool_above, cot, weight_fwd),
        2 * 12 * 64 * 864 * 128,
    )

    grads_below, grads_above = neighbours(grads, grads, "depth")
    (local_three,) = call(
        filters_three,
        [jax.ShapeDtypeStruct((3, filters, 288), F32)],
        [],
        (grads, parts_three),
        2 * 8 * 64 * 864 * 128,
    )
    (grad_two,) = call(
        backward_three,
        [jax.ShapeDtypeStruct((pool_rows + 2, 256, BREADTH), BF16)],
        [pltpu.VMEM((pool_rows + 4, 576, BREADTH), BF16), shift],
        (first + 2, count, grads_below, grads, grads_above, slope, weight_back),
        2 * 10 * 32 * 1728 * 128,
        scalars=2,
    )

    two_below, two_above = neighbours(grad_two[:, :128], grad_two[:, 128:], "depth")
    (local_two,) = call(
        filters_two,
        [jax.ShapeDtypeStruct((32, 768), F32)],
        [],
        (grad_two, parts_two),
        2 * 8 * 256 * 1024 * 128,
    )
    (back,) = call(
        backward_two,
        [jax.ShapeDtypeStruct((pool_rows, 64, 2 * BREADTH), BF16)],
        [
            pltpu.VMEM((height + 4, 512, BREADTH), BF16),
            shift,
            pltpu.VMEM((2 * BREADTH, 2 * BREADTH), BF16),
        ],
        (grad_two, two_below, two_above, taps_two(weight_two, True)),
        2 * 8 * 128 * 2048 * 128,
    )
    input_grad = jnp.transpose(
        back.reshape(pool_rows, 2, 2, chans, breadth), (3, 1, 0, 2, 4)
    ).reshape(inputs.shape)

    three = jnp.transpose(
        local_three.reshape(3, groups, share, 3, 3, 32), (1, 4, 0, 3, 2, 5)
    ).reshape(groups, -1, BREADTH)
    two = jnp.transpose(
        local_two.reshape(32, 3, 4, 4, 16)[:, :, :3, :3], (3, 1, 2, 0, 4)
    ).reshape(-1, BREADTH)
    size_two = two.shape[0]
    piece = -(-size_two // groups)
    two = jnp.pad(two, ((0, piece * groups - size_two), (0, 0))).reshape(groups, piece, BREADTH)
    mine = summed_parts(jnp.concatenate([three, two], axis=1), "grp")
    mine = gathered(summed_parts(mine.reshape(slabs, -1), "depth"), "depth").reshape(-1, BREADTH)
    rows_three = three.shape[1]
    weight_grad_three = mine[:rows_three].reshape(3, 3, 3, share, 32) * (1.0 / math.sqrt(cells / 8))
    full = gathered(mine[rows_three:], "grp").reshape(-1, BREADTH)[:size_two]
    weight_grad_two = full.reshape(3, 3, 3, 32, 16) * (1.0 / math.sqrt(cells))
    return (input_grad, weight_grad_two, weight_grad_three)


def solution(mesh):
    placed = (
        P(None, "depth", "grp", None),
        P(),
        P(None, None, None, "grp", None),
        P("grp", "depth", None, None),
    )
    return jax.shard_map(
        on_device,
        mesh=mesh,
        in_specs=placed,
        out_specs=(P(None, "depth", "grp", None), P(), P(None, None, None, "grp", None)),
        check_vma=False,
    )
```

time: 495 us -> 163 us (0.33)
  blocking collectives: 353 us -> 16.9 us
  matrix products: 27.2 us -> 2.85 us
  Pallas kernels: 0 us -> 21.8 us
  starting transfers between devices: 44.3 us -> 61.4 us
  between operations: 14.9 us -> 1.3 us
  other arithmetic: 13.5 us -> 3.37 us
  waiting for transfers between devices: 4.7 us -> 14.7 us
  local copies, waits for them, and re-layouts: 31.7 us -> 39.7 us
    psum x2 -> x0, blocking collectives: 323 us -> none  [the longest x1 211 us: on_device(): weight_grad_three = lax.psum(local_three, 'depth') * scale_three]
    all_gather x1 -> x0, blocking collectives: 29.8 us -> none  [on_device(): columns = lax.all_gather(pooled, 'grp', axis=2, tiled=True)]
    all_to_all x0 -> x4, starting transfers between devices: none -> 28.9 us  [exchange(): return lax.all_to_all(blocks, axis, 0, 0, tiled=True)]
    dot_general x18 -> x2, matrix products: 27.2 us -> 2.85 us  [taps_two(): jnp.einsum('pkt,tfc->pfkc', pick, taps, preferred_element_type=F32)]
    pallas_call x0 -> x6, Pallas kernels: none -> 21.8 us  [call(): pl.pallas_call(kernel, out_shape=outs, in_specs=specs, out_specs=[pl.Bloc...]
    all_to_all x0 -> x1, blocking collectives: none -> 16.9 us  [exchange(): return lax.all_to_all(blocks, axis, 0, 0, tiled=True)]
    all_to_all x0 -> x4, waiting for transfers between devices: none -> 14.7 us  [exchange(): return lax.all_to_all(blocks, axis, 0, 0, tiled=True)]
    ppermute x12 -> x10, starting transfers between devices: 44.2 us -> 32.5 us  [the longest x5 17.3 us: neighbours(): lax.ppermute(first, axis, shifted(axis, -1))]
  transfers between devices with their start and end apart: 13 -> 14, of which waited for: 2 -> 3; matrix products, arithmetic and copies ran while one was open for 5% -> 22% of each run, Pallas kernels for 0% -> 8%
where the time goes in v1:
time: 163 us; the launch traced here: 162 us
  starting transfers between devices  61.4 us (38%)
  local copies, waits for them, and re-layouts  39.7 us (24%)
  Pallas kernels  21.8 us (13%)
  blocking collectives  16.9 us (10%)
  waiting for transfers between devices  14.7 us (9%)
  other arithmetic  3.37 us (2%)
  matrix products  2.85 us (2%)
    all_to_all x4, starting transfers between devices, exchange(): return lax.all_to_all(blocks, axis, 0, 0, tiled=True)  28.9 us
    pallas_call x6, Pallas kernels, call(): pl.pallas_call(kernel, out_shape=outs, in_specs=specs, out_specs=[pl.Bloc...  21.8 us
    ppermute x5, starting transfers between devices, neighbours(): lax.ppermute(first, axis, shifted(axis, -1))  17.3 us
    all_to_all x1, blocking collectives, exchange(): return lax.all_to_all(blocks, axis, 0, 0, tiled=True)  16.9 us
    ppermute x5, starting transfers between devices, neighbours(): lax.ppermute(last, axis, shifted(axis, 1))  15.3 us
    all_to_all x4, waiting for transfers between devices, exchange(): return lax.all_to_all(blocks, axis, 0, 0, tiled=True)  14.7 us
    unnamed x29, local copies, waits for them, and re-layouts  6.67 us
    convert_element_type x2, local copies, waits for them, and re-layouts, taps_two(): jnp.einsum('pkt,tfc->pfkc', pick, taps, preferred_element_type=F32)  6.21 us
  transfers between devices with their start and end apart: 14, of which 3 were waited for; matrix products, arithmetic and copies ran while one was open for 22% of the time, Pallas kernels for 8%

profile of v1, /device:TPU:1, one launch (start us, length us, event | category | flops | bytes accessed | tf_op | source)
XLA Modules:
  0.0 162.1 jit_solution(15189714006212665566)
XLA Ops:
  0.6 1.1 copy.66
  1.8 8.8 %collective-permute-start.1 = (bf16[16,16,256]{2,1,0:T(8,128)(2,1)S(1)}, bf16[16,16,256]{2,1,0:T(8,128)(2,1)S(1)}, u32[]{:S(2)}, u32[]{:S(2)}) collective-permute-start(bf16[16,16,256]{2,1,0:T(8,128)(2,1)S(1)} %get-tuple-element.23), channel_id=1, source_target_pairs={{8,0},{16,8},{24,16},{32,24},{40,32},{48,40},{56,48},{64,56},{72,6... | collective-permute-start | bytes 393224 | tf_op jit(solution)/shard_map/ppermute | solution.py:262
  10.6 1.9 %collective-permute-start = (bf16[16,16,256]{2,1,0:T(8,128)(2,1)S(1)}, bf16[16,16,256]{2,1,0:T(8,128)(2,1)S(1)}, u32[]{:S(2)}, u32[]{:S(2)}) collective-permute-start(bf16[16,16,256]{2,1,0:T(8,128)(2,1)S(1)} %get-tuple-element.24), channel_id=1, source_target_pairs={{0,8},{8,16},{16,24},{24,32},{32,40},{40,48},{48,56},{56,64},{64,7... | collective-permute-start | bytes 393224 | tf_op jit(solution)/shard_map/ppermute | solution.py:261
  12.5 0.9 broadcast_in_dim.35
  13.4 1.1 pad_slice_fusion
  15.7 4.2 %all-to-all-start = ((bf16[8,150,128]{2,1,0:T(8,128)(2,1)}), bf16[8,150,128]{2,1,0:T(8,128)(2,1)}, u32[]{:S(2)}, u32[]{:S(2)}) async-start(bf16[8,150,128]{2,1,0:T(8,128)(2,1)} %pad_maximum_fusion), calls=%async_computation | async-start | bytes 622592 | tf_op jit(solution)/shard_map/all_to_all | solution.py:267
  20.9 3.9 %collective-permute-start.2 = (bf16[7,4,16,256]{3,2,0,1:T(8,128)(2,1)}, bf16[7,4,16,256]{3,2,0,1:T(8,128)(2,1)}, u32[]{:S(2)}, u32[]{:S(2)}) collective-permute-start(bf16[7,4,16,256]{3,2,0,1:T(8,128)(2,1)} %pad_maximum_fusion.2), channel_id=1, source_target_pairs={{0,1},{1,2},{2,3},{3,4},{4,5},{5,6},{6,7},{8,9},{9,10},{10,11},{11... | collective-permute-start | bytes 688136 | tf_op jit(solution)/shard_map/ppermute | solution.py:261
  25.5 1.3 collective-permute-start.3
  26.8 1.4 fusion
  28.4 4.2 %copy.43 = bf16[8,32,64,16]{1,0,3,2:T(8,128)(2,1)S(1)} copy(bf16[8,32,64,16]{2,1,3,0:T(8,128)(2,1)} %fusion) | data formatting | bytes 1048576 | tf_op jit(solution)/shard_map/convert_element_type | solution.py:248
  32.6 1.5 reshape.83
  34.3 1.0 copy.45.top
  35.3 6.5 %shard_map.85 = (bf16[14,32,128]{2,1,0:T(8,128)(2,1)S(1)}, f32[10,256,128]{2,1,0:T(8,128)S(1)}, bf16[30,256,128]{2,1,0:T(8,128)(2,1)S(1)}) custom-call(s32[1]{0:T(128)} %bitcast.first_ref, s32[1]{0:T(128)} %constant.9.clone.1.count_ref, bf16[16,2,16,256]{3,2,1,0:T(8,128)(2,1)S(1)} %copy.44.own, bf16[16,16,256]{2,1,0:T(8,128)(2,1)S(1)} %collective-permute-done.below, ...), custom_call_target="tpu_custom_call" | custom-call | flops 939524096 | bytes 4898824 | tf_op jit(solution)/shard_map/pallas_call | solution.py:22
  41.8 1.1 copy-done
  42.9 3.0 %collective-permute-start.5 = (bf16[14,32,128]{2,1,0:T(8,128)(2,1)S(1)}, bf16[14,32,128]{2,1,0:T(8,128)(2,1)S(1)}, u32[]{:S(2)}, u32[]{:S(2)}) collective-permute-start(bf16[14,32,128]{2,1,0:T(8,128)(2,1)S(1)} %get-tuple-element.8.own), channel_id=1, source_target_pairs={{8,0},{16,8},{24,16},{32,24},{40,32},{48,40},{56,48},{64,56},{72,6... | collective-permute-start | bytes 344072 | tf_op jit(solution)/shard_map/ppermute | solution.py:262
  45.8 2.6 %collective-permute-start.4 = (bf16[14,32,128]{2,1,0:T(8,128)(2,1)S(1)}, bf16[14,32,128]{2,1,0:T(8,128)(2,1)S(1)}, u32[]{:S(2)}, u32[]{:S(2)}) collective-permute-start(bf16[14,32,128]{2,1,0:T(8,128)(2,1)S(1)} %get-tuple-element.8.own), channel_id=1, source_target_pairs={{0,8},{8,16},{16,24},{24,32},{32,40},{40,48},{48,56},{56,64},{64,7... | collective-permute-start | bytes 344072 | tf_op jit(solution)/shard_map/ppermute | solution.py:261
  48.4 0.9 slice.116
  49.5 0.9 slice.117
  50.6 1.1 copy.48
  51.7 1.5 reshape.86.weight
  53.3 4.4 %shard_map.86 = (bf16[12,64,128]{2,1,0:T(8,128)(2,1)S(1)}, bf16[14,288,128]{2,1,0:T(8,128)(2,1)S(1)}) custom-call(bf16[14,32,128]{2,1,0:T(8,128)(2,1)S(1)} %collective-permute-done.4.below, bf16[14,32,128]{2,1,0:T(8,128)(2,1)S(1)} %get-tuple-element.8.own, bf16[14,32,128]{2,1,0:T(8,128)(2,1)S(1)} %collective-permute-done.5.above, ...), custom_call_target="tpu_custom_call" | custom-call | flops 169869312 | bytes 1880064 | tf_op jit(solution)/shard_map/pallas_call | solution.py:22
  57.7 1.0 copy-done.2
  58.6 1.9 %collective-permute-start.7 = (bf16[12,64,128]{2,1,0:T(8,128)(2,1)S(1)}, bf16[12,64,128]{2,1,0:T(8,128)(2,1)S(1)}, u32[]{:S(2)}, u32[]{:S(2)}) collective-permute-start(bf16[12,64,128]{2,1,0:T(8,128)(2,1)S(1)} %get-tuple-element.9.own.grads), channel_id=1, source_target_pairs={{8,0},{16,8},{24,16},{32,24},{40,32},{48,40},{56,48},{64,56},{72,6... | collective-permute-start | bytes 589832 | tf_op jit(solution)/shard_map/ppermute | solution.py:262
  60.5 3.6 %collective-permute-start.6 = (bf16[12,64,128]{2,1,0:T(8,128)(2,1)S(1)}, bf16[12,64,128]{2,1,0:T(8,128)(2,1)S(1)}, u32[]{:S(2)}, u32[]{:S(2)}) collective-permute-start(bf16[12,64,128]{2,1,0:T(8,128)(2,1)S(1)} %get-tuple-element.9.own.grads), channel_id=1, source_target_pairs={{0,8},{8,16},{16,24},{24,32},{32,40},{40,48},{48,56},{56,64},{64,7... | collective-permute-start | bytes 589832 | tf_op jit(solution)/shard_map/ppermute | solution.py:261
  64.2 1.1 reverse_bitcast_fusion
  65.6 1.2 copy-done.3
  67.5 1.5 reshape.92
  69.0 2.3 %copy.55 = f32[8,3,3,3,8,32]{5,4,3,2,1,0:T(8,128)} copy(f32[8,3,3,3,8,32]{5,1,3,4,0,2:T(4,128)} %bitcast.72) | data formatting | bytes 442368 | tf_op jit(solution)/shard_map/transpose | solution.py:386
  71.2 2.1 %reshape.93 = f32[8,54,128]{2,1,0:T(8,128)} reshape(f32[8,3,3,3,8,32]{5,4,3,2,1,0:T(8,128)} %copy.55) | data formatting | bytes 442368 | tf_op jit(solution)/shard_map/reshape | solution.py:388
  73.3 1.3 copy-done.1
  74.6 4.1 %shard_map.87.own.grads = bf16[10,256,128]{2,1,0:T(8,128)(2,1)S(1)} custom-call(s32[1]{0:T(128)S(6)} %add.8.first_ref, s32[1]{0:T(128)} %constant.9.clone.1.count_ref, bf16[12,64,128]{2,1,0:T(8,128)(2,1)S(1)} %collective-permute-done.6.below, bf16[12,64,128]{2,1,0:T(8,128)(2,1)S(1)} %get-tuple-element.9.own.grads, ...), custom_call_target="tpu_custom_call" | custom-call | flops 141557760 | bytes 2666504 | tf_op jit(solution)/shard_map/pallas_call | solution.py:22
  78.8 0.8 shard_map.90
  80.3 16.9 %all_to_all.30 = f32[8,68,128]{2,1,0:T(8,128)S(1)} all-to-all(f32[8,68,128]{2,1,0:T(8,128)S(1)} %pad_maximum_fusion.1), channel_id=1, replica_groups=mesh['depth'=64,'grp'=8] {'grp'}, dimensions={0} | all-to-all | bytes 557056 | tf_op jit(solution)/shard_map/all_to_all | solution.py:267
  98.0 15.7 %all-to-all-start.2 = ((f32[64,1,136]{2,1,0:T(1,128)}), f32[64,1,136]{2,1,0:T(1,128)S(1)}, u32[]{:S(2)}, u32[]{:S(2)}) async-start(f32[64,1,136]{2,1,0:T(1,128)} %all_to_all.21), calls=%async_computation.2 | async-start | bytes 131072 | tf_op jit(solution)/shard_map/all_to_all | solution.py:267
  113.7 0.9 fusion.4
  114.6 2.4 %collective-permute-start.9 = (bf16[10,128,128]{2,1,0:T(8,128)(2,1)}, bf16[10,128,128]{2,1,0:T(8,128)(2,1)S(1)}, u32[]{:S(2)}, u32[]{:S(2)}) collective-permute-start(bf16[10,128,128]{2,1,0:T(8,128)(2,1)} %get-tuple-element.19), channel_id=1, source_target_pairs={{8,0},{16,8},{24,16},{32,24},{40,32},{48,40},{56,48},{64,56},{72,6... | collective-permute-start | bytes 983048 | tf_op jit(solution)/shard_map/ppermute | solution.py:262
  117.0 3.2 %collective-permute-start.8 = (bf16[10,128,128]{2,1,0:T(8,128)(2,1)}, bf16[10,128,128]{2,1,0:T(8,128)(2,1)S(1)}, u32[]{:S(2)}, u32[]{:S(2)}) collective-permute-start(bf16[10,128,128]{2,1,0:T(8,128)(2,1)} %get-tuple-element.20), channel_id=1, source_target_pairs={{0,8},{8,16},{16,24},{24,32},{32,40},{40,48},{48,56},{56,64},{64,7... | collective-permute-start | bytes 983048 | tf_op jit(solution)/shard_map/ppermute | solution.py:261
  120.2 8.1 %all-to-all-done.2 = f32[64,1,136]{2,1,0:T(1,128)S(1)} async-done(((f32[64,1,136]{2,1,0:T(1,128)}), f32[64,1,136]{2,1,0:T(1,128)S(1)}, u32[]{:S(2)}, u32[]{:S(2)}) %all-to-all-start.2) | async-done | bytes 34848 | tf_op jit(solution)/shard_map/all_to_all | solution.py:267
  129.1 5.7 %all-to-all-start.3 = ((f32[64,1,136]{2,1,0:T(1,128)}), f32[64,1,136]{2,1,0:T(1,128)}, u32[]{:S(2)}, u32[]{:S(2)}) async-start(f32[64,1,136]{2,1,0:T(1,128)} %broadcast_in_dim.37), calls=%async_computation.3 | async-start | bytes 131072 | tf_op jit(solution)/shard_map/all_to_all | solution.py:267
  134.8 1.4 fusion.1
  136.2 2.0 %copy.52 = bf16[8,16,64,32]{3,2,1,0:T(8,128)(2,1)S(1)} copy(bf16[8,16,64,32]{2,3,1,0:T(8,128)(2,1)} %fusion.1) | data formatting | bytes 1048576 | tf_op jit(solution)/shard_map/convert_element_type | solution.py:248
  138.2 3.0 %reshape.88 = bf16[2,2,2,16,2048]{4,3,2,1,0:T(8,128)(2,1)} reshape(bf16[8,16,64,32]{3,2,1,0:T(8,128)(2,1)S(1)} %copy.52) | data formatting | bytes 1048576 | tf_op jit(solution)/shard_map/reshape | solution.py:250
  141.1 1.1 copy.53
  142.3 5.3 %shard_map.88 = bf16[8,64,256]{2,1,0:T(8,128)(2,1)S(1)} custom-call(bf16[10,256,128]{2,1,0:T(8,128)(2,1)S(1)} %shard_map.87.own.grads, bf16[10,128,128]{2,1,0:T(8,128)(2,1)S(1)} %collective-permute-done.8.below, bf16[10,128,128]{2,1,0:T(8,128)(2,1)S(1)} %collective-permute-done.9.above, bf16[128,2048]{1,0:T(8,128)(2,1)S(1)} %bitcast.69), custom_call_target="tpu_custom_call" | custom-call | flops 536870912 | bytes 2097152 | tf_op jit(solution)/shard_map/pallas_call | solution.py:22
  149.2 1.0 reduce.1
  151.0 3.4 %all-to-all-start.4 = ((f32[8,14,128]{2,1,0:T(8,128)}), f32[8,14,128]{2,1,0:T(8,128)S(1)}, u32[]{:S(2)}, u32[]{:S(2)}) async-start(f32[8,14,128]{2,1,0:T(8,128)} %broadcast_in_dim.38), calls=%async_computation.4 | async-start | bytes 131072 | tf_op jit(solution)/shard_map/all_to_all | solution.py:267
  155.1 5.9 %all-to-all-done.4 = f32[8,14,128]{2,1,0:T(8,128)S(1)} async-done(((f32[8,14,128]{2,1,0:T(8,128)}), f32[8,14,128]{2,1,0:T(8,128)S(1)}, u32[]{:S(2)}, u32[]{:S(2)}) %all-to-all-start.4) | async-done | bytes 57376 | tf_op jit(solution)/shard_map/all_to_all | solution.py:267
  161.2 0.9 copy.58
  (82 shorter events, 9.9 us)
Async XLA Ops:
  0.6 19.2 %copy-start.7 = (bf16[3,3,3,32,16]{3,4,2,1,0:T(8,128)(2,1)S(1)}, bf16[3,3,3,32,16]{3,4,2,1,0:T(8,128)(2,1)}, u32[]{:S(2)}) copy-start(bf16[3,3,3,32,16]{3,4,2,1,0:T(8,128)(2,1)} %param.7) | copy-start | bytes 82948
  1.8 18.3 %collective-permute-start.1 = (bf16[16,16,256]{2,1,0:T(8,128)(2,1)S(1)}, bf16[16,16,256]{2,1,0:T(8,128)(2,1)S(1)}, u32[]{:S(2)}, u32[]{:S(2)}) collective-permute-start(bf16[16,16,256]{2,1,0:T(8,128)(2,1)S(1)} %get-tuple-element.23), channel_id=1, source_target_pairs={{8,0},{16,8},{24,16},{32,24},{40,32},{48,40},{56,48},{64,56},{72,6... | collective-permute-start | bytes 393224 | tf_op jit(solution)/shard_map/ppermute | solution.py:262
  10.6 9.6 %collective-permute-start = (bf16[16,16,256]{2,1,0:T(8,128)(2,1)S(1)}, bf16[16,16,256]{2,1,0:T(8,128)(2,1)S(1)}, u32[]{:S(2)}, u32[]{:S(2)}) collective-permute-start(bf16[16,16,256]{2,1,0:T(8,128)(2,1)S(1)} %get-tuple-element.24), channel_id=1, source_target_pairs={{0,8},{8,16},{16,24},{24,32},{32,40},{40,48},{48,56},{56,64},{64,7... | collective-permute-start | bytes 393224 | tf_op jit(solution)/shard_map/ppermute | solution.py:261
  14.6 12.2 %copy-start.9 = (bf16[8,64,27,1]{1,2,3,0:T(8,128)(2,1)S(1)}, bf16[8,64,27,1]{1,2,3,0:T(8,128)(2,1)}, u32[]{:S(2)}) copy-start(bf16[8,64,27,1]{1,2,3,0:T(8,128)(2,1)} %constant.35) | copy-start | bytes 82948
  15.7 12.6 %copy-start.5 = (bf16[16,2,16,256]{3,2,1,0:T(8,128)(2,1)S(1)}, bf16[16,2,16,256]{3,2,1,0:T(8,128)(2,1)}, u32[]{:S(2)}) copy-start(bf16[16,2,16,256]{3,2,1,0:T(8,128)(2,1)} %param.6) | copy-start | bytes 786436
  15.7 32.8 %all-to-all-start = ((bf16[8,150,128]{2,1,0:T(8,128)(2,1)}), bf16[8,150,128]{2,1,0:T(8,128)(2,1)}, u32[]{:S(2)}, u32[]{:S(2)}) async-start(bf16[8,150,128]{2,1,0:T(8,128)(2,1)} %pad_maximum_fusion), calls=%async_computation | async-start | bytes 622592 | tf_op jit(solution)/shard_map/all_to_all | solution.py:267
  20.9 13.4 %collective-permute-start.2 = (bf16[7,4,16,256]{3,2,0,1:T(8,128)(2,1)}, bf16[7,4,16,256]{3,2,0,1:T(8,128)(2,1)}, u32[]{:S(2)}, u32[]{:S(2)}) collective-permute-start(bf16[7,4,16,256]{3,2,0,1:T(8,128)(2,1)} %pad_maximum_fusion.2), channel_id=1, source_target_pairs={{0,1},{1,2},{2,3},{3,4},{4,5},{5,6},{6,7},{8,9},{9,10},{10,11},{11... | collective-permute-start | bytes 688136 | tf_op jit(solution)/shard_map/ppermute | solution.py:261
  25.5 9.8 %collective-permute-start.3 = (bf16[7,4,16,256]{3,2,1,0:T(8,128)(2,1)}, bf16[7,4,16,256]{3,2,1,0:T(8,128)(2,1)S(1)}, u32[]{:S(2)}, u32[]{:S(2)}) collective-permute-start(bf16[7,4,16,256]{3,2,1,0:T(8,128)(2,1)} %pad_maximum_fusion.3), channel_id=1, source_target_pairs={{1,0},{2,1},{3,2},{4,3},{5,4},{6,5},{7,6},{9,8},{10,9},{11,10},{12... | collective-permute-start | bytes 688136 | tf_op jit(solution)/shard_map/ppermute | solution.py:262
  41.8 1.1 copy-start
  42.9 10.4 %collective-permute-start.5 = (bf16[14,32,128]{2,1,0:T(8,128)(2,1)S(1)}, bf16[14,32,128]{2,1,0:T(8,128)(2,1)S(1)}, u32[]{:S(2)}, u32[]{:S(2)}) collective-permute-start(bf16[14,32,128]{2,1,0:T(8,128)(2,1)S(1)} %get-tuple-element.8.own), channel_id=1, source_target_pairs={{8,0},{16,8},{24,16},{32,24},{40,32},{48,40},{56,48},{64,56},{72,6... | collective-permute-start | bytes 344072 | tf_op jit(solution)/shard_map/ppermute | solution.py:262
  45.8 7.4 %collective-permute-start.4 = (bf16[14,32,128]{2,1,0:T(8,128)(2,1)S(1)}, bf16[14,32,128]{2,1,0:T(8,128)(2,1)S(1)}, u32[]{:S(2)}, u32[]{:S(2)}) collective-permute-start(bf16[14,32,128]{2,1,0:T(8,128)(2,1)S(1)} %get-tuple-element.8.own), channel_id=1, source_target_pairs={{0,8},{8,16},{16,24},{24,32},{32,40},{40,48},{48,56},{56,64},{64,7... | collective-permute-start | bytes 344072 | tf_op jit(solution)/shard_map/ppermute | solution.py:261
  50.6 7.0 %copy-start.4 = (bf16[8,3,3,3,8,32]{5,4,3,2,1,0:T(8,128)(2,1)}, bf16[8,3,3,3,8,32]{5,4,3,2,1,0:T(8,128)(2,1)S(1)}, u32[]{:S(2)}) copy-start(bf16[8,3,3,3,8,32]{5,4,3,2,1,0:T(8,128)(2,1)S(1)} %reshape.85) | copy-start | bytes 331780
  57.7 1.0 copy-start.2
  58.6 14.7 %collective-permute-start.7 = (bf16[12,64,128]{2,1,0:T(8,128)(2,1)S(1)}, bf16[12,64,128]{2,1,0:T(8,128)(2,1)S(1)}, u32[]{:S(2)}, u32[]{:S(2)}) collective-permute-start(bf16[12,64,128]{2,1,0:T(8,128)(2,1)S(1)} %get-tuple-element.9.own.grads), channel_id=1, source_target_pairs={{8,0},{16,8},{24,16},{32,24},{40,32},{48,40},{56,48},{64,56},{72,6... | collective-permute-start | bytes 589832 | tf_op jit(solution)/shard_map/ppermute | solution.py:262
  60.5 12.8 %collective-permute-start.6 = (bf16[12,64,128]{2,1,0:T(8,128)(2,1)S(1)}, bf16[12,64,128]{2,1,0:T(8,128)(2,1)S(1)}, u32[]{:S(2)}, u32[]{:S(2)}) collective-permute-start(bf16[12,64,128]{2,1,0:T(8,128)(2,1)S(1)} %get-tuple-element.9.own.grads), channel_id=1, source_target_pairs={{0,8},{8,16},{16,24},{24,32},{32,40},{40,48},{48,56},{56,64},{64,7... | collective-permute-start | bytes 589832 | tf_op jit(solution)/shard_map/ppermute | solution.py:261
  65.6 1.2 copy-start.3
  73.3 1.3 copy-start.1
  78.8 1.5 copy-start.6
  80.0 54.7 %copy-start.8 = (bf16[8,64,27,1]{1,2,3,0:T(8,128)(2,1)S(1)}, bf16[8,64,27,1]{1,2,3,0:T(8,128)(2,1)}, u32[]{:S(2)}) copy-start(bf16[8,64,27,1]{1,2,3,0:T(8,128)(2,1)} %constant.36) | copy-start | bytes 82948
  98.0 30.3 %all-to-all-start.2 = ((f32[64,1,136]{2,1,0:T(1,128)}), f32[64,1,136]{2,1,0:T(1,128)S(1)}, u32[]{:S(2)}, u32[]{:S(2)}) async-start(f32[64,1,136]{2,1,0:T(1,128)} %all_to_all.21), calls=%async_computation.2 | async-start | bytes 131072 | tf_op jit(solution)/shard_map/all_to_all | solution.py:267
  114.6 27.6 %collective-permute-start.9 = (bf16[10,128,128]{2,1,0:T(8,128)(2,1)}, bf16[10,128,128]{2,1,0:T(8,128)(2,1)S(1)}, u32[]{:S(2)}, u32[]{:S(2)}) collective-permute-start(bf16[10,128,128]{2,1,0:T(8,128)(2,1)} %get-tuple-element.19), channel_id=1, source_target_pairs={{8,0},{16,8},{24,16},{32,24},{40,32},{48,40},{56,48},{64,56},{72,6... | collective-permute-start | bytes 983048 | tf_op jit(solution)/shard_map/ppermute | solution.py:262
  117.0 25.3 %collective-permute-start.8 = (bf16[10,128,128]{2,1,0:T(8,128)(2,1)}, bf16[10,128,128]{2,1,0:T(8,128)(2,1)S(1)}, u32[]{:S(2)}, u32[]{:S(2)}) collective-permute-start(bf16[10,128,128]{2,1,0:T(8,128)(2,1)} %get-tuple-element.20), channel_id=1, source_target_pairs={{0,8},{8,16},{16,24},{24,32},{32,40},{40,48},{48,56},{56,64},{64,7... | collective-permute-start | bytes 983048 | tf_op jit(solution)/shard_map/ppermute | solution.py:261
  129.1 20.2 %all-to-all-start.3 = ((f32[64,1,136]{2,1,0:T(1,128)}), f32[64,1,136]{2,1,0:T(1,128)}, u32[]{:S(2)}, u32[]{:S(2)}) async-start(f32[64,1,136]{2,1,0:T(1,128)} %broadcast_in_dim.37), calls=%async_computation.3 | async-start | bytes 131072 | tf_op jit(solution)/shard_map/all_to_all | solution.py:267
  151.0 10.0 %all-to-all-start.4 = ((f32[8,14,128]{2,1,0:T(8,128)}), f32[8,14,128]{2,1,0:T(8,128)S(1)}, u32[]{:S(2)}, u32[]{:S(2)}) async-start(f32[8,14,128]{2,1,0:T(8,128)} %broadcast_in_dim.38), calls=%async_computation.4 | async-start | bytes 131072 | tf_op jit(solution)/shard_map/all_to_all | solution.py:267

commit v2 on v1

v2 whole, which is shorter than its diff:
```python
import functools
import math

import jax
import jax.numpy as jnp
from jax import lax
from jax.experimental import pallas as pl
from jax.experimental.pallas import tpu as pltpu
from jax.sharding import PartitionSpec as P


F32 = jnp.float32
BF16 = jnp.bfloat16
BREADTH = 128


def call(kernel, outs, scratch, args, flops, scalars=0):
    specs = [pl.BlockSpec(memory_space=pltpu.SMEM)] * scalars
    specs += [pl.BlockSpec(memory_space=pltpu.VMEM)] * (len(args) - scalars)
    moved = sum(math.prod(a.shape) * a.dtype.itemsize for a in list(args) + list(outs))
    return pl.pallas_call(
        kernel,
        out_shape=outs,
        in_specs=specs,
        out_specs=[pl.BlockSpec(memory_space=pltpu.VMEM)] * len(outs),
        scratch_shapes=scratch,
        compiler_params=pltpu.CompilerParams(vmem_limit_bytes=16 * 1024 * 1024),
        cost_estimate=pl.CostEstimate(flops=flops, bytes_accessed=moved, transcendentals=0),
    )(*args)


def dot(left, right):
    return jnp.dot(left, right, preferred_element_type=F32)


def dot_nt(left, right):
    return lax.dot_general(left, right, (((1,), (1,)), ((), ())), preferred_element_type=F32)


def indicator(shape, test):
    row = lax.broadcasted_iota(jnp.int32, shape, 0)
    col = lax.broadcasted_iota(jnp.int32, shape, 1)
    return jnp.where(test(row, col), 1.0, 0.0).astype(BF16)


def splitter():
    def test(row, col):
        part, at = col // BREADTH, col % BREADTH
        return row == 2 * at + part - 1

    return indicator((2 * BREADTH, 4 * BREADTH), test)


def shifter():
    def test(row, col):
        part, at = col // BREADTH, col % BREADTH
        return row == at + 2 * part - 1

    return indicator((BREADTH, 2 * BREADTH), test)


def joiner():
    def test(row, col):
        return col == 2 * (row % BREADTH) + row // BREADTH

    return indicator((2 * BREADTH, 2 * BREADTH), test)


def weights_two(plain, turned, ahead, back):
    def blocks(source, outs, ins, flip):
        per = BREADTH // ins
        total = []
        for part in range(64 // per):
            summed = jnp.zeros((outs, BREADTH), F32)
            for at in range(per):
                place = part * per + at
                b, e, a = place // 16, (place // 4) % 4, place % 4
                if max(a, b, e) > 2:
                    continue
                if flip:
                    a, b, e = 2 - a, 2 - b, 2 - e
                spread = indicator((ins, BREADTH), lambda row, col: col == row + at * ins)
                summed = summed + dot(source[a * 9 + b * 3 + e], spread)
            total.append(summed)
        return jnp.concatenate(total, axis=1)

    def phases(out, base, outs, ins, row_of):
        for phase in range(8):
            deep, high, wide = phase // 4, (phase // 2) % 2, phase % 2
            move = (high * 16 + wide * 4 + deep) * ins
            full = pltpu.roll(base, move, 1) if move else base
            at = row_of(deep, high, wide) * outs
            out[at : at + outs, :] = full.astype(BF16)

    phases(ahead, blocks(plain, 32, 16, False), 32, 16, lambda d, h, w: d * 4 + h * 2 + w)
    phases(back, blocks(turned, 16, 32, True), 16, 32, lambda d, h, w: w * 4 + d * 2 + h)


def forward_two(first_ref, count_ref, own, below, above, top, bottom, weight, pooled, slope, parts, split):
    split[...] = splitter()
    edge = top.shape[0]
    height = own.shape[0]

    def place(row, many, block):
        cells = dot(block, split[...]).astype(BF16).reshape(many, 64, 4 * BREADTH)
        for part in range(4):
            to = part * 64
            parts[row : row + many, to : to + 64, :] = cells[:, :, part * BREADTH : (part + 1) * BREADTH]

    for row in range(0, height, 4):
        block = [ref[at] for at in range(row, row + 4) for ref in (below, own.at[:, 0], own.at[:, 1], above)]
        place(row + edge, 4, jnp.concatenate(block, axis=0))
    for ref, to in ((top, 0), (bottom, edge + height)):
        for row, many in ((0, 4), (4, edge - 4)):
            place(to + row, many, ref[row : row + many].reshape(many * 64, 2 * BREADTH))

    rows = pooled.shape[0]
    for row in range(0, rows, 2):
        cells = [parts[2 * at : 2 * at + 4].reshape(1024, BREADTH) for at in (row, row + 1)]
        pre = dot(weight[...], jnp.concatenate(cells, axis=1))
        small = jnp.exp(-jnp.abs(pre))
        whole = 1.0 + small
        value = 0.3 * pre + 0.7 * (jnp.maximum(pre, 0.0) + jnp.log(whole))
        summed = jnp.sum(value.reshape(8, 32, 2 * BREADTH), axis=0) * 0.125
        for off in range(2):
            at = first_ref[0] + row + off
            inside = jnp.logical_and(at >= 0, at < count_ref[0])
            half = summed[:, off * BREADTH : (off + 1) * BREADTH]
            pooled[row + off] = jnp.where(inside, half, 0.0).astype(BF16)
        if 2 <= row < rows - 2:
            rate = 0.3 + 0.7 * (jnp.where(pre >= 0.0, 1.0, small) / whole)
            slope[row - 2] = rate[:, :BREADTH]
            slope[row - 1] = rate[:, BREADTH:]


def place_shifted(refs, parts, shift, chans):
    span = 3 * chans
    rows = refs[0].shape[0]
    step = 256 // chans
    for plane, ref in enumerate(refs):
        at = plane * chans
        for row in range(0, rows, step):
            many = min(step, rows - row)
            block = ref[row : row + many]
            moved = dot(block.reshape(many * chans, BREADTH), shift[...]).astype(BF16)
            moved = moved.reshape(many, chans, 2 * BREADTH)
            parts[row : row + many, at : at + chans, :] = moved[:, :, :BREADTH]
            parts[row : row + many, span + at : span + at + chans, :] = block
            parts[row : row + many, 2 * span + at : 2 * span + at + chans, :] = moved[:, :, BREADTH:]


def side_by_side(parts, row, many, taken, step=1):
    size = taken * parts.shape[1]
    return jnp.concatenate(
        [parts[at * step : at * step + taken].reshape(size, BREADTH) for at in range(row, row + many)],
        axis=1,
    )


def forward_three(below, own, above, arrived, grads, parts, shift):
    shift[...] = shifter()
    place_shifted((below, own, above), parts, shift, 32)
    rows = grads.shape[0]
    weight = arrived[:, rows * BREADTH :][:, :864]
    for row in range(0, rows, 4):
        pre = dot(weight, side_by_side(parts, row, 4, 3))
        small = jnp.exp(-jnp.abs(pre))
        rate = 0.3 + 0.7 * (jnp.where(pre >= 0.0, 1.0, small) / (1.0 + small))
        full = arrived[:, row * BREADTH : (row + 4) * BREADTH].astype(F32) * rate
        for off in range(4):
            grads[row + off] = full[:, off * BREADTH : (off + 1) * BREADTH].astype(BF16)


def filters_three(grads, parts, arrived, out, back):
    rows = grads.shape[0]
    left = jnp.concatenate([grads[row] for row in range(2, rows - 2)], axis=1)
    out[:, :864] = dot_nt(left, side_by_side(parts, 2, rows - 4, 3)).astype(BF16)
    out[:, 864:] = jnp.zeros((out.shape[0], out.shape[1] - 864), BF16)
    weight = arrived[:, rows * BREADTH :].astype(F32)
    turned = jnp.transpose(jnp.concatenate([weight, weight], axis=0))
    lane = lax.broadcasted_iota(jnp.int32, (32, BREADTH), 1)
    for tap in range(0, 27, 2):
        one = turned[(26 - tap) * 32 : (27 - tap) * 32]
        if tap == 26:
            back[:, tap * 64 : tap * 64 + 64] = one[:, :64].astype(BF16)
        else:
            two = turned[(25 - tap) * 32 : (26 - tap) * 32]
            pair = jnp.where(lane < 64, one, two)
            back[:, tap * 64 : tap * 64 + 128] = pair.astype(BF16)


def backward_three(first_ref, count_ref, below, own, above, slope, weight, grads, parts, shift):
    shift[...] = shifter()
    place_shifted((below, own, above), parts, shift, 64)
    rows = grads.shape[0]
    for row in range(0, rows, 2):
        pool = dot(weight[...], side_by_side(parts, row, 2, 3)) * 0.125
        for off in range(2):
            at = first_ref[0] + row + off
            inside = jnp.logical_and(at >= 0, at < count_ref[0])
            half = jnp.where(inside, pool[:, off * BREADTH : (off + 1) * BREADTH], 0.0)
            full = half[None] * slope[row + off].reshape(8, 32, BREADTH)
            grads[row + off] = full.astype(BF16).reshape(256, BREADTH)


def filters_two(grads, parts, out):
    rows = grads.shape[0] - 2
    left = jnp.concatenate([grads[row] for row in range(1, rows + 1)], axis=1)
    blocks = []
    for off in range(4):
        right = jnp.concatenate([parts[2 * row + 4 + off] for row in range(1, rows + 1)], axis=1)
        blocks.append(dot_nt(left, right))
    total = jnp.zeros((32, 768), F32)
    for phase in range(8):
        deep, high, wide = phase // 4, (phase // 2) % 2, phase % 2
        part = jnp.concatenate(
            [block[phase * 32 : phase * 32 + 32] for block in blocks[high : high + 3]], axis=1
        )
        move = (wide * 4 + deep) * 16
        if move:
            part = pltpu.roll(part, 768 - move, 1)
        total = total + part
    for half in range(2):
        for piece in range(3):
            at = (half * 3 + piece) * BREADTH
            out[piece, half * 32 : half * 32 + 32, :] = total[:, at : at + BREADTH].astype(BF16)


def backward_two(own, below, above, weight, out, parts, shift, join):
    shift[...] = shifter()
    join[...] = joiner()
    for row in range(own.shape[0]):
        block = jnp.concatenate([below[row], own[row], above[row]], axis=0)
        moved = dot(block, shift[...]).astype(BF16)
        for high in range(2):
            for deep in range(4):
                at = deep * 128 + high * 64
                to = deep * 32
                both = 2 * row + high
                parts[both, to : to + 32, :] = moved[at + 32 : at + 64, :BREADTH]
                parts[both, 128 + to : 160 + to, :] = block[at : at + 32]
                parts[both, 256 + to : 288 + to, :] = block[at + 32 : at + 64]
                parts[both, 384 + to : 416 + to, :] = moved[at : at + 32, BREADTH:]
    for row in range(0, out.shape[0], 2):
        cells = [parts[2 * at + 1 : 2 * at + 5].reshape(2048, BREADTH) for at in (row, row + 1)]
        cells = dot(weight[...], jnp.concatenate(cells, axis=1)).astype(BF16)
        both = [
            jnp.concatenate([cells[:64, at : at + BREADTH], cells[64:, at : at + BREADTH]], axis=1)
            for at in (0, BREADTH)
        ]
        joined = dot(jnp.concatenate(both, axis=0), join[...]).astype(BF16)
        out[row] = joined[:64]
        out[row + 1] = joined[64:]


def spread_out(scale_two, scale_three, sums, two, three):
    for part in range(6):
        half, piece = part // 3, part % 3
        block = sums[piece, half * 32 : half * 32 + 32, :].astype(F32) * scale_two
        for at in range(8):
            b, e, a = part // 2, (part % 2) * 2 + at // 4, at % 4
            if max(a, e) <= 2:
                two[a * 9 + b * 3 + e] = block[:, at * 16 : at * 16 + 16]
    for part in range(7):
        block = sums[3, part * 8 : part * 8 + 8, :].astype(F32) * scale_three
        for at in range(4):
            tap = part * 4 + at
            if tap < 27:
                b, e, a = tap // 9, (tap // 3) % 3, tap % 3
                three[a * 9 + b * 3 + e] = block[:, at * 32 : at * 32 + 32]


def shifted(axis, step):
    count = lax.axis_size(axis)
    return [(i, i + step) for i in range(count) if 0 <= i + step < count]


def neighbours(first, last, axis):
    return (
        lax.ppermute(last, axis, shifted(axis, 1)),
        lax.ppermute(first, axis, shifted(axis, -1)),
    )


def exchange(blocks, axis):
    return lax.all_to_all(blocks, axis, 0, 0, tiled=True)


def gathered(block, axis):
    count = lax.axis_size(axis)
    return exchange(jnp.broadcast_to(block[None], (count,) + block.shape), axis)


def total_of(blocks):
    return jnp.sum(blocks.astype(F32), axis=0)


def on_device(inputs, weight_two, weight_three, cotangent):
    groups = lax.axis_size("grp")
    slabs = lax.axis_size("depth")
    group = lax.axis_index("grp")
    chans, planes, height, breadth = inputs.shape
    cells = planes * slabs * height * groups * breadth
    pool_rows = height // 2
    count = jnp.full((1,), pool_rows * groups, jnp.int32)
    share = weight_three.shape[3]
    filters = share * groups

    own = jnp.transpose(inputs, (2, 1, 0, 3))
    below, above = neighbours(own[:, 0], own[:, 1], "depth")

    def edge(lo):
        return jnp.concatenate(
            [below[lo : lo + 7, None], own[lo : lo + 7], above[lo : lo + 7, None]], axis=1
        )

    top, bottom = neighbours(edge(0), edge(height - 7), "grp")

    rows_out = jnp.pad(cotangent.reshape(share, -1), ((0, 0), (2 * BREADTH, 2 * BREADTH)))
    weight_out = jnp.transpose(weight_three, (3, 1, 2, 0, 4)).reshape(share, 864)
    weight_out = jnp.pad(weight_out, ((0, 0), (0, 32)))
    span = pool_rows * BREADTH
    arrived = exchange(
        jnp.stack(
            [
                jnp.concatenate(
                    [rows_out[:, span * to : span * (to + 1) + 4 * BREADTH], weight_out], axis=1
                )
                for to in range(groups)
            ]
        ),
        "grp",
    ).reshape(filters, -1)

    plain = weight_two.reshape(27, 32, 16)
    ahead, back = call(
        weights_two,
        [jax.ShapeDtypeStruct((256, 1024), BF16), jax.ShapeDtypeStruct((128, 2048), BF16)],
        [],
        (plain, jnp.transpose(plain, (0, 2, 1))),
        2 * 256 * 1024 * 128,
    )

    first = (pool_rows * group - 3).astype(jnp.int32).reshape(1)
    pooled, slope, parts_two = call(
        forward_two,
        [
            jax.ShapeDtypeStruct((pool_rows + 6, 32, BREADTH), BF16),
            jax.ShapeDtypeStruct((pool_rows + 2, 256, BREADTH), F32),
            jax.ShapeDtypeStruct((height + 14, 256, BREADTH), BF16),
        ],
        [pltpu.VMEM((2 * BREADTH, 4 * BREADTH), BF16)],
        (first, count, own, below, above, top, bottom, ahead),
        2 * 14 * 256 * 1024 * 128,
        scalars=2,
    )

    pool_below, pool_above = neighbours(pooled, pooled, "depth")
    shift = pltpu.VMEM((BREADTH, 2 * BREADTH), BF16)
    grads, parts_three = call(
        forward_three,
        [
            jax.ShapeDtypeStruct((pool_rows + 4, filters, BREADTH), BF16),
            jax.ShapeDtypeStruct((pool_rows + 6, 288, BREADTH), BF16),
        ],
        [shift],
        (pool_below, pooled, pool_above, arrived),
        2 * 12 * 64 * 864 * 128,
    )

    grads_below, grads_above = neighbours(grads, grads, "depth")
    local_three, weight_back = call(
        filters_three,
        [
            jax.ShapeDtypeStruct((filters, 1024), BF16),
            jax.ShapeDtypeStruct((32, 27 * filters), BF16),
        ],
        [],
        (grads, parts_three, arrived),
        2 * 8 * 64 * 864 * 128,
    )
    three = total_of(exchange(local_three.reshape(groups, share, 1024), "grp"))
    three = jnp.transpose(three.reshape(share, 8, BREADTH), (1, 0, 2)).reshape(1, -1, BREADTH)
    (grad_two,) = call(
        backward_three,
        [jax.ShapeDtypeStruct((pool_rows + 2, 256, BREADTH), BF16)],
        [pltpu.VMEM((pool_rows + 4, 576, BREADTH), BF16), shift],
        (first + 2, count, grads_below, grads, grads_above, slope, weight_back),
        2 * 10 * 32 * 1728 * 128,
        scalars=2,
    )

    (local_two,) = call(
        filters_two,
        [jax.ShapeDtypeStruct((3, 64, BREADTH), BF16)],
        [],
        (grad_two, parts_two),
        2 * 8 * 256 * 1024 * 128,
    )
    two_below, two_above = neighbours(grad_two[:, :128], grad_two[:, 128:], "depth")
    (cells_back,) = call(
        backward_two,
        [jax.ShapeDtypeStruct((pool_rows, 64, 2 * BREADTH), BF16)],
        [
            pltpu.VMEM((height + 4, 512, BREADTH), BF16),
            shift,
            pltpu.VMEM((2 * BREADTH, 2 * BREADTH), BF16),
        ],
        (grad_two, two_below, two_above, back),
        2 * 8 * 128 * 2048 * 128,
    )
    input_grad = jnp.transpose(
        cells_back.reshape(pool_rows, 2, 2, chans, breadth), (3, 1, 0, 2, 4)
    ).reshape(inputs.shape)

    sums = jnp.concatenate([local_two, three.astype(BF16)], axis=0)
    sums = jnp.transpose(sums.reshape(4, slabs, -1), (1, 0, 2))
    mine = total_of(exchange(sums, "depth"))
    both = total_of(gathered(mine.astype(BF16), "grp"))
    mine = jnp.concatenate([both[:3], mine[3:]], axis=0).astype(BF16)
    sums = jnp.transpose(gathered(mine, "depth"), (1, 0, 2)).reshape(4, 64, BREADTH)
    two, three = call(
        functools.partial(spread_out, 1.0 / math.sqrt(cells), 1.0 / math.sqrt(cells / 8)),
        [
            jax.ShapeDtypeStruct((27, 32, 16), F32),
            jax.ShapeDtypeStruct((27, share, 32), F32),
        ],
        [],
        (sums,),
        2 * 64 * 1024,
    )
    return (input_grad, two.reshape(weight_two.shape), three.reshape(weight_three.shape))


def solution(mesh):
    placed = (
        P(None, "depth", "grp", None),
        P(),
        P(None, None, None, "grp", None),
        P("grp", "depth", None, None),
    )
    return jax.shard_map(
        on_device,
        mesh=mesh,
        in_specs=placed,
        out_specs=(P(None, "depth", "grp", None), P(), P(None, None, None, "grp", None)),
        check_vma=False,
    )
```

time: 163 us -> 146 us (0.90)
  waiting for transfers between devices: 14.7 us -> 38.5 us
  local copies, waits for them, and re-layouts: 39.7 us -> 16.2 us
  blocking collectives: 16.9 us -> 0 us
  starting transfers between devices: 61.4 us -> 73.6 us
  Pallas kernels: 21.8 us -> 10.6 us
  matrix products: 2.85 us -> 0 us
  other arithmetic: 3.37 us -> 5.17 us
    all_to_all x4 -> x5, waiting for transfers between devices: 14.7 us -> 34.4 us  [exchange(): return lax.all_to_all(blocks, axis, 0, 0, tiled=True)]
    all_to_all x1 -> x0, blocking collectives: 16.9 us -> none  [exchange(): return lax.all_to_all(blocks, axis, 0, 0, tiled=True)]
    all_to_all x4 -> x5, starting transfers between devices: 28.9 us -> 42.1 us  [exchange(): return lax.all_to_all(blocks, axis, 0, 0, tiled=True)]
    pallas_call x6 -> x8, Pallas kernels: 21.8 us -> 10.6 us  [call(): pl.pallas_call(kernel, out_shape=outs, in_specs=specs, out_specs=[pl.Bloc...]
    reshape x16 -> x3, local copies, waits for them, and re-layouts: 11.6 us -> 1.07 us  [the longest x1 0.81 us: on_device(): input_grad = jnp.transpose(cells_back.reshape(pool_rows, 2, 2, chans, bre...]
    convert_element_type x2 -> x0, local copies, waits for them, and re-layouts: 6.21 us -> none  [taps_two(): jnp.einsum('pkt,tfc->pfkc', pick, taps, preferred_element_type=F32)]
    ppermute x5, starting transfers between devices: 17.3 us -> 12.7 us  [neighbours(): lax.ppermute(first, axis, shifted(axis, -1))]
    unnamed x29 -> x25, local copies, waits for them, and re-layouts: 6.67 us -> 11.1 us
  transfers between devices with their start and end apart: 14 -> 15, of which waited for: 3 -> 5; matrix products, arithmetic and copies ran while one was open for 22% -> 7% of each run, Pallas kernels for 8% -> 5%
where the time goes in v2:
time: 146 us; the launch traced here: 145 us
  starting transfers between devices  73.6 us (50%)
  waiting for transfers between devices  38.5 us (26%)
  local copies, waits for them, and re-layouts  16.2 us (11%)
  Pallas kernels  10.6 us (7%)
  other arithmetic  5.17 us (4%)
    all_to_all x5, starting transfers between devices, exchange(): return lax.all_to_all(blocks, axis, 0, 0, tiled=True)  42.1 us
    all_to_all x5, waiting for transfers between devices, exchange(): return lax.all_to_all(blocks, axis, 0, 0, tiled=True)  34.4 us
    ppermute x5, starting transfers between devices, neighbours(): lax.ppermute(last, axis, shifted(axis, 1))  18.9 us
    ppermute x5, starting transfers between devices, neighbours(): lax.ppermute(first, axis, shifted(axis, -1))  12.7 us
    unnamed x25, local copies, waits for them, and re-layouts  11.1 us
    pallas_call x8, Pallas kernels, call(): pl.pallas_call(kernel, out_shape=outs, in_specs=specs, out_specs=[pl.Bloc...  10.6 us
    unnamed x7, other arithmetic  4.35 us
    ppermute x5, waiting for transfers between devices, neighbours(): lax.ppermute(first, axis, shifted(axis, -1))  4.17 us
  transfers between devices with their start and end apart: 15, of which 5 were waited for; matrix products, arithmetic and copies ran while one was open for 7% of the time, Pallas kernels for 5%

profile of v2, /device:TPU:1, one launch (start us, length us, event | category | flops | bytes accessed | tf_op | source)
XLA Modules:
  0.0 145.2 jit_solution(6376362430700076370)
XLA Ops:
  0.6 1.1 copy.67
  1.8 4.9 %collective-permute-start = (bf16[16,16,256]{2,1,0:T(8,128)(2,1)S(1)}, bf16[16,16,256]{2,1,0:T(8,128)(2,1)S(1)}, u32[]{:S(2)}, u32[]{:S(2)}) collective-permute-start(bf16[16,16,256]{2,1,0:T(8,128)(2,1)S(1)} %get-tuple-element.45), channel_id=1, source_target_pairs={{0,8},{8,16},{16,24},{24,32},{32,40},{40,48},{48,56},{56,64},{64,7... | collective-permute-start | bytes 393224 | tf_op jit(solution)/shard_map/ppermute | solution.py:280
  6.7 5.1 %collective-permute-start.1 = (bf16[16,16,256]{2,1,0:T(8,128)(2,1)S(1)}, bf16[16,16,256]{2,1,0:T(8,128)(2,1)S(1)}, u32[]{:S(2)}, u32[]{:S(2)}) collective-permute-start(bf16[16,16,256]{2,1,0:T(8,128)(2,1)S(1)} %get-tuple-element.44), channel_id=1, source_target_pairs={{8,0},{16,8},{24,16},{32,24},{40,32},{48,40},{56,48},{64,56},{72,6... | collective-permute-start | bytes 393224 | tf_op jit(solution)/shard_map/ppermute | solution.py:281
  11.9 1.0 copy.68
  12.9 0.9 copy.52
  14.5 0.6 fusion.2
  15.1 0.6 fusion.3
  17.6 0.6 fusion.7
  18.4 1.3 collective-permute-start.3
  19.7 4.0 %collective-permute-start.2 = (bf16[7,4,16,256]{3,2,0,1:T(8,128)(2,1)S(1)}, bf16[7,4,16,256]{3,2,0,1:T(8,128)(2,1)S(1)}, u32[]{:S(2)}, u32[]{:S(2)}) collective-permute-start(bf16[7,4,16,256]{3,2,0,1:T(8,128)(2,1)S(1)} %pad_maximum_fusion), channel_id=1, source_target_pairs={{0,1},{1,2},{2,3},{3,4},{4,5},{5,6},{6,7},{8,9},{9,10},{10,11},{11... | collective-permute-start | bytes 688136 | tf_op jit(solution)/shard_map/ppermute | solution.py:280
  23.7 0.6 fusion.8
  24.3 4.1 %all-to-all-start = ((bf16[8,8,2432]{2,1,0:T(8,128)(2,1)}), bf16[8,8,2432]{2,1,0:T(8,128)(2,1)S(1)}, u32[]{:S(2)}, u32[]{:S(2)}) async-start(bf16[8,8,2432]{2,1,0:T(8,128)(2,1)} %fusion.8), calls=%async_computation | async-start | bytes 622592 | tf_op jit(solution)/shard_map/all_to_all | solution.py:286
  28.6 0.9 copy.50.own
  29.9 0.7 copy-done.8
  30.6 0.9 copy-done.3
  31.5 0.9 copy-done.9
  32.5 2.5 %shard_map.68 = (bf16[14,32,128]{2,1,0:T(8,128)(2,1)S(1)}, f32[10,256,128]{2,1,0:T(8,128)S(1)}, bf16[30,256,128]{2,1,0:T(8,128)(2,1)S(1)}) custom-call(s32[1]{0:T(128)} %bitcast.first_ref, s32[1]{0:T(128)} %constant.16.clone.1.count_ref, bf16[16,2,16,256]{3,2,1,0:T(8,128)(2,1)S(1)} %copy-done.3, bf16[16,16,256]{2,1,0:T(8,128)(2,1)S(1)} %collective-permute-done.below, ...), custom_call_target="tpu_custom_call" | custom-call | flops 939524096 | bytes 4898824 | tf_op jit(solution)/shard_map/pallas_call | solution.py:21
  35.0 1.1 copy-done
  36.1 4.5 %collective-permute-start.4 = (bf16[14,32,128]{2,1,0:T(8,128)(2,1)S(1)}, bf16[14,32,128]{2,1,0:T(8,128)(2,1)S(1)}, u32[]{:S(2)}, u32[]{:S(2)}) collective-permute-start(bf16[14,32,128]{2,1,0:T(8,128)(2,1)S(1)} %get-tuple-element.15.own), channel_id=1, source_target_pairs={{0,8},{8,16},{16,24},{24,32},{32,40},{40,48},{48,56},{56,64},{64,7... | collective-permute-start | bytes 344072 | tf_op jit(solution)/shard_map/ppermute | solution.py:280
  40.5 1.9 %collective-permute-start.5 = (bf16[14,32,128]{2,1,0:T(8,128)(2,1)S(1)}, bf16[14,32,128]{2,1,0:T(8,128)(2,1)S(1)}, u32[]{:S(2)}, u32[]{:S(2)}) collective-permute-start(bf16[14,32,128]{2,1,0:T(8,128)(2,1)S(1)} %get-tuple-element.15.own), channel_id=1, source_target_pairs={{8,0},{16,8},{24,16},{32,24},{40,32},{48,40},{56,48},{64,56},{72,6... | collective-permute-start | bytes 344072 | tf_op jit(solution)/shard_map/ppermute | solution.py:281
  42.5 4.2 %collective-permute-done.5.above = bf16[14,32,128]{2,1,0:T(8,128)(2,1)S(1)} collective-permute-done((bf16[14,32,128]{2,1,0:T(8,128)(2,1)S(1)}, bf16[14,32,128]{2,1,0:T(8,128)(2,1)S(1)}, u32[]{:S(2)}, u32[]{:S(2)}) %collective-permute-start.5) | collective-permute-done | bytes 114720 | tf_op jit(solution)/shard_map/ppermute | solution.py:281
  46.7 0.9 shard_map.69
  47.5 1.9 %collective-permute-start.6 = (bf16[12,64,128]{2,1,0:T(8,128)(2,1)S(1)}, bf16[12,64,128]{2,1,0:T(8,128)(2,1)S(1)}, u32[]{:S(2)}, u32[]{:S(2)}) collective-permute-start(bf16[12,64,128]{2,1,0:T(8,128)(2,1)S(1)} %get-tuple-element.16.grads.own), channel_id=1, source_target_pairs={{0,8},{8,16},{16,24},{24,32},{32,40},{40,48},{48,56},{56,64},{64,7... | collective-permute-start | bytes 589832 | tf_op jit(solution)/shard_map/ppermute | solution.py:280
  49.5 2.4 %collective-permute-start.7 = (bf16[12,64,128]{2,1,0:T(8,128)(2,1)S(1)}, bf16[12,64,128]{2,1,0:T(8,128)(2,1)S(1)}, u32[]{:S(2)}, u32[]{:S(2)}) collective-permute-start(bf16[12,64,128]{2,1,0:T(8,128)(2,1)S(1)} %get-tuple-element.16.grads.own), channel_id=1, source_target_pairs={{8,0},{16,8},{24,16},{32,24},{40,32},{48,40},{56,48},{64,56},{72,6... | collective-permute-start | bytes 589832 | tf_op jit(solution)/shard_map/ppermute | solution.py:281
  51.9 1.3 shard_map.70
  53.2 0.6 copy-done.6
  53.9 6.9 %all-to-all-start.1 = ((bf16[8,8,1024]{2,1,0:T(8,128)(2,1)}), bf16[8,8,1024]{2,1,0:T(8,128)(2,1)S(1)}, u32[]{:S(2)}, u32[]{:S(2)}) async-start(bf16[8,8,1024]{2,1,0:T(8,128)(2,1)} %bitcast.24), calls=%async_computation.1 | async-start | bytes 262144 | tf_op jit(solution)/shard_map/all_to_all | solution.py:286
  60.8 7.8 %all-to-all-done.1 = bf16[8,8,1024]{2,1,0:T(8,128)(2,1)S(1)} async-done(((bf16[8,8,1024]{2,1,0:T(8,128)(2,1)}), bf16[8,8,1024]{2,1,0:T(8,128)(2,1)S(1)}, u32[]{:S(2)}, u32[]{:S(2)}) %all-to-all-start.1) | async-done | bytes 131104 | tf_op jit(solution)/shard_map/all_to_all | solution.py:286
  68.6 0.7 copy-done.4
  69.3 1.3 copy-done.1
  70.6 0.9 copy-done.5
  71.6 0.9 copy-done.7
  72.5 1.4 shard_map.71.own.grads
  73.9 0.8 shard_map.73
  74.8 0.7 copy.54
  75.4 20.6 %all-to-all-start.2 = ((bf16[64,4,128]{2,1,0:T(4,128)(2,1)}), bf16[64,4,128]{2,1,0:T(4,128)(2,1)S(1)}, u32[]{:S(2)}, u32[]{:S(2)}) async-start(bf16[64,4,128]{2,1,0:T(4,128)(2,1)} %copy.54), calls=%async_computation.2 | async-start | bytes 131072 | tf_op jit(solution)/shard_map/all_to_all | solution.py:286
  96.1 3.5 %collective-permute-start.8 = (bf16[10,128,128]{2,1,0:T(8,128)(2,1)S(1)}, bf16[10,128,128]{2,1,0:T(8,128)(2,1)S(1)}, u32[]{:S(2)}, u32[]{:S(2)}) collective-permute-start(bf16[10,128,128]{2,1,0:T(8,128)(2,1)S(1)} %get-tuple-element.41), channel_id=1, source_target_pairs={{0,8},{8,16},{16,24},{24,32},{32,40},{40,48},{48,56},{56,64},{64,7... | collective-permute-start | bytes 983048 | tf_op jit(solution)/shard_map/ppermute | solution.py:280
  99.6 1.9 %collective-permute-start.9 = (bf16[10,128,128]{2,1,0:T(8,128)(2,1)S(1)}, bf16[10,128,128]{2,1,0:T(8,128)(2,1)S(1)}, u32[]{:S(2)}, u32[]{:S(2)}) collective-permute-start(bf16[10,128,128]{2,1,0:T(8,128)(2,1)S(1)} %get-tuple-element.40), channel_id=1, source_target_pairs={{8,0},{16,8},{24,16},{32,24},{40,32},{48,40},{56,48},{64,56},{72,6... | collective-permute-start | bytes 983048 | tf_op jit(solution)/shard_map/ppermute | solution.py:281
  101.6 9.1 %all-to-all-done.2 = bf16[64,4,128]{2,1,0:T(4,128)(2,1)S(1)} async-done(((bf16[64,4,128]{2,1,0:T(4,128)(2,1)}), bf16[64,4,128]{2,1,0:T(4,128)(2,1)S(1)}, u32[]{:S(2)}, u32[]{:S(2)}) %all-to-all-start.2) | async-done | bytes 65568 | tf_op jit(solution)/shard_map/all_to_all | solution.py:286
  111.3 3.3 %all-to-all-start.3 = ((bf16[8,4,128]{2,1,0:T(4,128)(2,1)}), bf16[8,4,128]{2,1,0:T(4,128)(2,1)S(1)}, u32[]{:S(2)}, u32[]{:S(2)}) async-start(bf16[8,4,128]{2,1,0:T(4,128)(2,1)} %broadcast_in_dim.28), calls=%async_computation.3 | async-start | bytes 16384 | tf_op jit(solution)/shard_map/all_to_all | solution.py:286
  114.7 6.5 %all-to-all-done.3 = bf16[8,4,128]{2,1,0:T(4,128)(2,1)S(1)} async-done(((bf16[8,4,128]{2,1,0:T(4,128)(2,1)}), bf16[8,4,128]{2,1,0:T(4,128)(2,1)S(1)}, u32[]{:S(2)}, u32[]{:S(2)}) %all-to-all-start.3) | async-done | bytes 8224 | tf_op jit(solution)/shard_map/all_to_all | solution.py:286
  121.2 0.7 broadcast_in_dim.29
  121.8 7.1 %all-to-all-start.4 = ((bf16[64,4,128]{2,1,0:T(4,128)(2,1)}), bf16[64,4,128]{2,1,0:T(4,128)(2,1)S(1)}, u32[]{:S(2)}, u32[]{:S(2)}) async-start(bf16[64,4,128]{2,1,0:T(4,128)(2,1)} %broadcast_in_dim.29), calls=%async_computation.4 | async-start | bytes 131072 | tf_op jit(solution)/shard_map/all_to_all | solution.py:286
  128.9 2.5 %shard_map.72 = bf16[8,64,256]{2,1,0:T(8,128)(2,1)S(1)} custom-call(bf16[10,256,128]{2,1,0:T(8,128)(2,1)S(1)} %shard_map.71.own.grads, bf16[10,128,128]{2,1,0:T(8,128)(2,1)S(1)} %collective-permute-done.8.below, bf16[10,128,128]{2,1,0:T(8,128)(2,1)S(1)} %collective-permute-done.9.above, bf16[128,2048]{1,0:T(8,128)(2,1)S(1)} %get-tuple-element.20.weight), custom_call_target="tpu_custom_call" | custom-call | flops 536870912 | bytes 2097152 | tf_op jit(solution)/shard_map/pallas_call | solution.py:21
  131.7 0.8 reshape.76
  132.5 11.0 %all-to-all-done.4 = bf16[64,4,128]{2,1,0:T(4,128)(2,1)S(1)} async-done(((bf16[64,4,128]{2,1,0:T(4,128)(2,1)}), bf16[64,4,128]{2,1,0:T(4,128)(2,1)S(1)}, u32[]{:S(2)}, u32[]{:S(2)}) %all-to-all-start.4) | async-done | bytes 65568 | tf_op jit(solution)/shard_map/all_to_all | solution.py:286
  143.5 0.8 shard_map.74
  144.3 0.9 copy.57
  (48 shorter events, 4.4 us)
Async XLA Ops:
  1.8 16.5 %collective-permute-start = (bf16[16,16,256]{2,1,0:T(8,128)(2,1)S(1)}, bf16[16,16,256]{2,1,0:T(8,128)(2,1)S(1)}, u32[]{:S(2)}, u32[]{:S(2)}) collective-permute-start(bf16[16,16,256]{2,1,0:T(8,128)(2,1)S(1)} %get-tuple-element.45), channel_id=1, source_target_pairs={{0,8},{8,16},{16,24},{24,32},{32,40},{40,48},{48,56},{56,64},{64,7... | collective-permute-start | bytes 393224 | tf_op jit(solution)/shard_map/ppermute | solution.py:280
  6.7 11.6 %collective-permute-start.1 = (bf16[16,16,256]{2,1,0:T(8,128)(2,1)S(1)}, bf16[16,16,256]{2,1,0:T(8,128)(2,1)S(1)}, u32[]{:S(2)}, u32[]{:S(2)}) collective-permute-start(bf16[16,16,256]{2,1,0:T(8,128)(2,1)S(1)} %get-tuple-element.44), channel_id=1, source_target_pairs={{8,0},{16,8},{24,16},{32,24},{40,32},{48,40},{56,48},{64,56},{72,6... | collective-permute-start | bytes 393224 | tf_op jit(solution)/shard_map/ppermute | solution.py:281
  12.9 15.6 %copy-start.2 = (bf16[3,3,3,32,16]{3,4,2,1,0:T(8,128)(2,1)S(1)}, bf16[3,3,3,32,16]{3,4,2,1,0:T(8,128)(2,1)}, u32[]{:S(2)}) copy-start(bf16[3,3,3,32,16]{3,4,2,1,0:T(8,128)(2,1)} %param.5) | copy-start | bytes 82948
  12.9 15.8 %copy-start.10 = (bf16[16,2,16,256]{3,2,1,0:T(8,128)(2,1)S(1)}, bf16[16,2,16,256]{3,2,1,0:T(8,128)(2,1)}, u32[]{:S(2)}) copy-start(bf16[16,2,16,256]{3,2,1,0:T(8,128)(2,1)} %param.4) | copy-start | bytes 786436
  18.4 11.5 %collective-permute-start.3 = (bf16[7,4,16,256]{3,2,1,0:T(8,128)(2,1)S(1)}, bf16[7,4,16,256]{3,2,1,0:T(8,128)(2,1)S(1)}, u32[]{:S(2)}, u32[]{:S(2)}) collective-permute-start(bf16[7,4,16,256]{3,2,1,0:T(8,128)(2,1)S(1)} %pad_maximum_fusion.1), channel_id=1, source_target_pairs={{1,0},{2,1},{3,2},{4,3},{5,4},{6,5},{7,6},{9,8},{10,9},{11,10},{12... | collective-permute-start | bytes 688136 | tf_op jit(solution)/shard_map/ppermute | solution.py:281
  19.7 10.2 %collective-permute-start.2 = (bf16[7,4,16,256]{3,2,0,1:T(8,128)(2,1)S(1)}, bf16[7,4,16,256]{3,2,0,1:T(8,128)(2,1)S(1)}, u32[]{:S(2)}, u32[]{:S(2)}) collective-permute-start(bf16[7,4,16,256]{3,2,0,1:T(8,128)(2,1)S(1)} %pad_maximum_fusion), channel_id=1, source_target_pairs={{0,1},{1,2},{2,3},{3,4},{4,5},{5,6},{6,7},{8,9},{9,10},{10,11},{11... | collective-permute-start | bytes 688136 | tf_op jit(solution)/shard_map/ppermute | solution.py:280
  24.3 18.1 %all-to-all-start = ((bf16[8,8,2432]{2,1,0:T(8,128)(2,1)}), bf16[8,8,2432]{2,1,0:T(8,128)(2,1)S(1)}, u32[]{:S(2)}, u32[]{:S(2)}) async-start(bf16[8,8,2432]{2,1,0:T(8,128)(2,1)} %fusion.8), calls=%async_computation | async-start | bytes 622592 | tf_op jit(solution)/shard_map/all_to_all | solution.py:286
  29.9 0.7 copy-start.8
  30.6 0.9 copy-start.3
  31.5 0.9 copy-start.9
  35.0 1.1 copy-start
  36.1 6.4 %collective-permute-start.4 = (bf16[14,32,128]{2,1,0:T(8,128)(2,1)S(1)}, bf16[14,32,128]{2,1,0:T(8,128)(2,1)S(1)}, u32[]{:S(2)}, u32[]{:S(2)}) collective-permute-start(bf16[14,32,128]{2,1,0:T(8,128)(2,1)S(1)} %get-tuple-element.15.own), channel_id=1, source_target_pairs={{0,8},{8,16},{16,24},{24,32},{32,40},{40,48},{48,56},{56,64},{64,7... | collective-permute-start | bytes 344072 | tf_op jit(solution)/shard_map/ppermute | solution.py:280
  40.5 6.1 %collective-permute-start.5 = (bf16[14,32,128]{2,1,0:T(8,128)(2,1)S(1)}, bf16[14,32,128]{2,1,0:T(8,128)(2,1)S(1)}, u32[]{:S(2)}, u32[]{:S(2)}) collective-permute-start(bf16[14,32,128]{2,1,0:T(8,128)(2,1)S(1)} %get-tuple-element.15.own), channel_id=1, source_target_pairs={{8,0},{16,8},{24,16},{32,24},{40,32},{48,40},{56,48},{64,56},{72,6... | collective-permute-start | bytes 344072 | tf_op jit(solution)/shard_map/ppermute | solution.py:281
  47.5 21.1 %collective-permute-start.6 = (bf16[12,64,128]{2,1,0:T(8,128)(2,1)S(1)}, bf16[12,64,128]{2,1,0:T(8,128)(2,1)S(1)}, u32[]{:S(2)}, u32[]{:S(2)}) collective-permute-start(bf16[12,64,128]{2,1,0:T(8,128)(2,1)S(1)} %get-tuple-element.16.grads.own), channel_id=1, source_target_pairs={{0,8},{8,16},{16,24},{24,32},{32,40},{40,48},{48,56},{56,64},{64,7... | collective-permute-start | bytes 589832 | tf_op jit(solution)/shard_map/ppermute | solution.py:280
  49.5 19.2 %collective-permute-start.7 = (bf16[12,64,128]{2,1,0:T(8,128)(2,1)S(1)}, bf16[12,64,128]{2,1,0:T(8,128)(2,1)S(1)}, u32[]{:S(2)}, u32[]{:S(2)}) collective-permute-start(bf16[12,64,128]{2,1,0:T(8,128)(2,1)S(1)} %get-tuple-element.16.grads.own), channel_id=1, source_target_pairs={{8,0},{16,8},{24,16},{32,24},{40,32},{48,40},{56,48},{64,56},{72,6... | collective-permute-start | bytes 589832 | tf_op jit(solution)/shard_map/ppermute | solution.py:281
  53.2 0.6 copy-start.6
  53.9 14.7 %all-to-all-start.1 = ((bf16[8,8,1024]{2,1,0:T(8,128)(2,1)}), bf16[8,8,1024]{2,1,0:T(8,128)(2,1)S(1)}, u32[]{:S(2)}, u32[]{:S(2)}) async-start(bf16[8,8,1024]{2,1,0:T(8,128)(2,1)} %bitcast.24), calls=%async_computation.1 | async-start | bytes 262144 | tf_op jit(solution)/shard_map/all_to_all | solution.py:286
  68.6 0.7 copy-start.4
  69.3 1.3 copy-start.1
  70.6 0.9 copy-start.5
  71.6 0.9 copy-start.7
  75.4 35.2 %all-to-all-start.2 = ((bf16[64,4,128]{2,1,0:T(4,128)(2,1)}), bf16[64,4,128]{2,1,0:T(4,128)(2,1)S(1)}, u32[]{:S(2)}, u32[]{:S(2)}) async-start(bf16[64,4,128]{2,1,0:T(4,128)(2,1)} %copy.54), calls=%async_computation.2 | async-start | bytes 131072 | tf_op jit(solution)/shard_map/all_to_all | solution.py:286
  96.1 32.8 %collective-permute-start.8 = (bf16[10,128,128]{2,1,0:T(8,128)(2,1)S(1)}, bf16[10,128,128]{2,1,0:T(8,128)(2,1)S(1)}, u32[]{:S(2)}, u32[]{:S(2)}) collective-permute-start(bf16[10,128,128]{2,1,0:T(8,128)(2,1)S(1)} %get-tuple-element.41), channel_id=1, source_target_pairs={{0,8},{8,16},{16,24},{24,32},{32,40},{40,48},{48,56},{56,64},{64,7... | collective-permute-start | bytes 983048 | tf_op jit(solution)/shard_map/ppermute | solution.py:280
  99.6 29.3 %collective-permute-start.9 = (bf16[10,128,128]{2,1,0:T(8,128)(2,1)S(1)}, bf16[10,128,128]{2,1,0:T(8,128)(2,1)S(1)}, u32[]{:S(2)}, u32[]{:S(2)}) collective-permute-start(bf16[10,128,128]{2,1,0:T(8,128)(2,1)S(1)} %get-tuple-element.40), channel_id=1, source_target_pairs={{8,0},{16,8},{24,16},{32,24},{40,32},{48,40},{56,48},{64,56},{72,6... | collective-permute-start | bytes 983048 | tf_op jit(solution)/shard_map/ppermute | solution.py:281
  111.3 9.8 %all-to-all-start.3 = ((bf16[8,4,128]{2,1,0:T(4,128)(2,1)}), bf16[8,4,128]{2,1,0:T(4,128)(2,1)S(1)}, u32[]{:S(2)}, u32[]{:S(2)}) async-start(bf16[8,4,128]{2,1,0:T(4,128)(2,1)} %broadcast_in_dim.28), calls=%async_computation.3 | async-start | bytes 16384 | tf_op jit(solution)/shard_map/all_to_all | solution.py:286
  121.8 21.7 %all-to-all-start.4 = ((bf16[64,4,128]{2,1,0:T(4,128)(2,1)}), bf16[64,4,128]{2,1,0:T(4,128)(2,1)S(1)}, u32[]{:S(2)}, u32[]{:S(2)}) async-start(bf16[64,4,128]{2,1,0:T(4,128)(2,1)} %broadcast_in_dim.29), calls=%async_computation.4 | async-start | bytes 131072 | tf_op jit(solution)/shard_map/all_to_all | solution.py:286

commit v3 on v2

v3 whole, which is shorter than its diff:
```python
import functools
import math

import jax
import jax.numpy as jnp
from jax import lax
from jax.experimental import pallas as pl
from jax.experimental.pallas import tpu as pltpu
from jax.sharding import PartitionSpec as P


F32 = jnp.float32
BF16 = jnp.bfloat16
BREADTH = 128


def call(kernel, outs, scratch, args, flops):
    specs = [pl.BlockSpec(memory_space=pltpu.VMEM)] * len(args)
    moved = sum(math.prod(a.shape) * a.dtype.itemsize for a in list(args) + list(outs))
    return pl.pallas_call(
        kernel,
        out_shape=outs,
        in_specs=specs,
        out_specs=[pl.BlockSpec(memory_space=pltpu.VMEM)] * len(outs),
        scratch_shapes=scratch,
        compiler_params=pltpu.CompilerParams(vmem_limit_bytes=16 * 1024 * 1024),
        cost_estimate=pl.CostEstimate(flops=flops, bytes_accessed=moved, transcendentals=0),
    )(*args)


def dot(left, right):
    return jnp.dot(left, right, preferred_element_type=F32)


def dot_nt(left, right):
    return lax.dot_general(left, right, (((1,), (1,)), ((), ())), preferred_element_type=F32)


def indicator(shape, test):
    row = lax.broadcasted_iota(jnp.int32, shape, 0)
    col = lax.broadcasted_iota(jnp.int32, shape, 1)
    return jnp.where(test(row, col), 1.0, 0.0).astype(BF16)


def splitter():
    def test(row, col):
        part, at = col // BREADTH, col % BREADTH
        return row == 2 * at + part - 1

    return indicator((2 * BREADTH, 4 * BREADTH), test)


def shifter():
    def test(row, col):
        part, at = col // BREADTH, col % BREADTH
        return row == at + 2 * part - 1

    return indicator((BREADTH, 2 * BREADTH), test)


def joiner():
    def test(row, col):
        return col == 2 * (row % BREADTH) + row // BREADTH

    return indicator((2 * BREADTH, 2 * BREADTH), test)


def weights_two(plain, turned, ahead, back):
    def blocks(source, outs, ins, flip):
        per = BREADTH // ins
        total = []
        for part in range(64 // per):
            summed = jnp.zeros((outs, BREADTH), F32)
            for at in range(per):
                place = part * per + at
                b, e, a = place // 16, (place // 4) % 4, place % 4
                if max(a, b, e) > 2:
                    continue
                if flip:
                    a, b, e = 2 - a, 2 - b, 2 - e
                spread = indicator((ins, BREADTH), lambda row, col: col == row + at * ins)
                summed = summed + dot(source[a * 9 + b * 3 + e], spread)
            total.append(summed)
        return jnp.concatenate(total, axis=1)

    def phases(out, base, outs, ins, row_of):
        for phase in range(8):
            deep, high, wide = phase // 4, (phase // 2) % 2, phase % 2
            move = (high * 16 + wide * 4 + deep) * ins
            full = pltpu.roll(base, move, 1) if move else base
            at = row_of(deep, high, wide) * outs
            out[at : at + outs, :] = full.astype(BF16)

    phases(ahead, blocks(plain, 32, 16, False), 32, 16, lambda d, h, w: d * 4 + h * 2 + w)
    phases(back, blocks(turned, 16, 32, True), 16, 32, lambda d, h, w: w * 4 + d * 2 + h)


def inside(at, rows):
    return jnp.logical_and(at >= 0, at < rows * lax.axis_size("grp"))


def forward_two(own, below, above, top, bottom, weight, pooled, slope, parts, split):
    split[...] = splitter()
    first = pooled.shape[0] - 6
    first = first * lax.axis_index("grp") - 3
    edge = top.shape[0]
    height = own.shape[0]

    def place(row, many, block):
        cells = dot(block, split[...]).astype(BF16).reshape(many, 64, 4 * BREADTH)
        for part in range(4):
            to = part * 64
            parts[row : row + many, to : to + 64, :] = cells[:, :, part * BREADTH : (part + 1) * BREADTH]

    for ref, to in ((top, 0), (own, edge), (bottom, edge + height)):
        for row in range(0, ref.shape[0], 4):
            block = []
            for at in range(row, min(row + 4, ref.shape[0])):
                block += [below[to + at], ref[at, 0], ref[at, 1], above[to + at]]
            place(to + row, len(block) // 4, jnp.concatenate(block, axis=0))

    rows = pooled.shape[0]
    for row in range(0, rows, 2):
        cells = [parts[2 * at : 2 * at + 4].reshape(1024, BREADTH) for at in (row, row + 1)]
        pre = dot(weight[...], jnp.concatenate(cells, axis=1))
        small = jnp.exp(-jnp.abs(pre))
        whole = 1.0 + small
        value = 0.3 * pre + 0.7 * (jnp.maximum(pre, 0.0) + jnp.log(whole))
        summed = jnp.sum(value.reshape(8, 32, 2 * BREADTH), axis=0) * 0.125
        for off in range(2):
            half = summed[:, off * BREADTH : (off + 1) * BREADTH]
            kept = inside(first + row + off, rows - 6)
            pooled[row + off] = jnp.where(kept, half, 0.0).astype(BF16)
        if 2 <= row < rows - 2:
            rate = 0.3 + 0.7 * (jnp.where(pre >= 0.0, 1.0, small) / whole)
            slope[row - 2] = rate[:, :BREADTH]
            slope[row - 1] = rate[:, BREADTH:]


def place_shifted(refs, parts, shift, chans):
    span = len(refs) * chans
    rows = refs[0].shape[0]
    step = 256 // chans
    for plane, ref in enumerate(refs):
        at = plane * chans
        for row in range(0, rows, step):
            many = min(step, rows - row)
            block = ref[row : row + many]
            moved = dot(block.reshape(many * chans, BREADTH), shift[...]).astype(BF16)
            moved = moved.reshape(many, chans, 2 * BREADTH)
            parts[row : row + many, at : at + chans, :] = moved[:, :, :BREADTH]
            parts[row : row + many, span + at : span + at + chans, :] = block
            parts[row : row + many, 2 * span + at : 2 * span + at + chans, :] = moved[:, :, BREADTH:]


def side_by_side(parts, row, many, taken, step=1):
    size = taken * parts.shape[1]
    return jnp.concatenate(
        [parts[at * step : at * step + taken].reshape(size, BREADTH) for at in range(row, row + many)],
        axis=1,
    )


def pack(cot, taps, out):
    count, share, width = out.shape
    rows = cot.shape[0] // count
    extra = (width - 896) // BREADTH - rows
    blocks = []
    for part in range(7):
        piece = []
        for tap in range(part * 4, part * 4 + 4):
            at = (tap % 3) * 9 + (tap // 9) * 3 + (tap // 3) % 3
            piece.append(taps[at].astype(F32) if tap < 27 else jnp.zeros((share, 32), F32))
        blocks.append(jnp.concatenate(piece, axis=1).astype(BF16))
    for to in range(count):
        for row in range(rows + extra):
            at = rows * to - extra // 2 + row
            lane = row * BREADTH
            if 0 <= at < cot.shape[0]:
                out[to, :, lane : lane + BREADTH] = cot[at]
            else:
                out[to, :, lane : lane + BREADTH] = jnp.zeros((share, BREADTH), BF16)
        for part in range(7):
            lane = (rows + extra + part) * BREADTH
            out[to, :, lane : lane + BREADTH] = blocks[part]


def middle_three(below, own, above, arrived, grads, parts, down, same, up, shift, around, turned):
    shift[...] = shifter()
    place_shifted((below, own, above), parts, shift, 32)
    rows = grads.shape[0]
    span = rows * BREADTH
    weight = arrived[:, span:]
    for row in range(0, rows, 4):
        pre = dot(weight[:, :864], side_by_side(parts, row, 4, 3))
        small = jnp.exp(-jnp.abs(pre))
        rate = 0.3 + 0.7 * (jnp.where(pre >= 0.0, 1.0, small) / (1.0 + small))
        full = arrived[:, row * BREADTH : (row + 4) * BREADTH].astype(F32) * rate
        for off in range(4):
            grads[row + off] = full[:, off * BREADTH : (off + 1) * BREADTH].astype(BF16)
    weight = weight.astype(F32)
    flat = jnp.transpose(jnp.concatenate([weight, weight], axis=0))
    lane = lax.broadcasted_iota(jnp.int32, (32, BREADTH), 1)
    for plane in range(3):

        def tap(at, plane=plane):
            first = ((8 - at) * 3 + 2 - plane) * 32
            return flat[first : first + 32]

        to = plane * 32
        for at in range(0, 8, 2):
            pair = jnp.where(lane < 64, tap(at), tap(at + 1))
            turned[to : to + 32, at * 64 : at * 64 + 128] = pair.astype(BF16)
        turned[to : to + 32, 512:576] = tap(8)[:, :64].astype(BF16)
    place_shifted((grads,), around, shift, 64)
    for row in range(0, rows - 2, 2):
        pool = dot(turned[...], side_by_side(around, row, 2, 3))
        for off in range(2):
            half = pool[:, off * BREADTH : (off + 1) * BREADTH]
            up[row + off] = half[:32].astype(BF16)
            same[row + off] = half[32:64]
            down[row + off] = half[64:].astype(BF16)


def filters_three(grads, parts, out):
    rows = grads.shape[0]
    left = jnp.concatenate([grads[row] for row in range(2, rows - 2)], axis=1)
    full = dot_nt(left, side_by_side(parts, 2, rows - 4, 3))
    full = jnp.concatenate([full, jnp.zeros((full.shape[0], 160), F32)], axis=1)
    for half in range(2):
        for to in range(8):
            for part in range(4):
                lane = (half * 4 + part) * BREADTH
                at = to * 32 + part * 8
                out[half, at : at + 8, :] = full[to * 8 : to * 8 + 8, lane : lane + BREADTH]


def middle_two(below, own, above, slope, parts, three, low, high, keep, send):
    rows = own.shape[0] - 2
    first = rows * lax.axis_index("grp") - 1
    left = []
    for row in range(rows + 2):
        pool = own[row] + below[row].astype(F32) + above[row].astype(F32)
        pool = jnp.where(inside(first + row, rows), pool, 0.0) * 0.125
        full = pool[None] * slope[row].reshape(8, 32, BREADTH)
        full = full.astype(BF16).reshape(256, BREADTH)
        low[row] = full[:128]
        high[row] = full[128:]
        if 1 <= row <= rows:
            left.append(full)
    left = jnp.concatenate(left, axis=1)
    blocks = []
    for off in range(4):
        right = jnp.concatenate([parts[2 * row + 4 + off] for row in range(1, rows + 1)], axis=1)
        blocks.append(dot_nt(left, right))
    total = jnp.zeros((32, 768), F32)
    for phase in range(8):
        deep, tall, wide = phase // 4, (phase // 2) % 2, phase % 2
        part = jnp.concatenate(
            [block[phase * 32 : phase * 32 + 32] for block in blocks[tall : tall + 3]], axis=1
        )
        move = (wide * 4 + deep) * 16
        if move:
            part = pltpu.roll(part, 768 - move, 1)
        total = total + part
    slot = lax.broadcasted_iota(jnp.int32, (32, BREADTH), 1) // 16
    dense = []
    rest = jnp.zeros((32, BREADTH), F32)
    for off in range(3):
        one = total[:, off * 256 : off * 256 + 128]
        two = total[:, off * 256 + 128 : off * 256 + 256]
        one = jnp.where(slot == 3, pltpu.roll(two, 48, 1), one)
        dense.append(jnp.where(slot == 7, pltpu.roll(two, 96, 1), one))
        moved = pltpu.roll(two, 96 + off * 16, 1) if off != 2 else two
        rest = jnp.where(slot == off, moved, rest)
    dense.append(rest)
    second = jnp.bitwise_and(lax.axis_index("depth"), 1) != 0
    one = jnp.concatenate(dense[:2] + [three[0]], axis=0)
    two = jnp.concatenate(dense[2:] + [three[1]], axis=0)
    keep[...] = jnp.where(second, two, one)
    send[...] = jnp.where(second, one, two)


def slot_of(b, e, a):
    if e < 2:
        return b, e * 4 + a
    return ((b, 3), (b, 7), (3, b))[a]


def halved(bit, mine, came, keep, send):
    count = (mine.shape[0] - 64) // 32
    total = (mine[...].astype(F32) + came[...].astype(F32)).astype(BF16)
    keep[:64, :] = total[:64]
    send[:64, :] = total[:64]
    group = lax.axis_index("grp")
    on = jnp.bitwise_and(group, bit) != 0
    for at in range(count // 2):
        zero, one = 64 + 64 * at, 96 + 64 * at
        to = 64 + 32 * at
        first, second = total[zero : zero + 32], total[one : one + 32]
        keep[to : to + 32, :] = jnp.where(on, second, first)
        send[to : to + 32, :] = jnp.where(on, first, second)


def backward_two(below, low, high, above, weight, out, parts, shift, join):
    shift[...] = shifter()
    join[...] = joiner()
    for row in range(low.shape[0]):
        block = jnp.concatenate([below[row], low[row], high[row], above[row]], axis=0)
        moved = dot(block, shift[...]).astype(BF16)
        for tall in range(2):
            for deep in range(4):
                at = deep * 128 + tall * 64
                to = deep * 32
                both = 2 * row + tall
                parts[both, to : to + 32, :] = moved[at + 32 : at + 64, :BREADTH]
                parts[both, 128 + to : 160 + to, :] = block[at : at + 32]
                parts[both, 256 + to : 288 + to, :] = block[at + 32 : at + 64]
                parts[both, 384 + to : 416 + to, :] = moved[at : at + 32, BREADTH:]
    for row in range(0, out.shape[0], 2):
        cells = [parts[2 * at + 1 : 2 * at + 5].reshape(2048, BREADTH) for at in (row, row + 1)]
        cells = dot(weight[...], jnp.concatenate(cells, axis=1)).astype(BF16)
        both = [
            jnp.concatenate([cells[:64, at : at + BREADTH], cells[64:, at : at + BREADTH]], axis=1)
            for at in (0, BREADTH)
        ]
        joined = dot(jnp.concatenate(both, axis=0), join[...]).astype(BF16)
        out[row] = joined[:64]
        out[row + 1] = joined[64:]


def spread_out(scale_two, scale_three, mine, other, two, three):
    second = jnp.bitwise_and(lax.axis_index("depth"), 1) != 0
    one, another = mine[...], other[...]
    lower, upper = jnp.where(second, another, one), jnp.where(second, one, another)
    flat = jnp.transpose(jnp.concatenate([lower[:64], upper[:64]], axis=0) * scale_two)
    for tap in range(27):
        a, b, e = tap // 9, (tap // 3) % 3, tap % 3
        block, slot = slot_of(b, e, a)
        two[tap] = flat[slot * 16 : slot * 16 + 16, block * 32 : block * 32 + 32]
    for part in range(7):
        at = 64 + (part % 4) * 8
        block = (lower, upper)[part // 4][at : at + 8] * scale_three
        for at in range(4):
            tap = part * 4 + at
            if tap < 27:
                b, e, a = tap // 9, (tap // 3) % 3, tap % 3
                three[a * 9 + b * 3 + e] = block[:, at * 32 : at * 32 + 32]


def shifted(axis, step):
    count = lax.axis_size(axis)
    return [(i, i + step) for i in range(count) if 0 <= i + step < count]


def neighbours(first, last, axis):
    return (
        lax.ppermute(last, axis, shifted(axis, 1)),
        lax.ppermute(first, axis, shifted(axis, -1)),
    )


def exchange(blocks, axis):
    return lax.all_to_all(blocks, axis, 0, 0, tiled=True)


def traded(block, axis, reach):
    return lax.ppermute(block, axis, [(i, i ^ reach) for i in range(lax.axis_size(axis))])


def on_device(inputs, weight_two, weight_three, cotangent):
    groups = lax.axis_size("grp")
    slabs = lax.axis_size("depth")
    chans, planes, height, breadth = inputs.shape
    cells = planes * slabs * height * groups * breadth
    pool_rows = height // 2
    share = weight_three.shape[3]
    filters = share * groups

    own = jnp.transpose(inputs, (2, 1, 0, 3))
    own, cotangent = lax.optimization_barrier((own, cotangent))
    top, bottom = neighbours(own[:7], own[height - 7 :], "grp")

    (packed,) = call(
        pack,
        [jax.ShapeDtypeStruct((groups, share, (pool_rows + 4) * BREADTH + 896), BF16)],
        [],
        (jnp.transpose(cotangent[:, 0], (1, 0, 2)), weight_three.reshape(27, share, 32)),
        2 * 64 * 1024,
    )
    arrived = exchange(packed, "grp").reshape(filters, -1)

    def whole(plane):
        return jnp.concatenate([top[:, plane], own[:, plane], bottom[:, plane]], axis=0)

    below, above = neighbours(whole(0), whole(1), "depth")

    plain = weight_two.reshape(27, 32, 16)
    ahead, back = call(
        weights_two,
        [jax.ShapeDtypeStruct((256, 1024), BF16), jax.ShapeDtypeStruct((128, 2048), BF16)],
        [],
        (plain, jnp.transpose(plain, (0, 2, 1))),
        2 * 256 * 1024 * 128,
    )

    pooled, slope, parts_two = call(
        forward_two,
        [
            jax.ShapeDtypeStruct((pool_rows + 6, 32, BREADTH), BF16),
            jax.ShapeDtypeStruct((pool_rows + 2, 256, BREADTH), F32),
            jax.ShapeDtypeStruct((height + 14, 256, BREADTH), BF16),
        ],
        [pltpu.VMEM((2 * BREADTH, 4 * BREADTH), BF16)],
        (own, below, above, top, bottom, ahead),
        2 * 14 * 256 * 1024 * 128,
    )

    pool_below, pool_above = neighbours(pooled, pooled, "depth")
    shift = pltpu.VMEM((BREADTH, 2 * BREADTH), BF16)
    terms = jax.ShapeDtypeStruct((pool_rows + 2, 32, BREADTH), BF16)
    grads, parts_three, down, same, up = call(
        middle_three,
        [
            jax.ShapeDtypeStruct((pool_rows + 4, filters, BREADTH), BF16),
            jax.ShapeDtypeStruct((pool_rows + 6, 288, BREADTH), BF16),
            terms,
            jax.ShapeDtypeStruct(terms.shape, F32),
            terms,
        ],
        [
            shift,
            pltpu.VMEM((pool_rows + 4, 3 * filters, BREADTH), BF16),
            pltpu.VMEM((96, 9 * filters), BF16),
        ],
        (pool_below, pooled, pool_above, arrived),
        2 * 12 * 64 * 864 * 128 * 2,
    )

    terms_below, terms_above = neighbours(down, up, "depth")
    (local_three,) = call(
        filters_three,
        [jax.ShapeDtypeStruct((2, groups * 32, BREADTH), F32)],
        [],
        (grads, parts_three),
        2 * 8 * 64 * 864 * 128,
    )
    halves = jax.ShapeDtypeStruct((64 + groups * 32, BREADTH), F32)
    plane = jax.ShapeDtypeStruct((pool_rows + 2, 128, BREADTH), BF16)
    low, high, keep, send = call(
        middle_two,
        [plane, plane, halves, halves],
        [],
        (terms_below, same, terms_above, slope, parts_two, local_three),
        2 * 8 * 256 * 1024 * 128,
    )

    came = traded(send, "depth", 1)
    two_below, two_above = neighbours(low, high, "depth")
    reach = 1
    while reach < groups:
        half = jax.ShapeDtypeStruct(((keep.shape[0] - 64) // 2 + 64, BREADTH), BF16)
        keep, send = call(
            functools.partial(halved, reach), [half, half], [], (keep, came), 1024 * 1024
        )
        if reach == 2:
            send, two_below, two_above = lax.optimization_barrier((send, two_below, two_above))
        came = traded(send, "grp", reach)
        reach *= 2
    mine = keep.astype(F32) + came.astype(F32)
    for reach in [slabs // 2] + [2**at for at in range(1, slabs.bit_length() - 2)]:
        mine = mine.astype(BF16)
        mine = mine.astype(F32) + traded(mine, "depth", reach).astype(F32)
    other = traded(mine, "depth", 1)
    two, three = call(
        functools.partial(spread_out, 1.0 / math.sqrt(cells), 1.0 / math.sqrt(cells / 8)),
        [
            jax.ShapeDtypeStruct((27, 16, 32), F32),
            jax.ShapeDtypeStruct((27, share, 32), F32),
        ],
        [],
        (mine, other),
        2 * 64 * 1024,
    )

    (cells_back,) = call(
        backward_two,
        [jax.ShapeDtypeStruct((pool_rows, 64, 2 * BREADTH), BF16)],
        [
            pltpu.VMEM((height + 4, 512, BREADTH), BF16),
            shift,
            pltpu.VMEM((2 * BREADTH, 2 * BREADTH), BF16),
        ],
        (two_below, low, high, two_above, back),
        2 * 8 * 128 * 2048 * 128,
    )
    input_grad = jnp.transpose(
        cells_back.reshape(pool_rows, 2, 2, chans, breadth), (3, 1, 0, 2, 4)
    ).reshape(inputs.shape)
    weight_grad_two = jnp.transpose(two, (0, 2, 1)).reshape(weight_two.shape)
    return (input_grad, weight_grad_two, three.reshape(weight_three.shape))


def solution(mesh):
    placed = (
        P(None, "depth", "grp", None),
        P(),
        P(None, None, None, "grp", None),
        P("grp", "depth", None, None),
    )
    return jax.shard_map(
        on_device,
        mesh=mesh,
        in_specs=placed,
        out_specs=(P(None, "depth", "grp", None), P(), P(None, None, None, "grp", None)),
        check_vma=False,
    )
```

time: 146 us -> 150 us (1.027)
  starting transfers between devices: 73.6 us -> 94.8 us
  local copies, waits for them, and re-layouts: 16.2 us -> 7.5 us
  other arithmetic: 5.17 us -> 0.12 us
  waiting for transfers between devices: 38.5 us -> 33.8 us
    ppermute x0 -> x10, starting transfers between devices: none -> 54.3 us  [traded(): lax.ppermute(block, axis, [(i, i ^ reach) for i in range(lax.axis_size(ax...]
    all_to_all x5 -> x1, starting transfers between devices: 42.1 us -> 7.5 us  [exchange(): return lax.all_to_all(blocks, axis, 0, 0, tiled=True)]
    all_to_all x5 -> x1, waiting for transfers between devices: 34.4 us -> 0.01 us  [exchange(): return lax.all_to_all(blocks, axis, 0, 0, tiled=True)]
    ppermute x0 -> x10, waiting for transfers between devices: none -> 26.8 us  [traded(): lax.ppermute(block, axis, [(i, i ^ reach) for i in range(lax.axis_size(ax...]
    unnamed x25 -> x23, local copies, waits for them, and re-layouts: 11.1 us -> 6.11 us
    unnamed x7 -> x0, other arithmetic: 4.35 us -> none
    ppermute x5, waiting for transfers between devices: 0.01 us -> 2.92 us  [neighbours(): lax.ppermute(last, axis, shifted(axis, 1))]
    transpose x3 -> x0, local copies, waits for them, and re-layouts: 2.42 us -> none  [the longest x1 0.89 us: on_device(): jnp.transpose(weight_three, (3, 1, 2, 0, 4)).reshape(share, 864)]
  transfers between devices with their start and end apart: 15 -> 21, of which waited for: 5 -> 14; matrix products, arithmetic and copies ran while one was open for 7% -> 1% of each run, Pallas kernels for 5% -> 5%
where the time goes in v3:
time: 150 us; the launch traced here: 149 us
  starting transfers between devices  94.8 us (63%)
  waiting for transfers between devices  33.8 us (23%)
  Pallas kernels  11.8 us (8%)
  local copies, waits for them, and re-layouts  7.5 us (5%)
    ppermute x10, starting transfers between devices, traded(): lax.ppermute(block, axis, [(i, i ^ reach) for i in range(lax.axis_size(ax...  54.3 us
    ppermute x10, waiting for transfers between devices, traded(): lax.ppermute(block, axis, [(i, i ^ reach) for i in range(lax.axis_size(ax...  26.8 us
    ppermute x5, starting transfers between devices, neighbours(): lax.ppermute(last, axis, shifted(axis, 1))  20.1 us
    ppermute x5, starting transfers between devices, neighbours(): lax.ppermute(first, axis, shifted(axis, -1))  12.8 us
    pallas_call x11, Pallas kernels, call(): pl.pallas_call(kernel, out_shape=outs, in_specs=specs, out_specs=[pl.Bloc...  11.8 us
    all_to_all x1, starting transfers between devices, exchange(): return lax.all_to_all(blocks, axis, 0, 0, tiled=True)  7.5 us
    unnamed x23, local copies, waits for them, and re-layouts  6.11 us
    ppermute x5, waiting for transfers between devices, neighbours(): lax.ppermute(first, axis, shifted(axis, -1))  4.07 us
  transfers between devices with their start and end apart: 21, of which 14 were waited for; matrix products, arithmetic and copies ran while one was open for 1% of the time, Pallas kernels for 5%

profile of v3, /device:TPU:1, one launch (start us, length us, event | category | flops | bytes accessed | tf_op | source)
XLA Modules:
  0.0 149.0 jit_solution(12341604921529575352)
XLA Ops:
  0.7 1.1 copy.15
  1.8 1.4 collective-permute-start.1
  3.3 4.6 %collective-permute-start = (bf16[7,2,16,256]{3,2,0,1:T(8,128)(2,1)S(1)}, bf16[7,2,16,256]{3,2,0,1:T(8,128)(2,1)S(1)}, u32[]{:S(2)}, u32[]{:S(2)}) collective-permute-start(bf16[7,2,16,256]{3,2,0,1:T(8,128)(2,1)S(1)} %slice.32), channel_id=1, source_target_pairs={{0,1},{1,2},{2,3},{3,4},{4,5},{5,6},{6,7},{8,9},{9,10},{10,11},{11... | collective-permute-start | bytes 344072 | tf_op jit(solution)/shard_map/ppermute | solution.py:358
  8.1 1.6 %collective-permute-done = bf16[7,2,16,256]{3,2,0,1:T(8,128)(2,1)S(1)} collective-permute-done((bf16[7,2,16,256]{3,2,0,1:T(8,128)(2,1)S(1)}, bf16[7,2,16,256]{3,2,0,1:T(8,128)(2,1)S(1)}, u32[]{:S(2)}, u32[]{:S(2)}) %collective-permute-start) | collective-permute-done | bytes 114720 | tf_op jit(solution)/shard_map/ppermute | solution.py:358
  9.7 5.5 %collective-permute-start.2 = (bf16[30,16,256]{2,1,0:T(8,128)(2,1)S(1)}, bf16[30,16,256]{2,1,0:T(8,128)(2,1)S(1)}, u32[]{:S(2)}, u32[]{:S(2)}) collective-permute-start(bf16[30,16,256]{2,1,0:T(8,128)(2,1)S(1)} %pad_maximum_fusion), channel_id=1, source_target_pairs={{0,8},{8,16},{16,24},{24,32},{32,40},{40,48},{48,56},{56,64},{64,7... | collective-permute-start | bytes 737288 | tf_op jit(solution)/shard_map/ppermute | solution.py:358
  15.2 5.2 %collective-permute-start.3 = (bf16[30,16,256]{2,1,0:T(8,128)(2,1)S(1)}, bf16[30,16,256]{2,1,0:T(8,128)(2,1)S(1)}, u32[]{:S(2)}, u32[]{:S(2)}) collective-permute-start(bf16[30,16,256]{2,1,0:T(8,128)(2,1)S(1)} %pad_maximum_fusion.1), channel_id=1, source_target_pairs={{8,0},{16,8},{24,16},{32,24},{40,32},{48,40},{56,48},{64,56},{72,6... | collective-permute-start | bytes 737288 | tf_op jit(solution)/shard_map/ppermute | solution.py:359
  20.5 0.8 shard_map.69
  21.3 7.5 %all-to-all-start = ((bf16[8,8,2432]{2,1,0:T(8,128)(2,1)}), bf16[8,8,2432]{2,1,0:T(8,128)(2,1)}, u32[]{:S(2)}, u32[]{:S(2)}) async-start(bf16[8,8,2432]{2,1,0:T(8,128)(2,1)} %shard_map.69), calls=%async_computation | async-start | bytes 622592 | tf_op jit(solution)/shard_map/all_to_all | solution.py:364
  29.4 0.8 copy-done
  30.2 0.7 copy-done.6
  30.9 0.7 copy-done.8
  31.6 0.9 copy-done.4
  32.5 0.9 copy-done.7
  33.4 0.9 copy-done.9
  34.4 3.2 %shard_map.68 = (bf16[14,32,128]{2,1,0:T(8,128)(2,1)}, f32[10,256,128]{2,1,0:T(8,128)S(1)}, bf16[30,256,128]{2,1,0:T(8,128)(2,1)S(1)}) custom-call(bf16[16,2,16,256]{3,2,1,0:T(8,128)(2,1)S(1)} %bitcast.35, bf16[30,16,256]{2,1,0:T(8,128)(2,1)S(1)} %copy-done.7, bf16[30,16,256]{2,1,0:T(8,128)(2,1)S(1)} %copy-done.9, bf16[7,2,16,256]{3,2,1,0:T(8,128)(2,1)S(1)} %copy.10.top, ...), custom_call_target="tpu_custom_call" | custom-call | flops 939524096 | bytes 4898816 | tf_op jit(solution)/shard_map/pallas_call | solution.py:20
  37.6 1.9 %collective-permute-start.5 = (bf16[14,32,128]{2,1,0:T(8,128)(2,1)}, bf16[14,32,128]{2,1,0:T(8,128)(2,1)S(1)}, u32[]{:S(2)}, u32[]{:S(2)}) collective-permute-start(bf16[14,32,128]{2,1,0:T(8,128)(2,1)} %get-tuple-element.32.own), channel_id=1, source_target_pairs={{8,0},{16,8},{24,16},{32,24},{40,32},{48,40},{56,48},{64,56},{72,6... | collective-permute-start | bytes 344072 | tf_op jit(solution)/shard_map/ppermute | solution.py:359
  39.5 3.9 %collective-permute-start.4 = (bf16[14,32,128]{2,1,0:T(8,128)(2,1)}, bf16[14,32,128]{2,1,0:T(8,128)(2,1)S(1)}, u32[]{:S(2)}, u32[]{:S(2)}) collective-permute-start(bf16[14,32,128]{2,1,0:T(8,128)(2,1)} %get-tuple-element.32.own), channel_id=1, source_target_pairs={{0,8},{8,16},{16,24},{24,32},{32,40},{40,48},{48,56},{56,64},{64,7... | collective-permute-start | bytes 344072 | tf_op jit(solution)/shard_map/ppermute | solution.py:358
  43.4 0.7 collective-permute-done.5.above
  44.1 1.3 collective-permute-done.4.below
  45.5 2.4 %shard_map.70 = (bf16[12,64,128]{2,1,0:T(8,128)(2,1)S(1)}, bf16[14,288,128]{2,1,0:T(8,128)(2,1)S(1)}, bf16[10,32,128]{2,1,0:T(8,128)(2,1)S(1)}, f32[10,32,128]{2,1,0:T(8,128)S(1)}, bf16[10,32,128]{2,1,0:T(8,128)(2,1)S(1)}) custom-call(bf16[14,32,128]{2,1,0:T(8,128)(2,1)S(1)} %collective-permute-done.4.below, bf16[14,32,128]{2,1,0:T(8,128)(2,1)} %get-tuple-element.32.own, ...), custom_call_target="tpu_custom_call" | custom-call | flops 339738624 | bytes 2211840 | tf_op jit(solution)/shard_map/pallas_call | solution.py:20
  47.9 4.2 %collective-permute-start.6 = (bf16[10,32,128]{2,1,0:T(8,128)(2,1)S(1)}, bf16[10,32,128]{2,1,0:T(8,128)(2,1)S(1)}, u32[]{:S(2)}, u32[]{:S(2)}) collective-permute-start(bf16[10,32,128]{2,1,0:T(8,128)(2,1)S(1)} %get-tuple-element.34), channel_id=1, source_target_pairs={{0,8},{8,16},{16,24},{24,32},{32,40},{40,48},{48,56},{56,64},{64,7... | collective-permute-start | bytes 245768 | tf_op jit(solution)/shard_map/ppermute | solution.py:358
  52.1 1.9 %collective-permute-start.7 = (bf16[10,32,128]{2,1,0:T(8,128)(2,1)S(1)}, bf16[10,32,128]{2,1,0:T(8,128)(2,1)S(1)}, u32[]{:S(2)}, u32[]{:S(2)}) collective-permute-start(bf16[10,32,128]{2,1,0:T(8,128)(2,1)S(1)} %get-tuple-element.36), channel_id=1, source_target_pairs={{8,0},{16,8},{24,16},{32,24},{40,32},{48,40},{56,48},{64,56},{72,6... | collective-permute-start | bytes 245768 | tf_op jit(solution)/shard_map/ppermute | solution.py:359
  54.7 3.2 %collective-permute-done.7.above = bf16[10,32,128]{2,1,0:T(8,128)(2,1)S(1)} collective-permute-done((bf16[10,32,128]{2,1,0:T(8,128)(2,1)S(1)}, bf16[10,32,128]{2,1,0:T(8,128)(2,1)S(1)}, u32[]{:S(2)}, u32[]{:S(2)}) %collective-permute-start.7) | collective-permute-done | bytes 81952 | tf_op jit(solution)/shard_map/ppermute | solution.py:359
  57.9 0.9 shard_map.72
  58.8 1.9 %collective-permute-start.10 = (bf16[10,128,128]{2,1,0:T(8,128)(2,1)S(1)}, bf16[10,128,128]{2,1,0:T(8,128)(2,1)S(1)}, u32[]{:S(2)}, u32[]{:S(2)}) collective-permute-start(bf16[10,128,128]{2,1,0:T(8,128)(2,1)S(1)} %get-tuple-element.46.high), channel_id=1, source_target_pairs={{0,8},{8,16},{16,24},{24,32},{32,40},{40,48},{48,56},{56,64},{64,7... | collective-permute-start | bytes 983048 | tf_op jit(solution)/shard_map/ppermute | solution.py:358
  60.7 2.4 %collective-permute-start.11 = (bf16[10,128,128]{2,1,0:T(8,128)(2,1)S(1)}, bf16[10,128,128]{2,1,0:T(8,128)(2,1)S(1)}, u32[]{:S(2)}, u32[]{:S(2)}) collective-permute-start(bf16[10,128,128]{2,1,0:T(8,128)(2,1)S(1)} %get-tuple-element.47.low), channel_id=1, source_target_pairs={{8,0},{16,8},{24,16},{32,24},{40,32},{48,40},{56,48},{64,56},{72,6... | collective-permute-start | bytes 983048 | tf_op jit(solution)/shard_map/ppermute | solution.py:359
  63.2 1.9 %collective-permute-start.8 = (f32[320,128]{1,0:T(8,128)S(1)}, f32[320,128]{1,0:T(8,128)S(1)}, u32[]{:S(2)}, u32[]{:S(2)}) collective-permute-start(f32[320,128]{1,0:T(8,128)S(1)} %get-tuple-element.42), channel_id=1, source_target_pairs={{0,8},{8,0},{16,24},{24,16},{32,40},{40,32},{48,56},{56,48},{64,72... | collective-permute-start | bytes 491528 | tf_op jit(solution)/shard_map/ppermute | solution.py:368
  65.1 1.4 collective-permute-done.8.came
  66.5 3.7 %collective-permute-start.9 = (bf16[192,128]{1,0:T(8,128)(2,1)S(1)}, bf16[192,128]{1,0:T(8,128)(2,1)S(1)}, u32[]{:S(2)}, u32[]{:S(2)}) collective-permute-start(bf16[192,128]{1,0:T(8,128)(2,1)S(1)} %get-tuple-element.44), channel_id=1, source_target_pairs={{0,1},{1,0},{2,3},{3,2},{4,5},{5,4},{6,7},{7,6},{8,9},{9,8},{10,11... | collective-permute-start | bytes 147464 | tf_op jit(solution)/shard_map/ppermute | solution.py:368
  70.1 2.0 %collective-permute-done.9.came = bf16[192,128]{1,0:T(8,128)(2,1)S(1)} collective-permute-done((bf16[192,128]{1,0:T(8,128)(2,1)S(1)}, bf16[192,128]{1,0:T(8,128)(2,1)S(1)}, u32[]{:S(2)}, u32[]{:S(2)}) %collective-permute-start.9) | collective-permute-done | bytes 49184 | tf_op jit(solution)/shard_map/ppermute | solution.py:368
  72.1 4.4 %collective-permute-start.12 = (bf16[128,128]{1,0:T(8,128)(2,1)S(1)}, bf16[128,128]{1,0:T(8,128)(2,1)S(1)}, u32[]{:S(2)}, u32[]{:S(2)}) collective-permute-start(bf16[128,128]{1,0:T(8,128)(2,1)S(1)} %get-tuple-element.52), channel_id=1, source_target_pairs={{0,2},{1,3},{2,0},{3,1},{4,6},{5,7},{6,4},{7,5},{8,10},{9,11},{10,... | collective-permute-start | bytes 98312 | tf_op jit(solution)/shard_map/ppermute | solution.py:368
  76.5 1.8 %collective-permute-done.12.came = bf16[128,128]{1,0:T(8,128)(2,1)S(1)} collective-permute-done((bf16[128,128]{1,0:T(8,128)(2,1)S(1)}, bf16[128,128]{1,0:T(8,128)(2,1)S(1)}, u32[]{:S(2)}, u32[]{:S(2)}) %collective-permute-start.12) | collective-permute-done | bytes 32800 | tf_op jit(solution)/shard_map/ppermute | solution.py:368
  78.3 4.4 %collective-permute-start.13 = (bf16[96,128]{1,0:T(8,128)(2,1)S(1)}, bf16[96,128]{1,0:T(8,128)(2,1)S(1)}, u32[]{:S(2)}, u32[]{:S(2)}) collective-permute-start(bf16[96,128]{1,0:T(8,128)(2,1)S(1)} %get-tuple-element.54), channel_id=1, source_target_pairs={{0,4},{1,5},{2,6},{3,7},{4,0},{5,1},{6,2},{7,3},{8,12},{9,13},{10,... | collective-permute-start | bytes 73736 | tf_op jit(solution)/shard_map/ppermute | solution.py:368
  82.7 1.7 %collective-permute-done.13 = bf16[96,128]{1,0:T(8,128)(2,1)S(1)} collective-permute-done((bf16[96,128]{1,0:T(8,128)(2,1)S(1)}, bf16[96,128]{1,0:T(8,128)(2,1)S(1)}, u32[]{:S(2)}, u32[]{:S(2)}) %collective-permute-start.13) | collective-permute-done | bytes 24608 | tf_op jit(solution)/shard_map/ppermute | solution.py:368
  84.4 15.6 %collective-permute-start.14 = (bf16[96,128]{1,0:T(8,128)(2,1)S(1)}, bf16[96,128]{1,0:T(8,128)(2,1)S(1)}, u32[]{:S(2)}, u32[]{:S(2)}) collective-permute-start(bf16[96,128]{1,0:T(8,128)(2,1)S(1)} %add_convert_fusion.4), channel_id=1, source_target_pairs={{0,256},{8,264},{16,272},{24,280},{32,288},{40,296},{48,304},{56,3... | collective-permute-start | bytes 73736 | tf_op jit(solution)/shard_map/ppermute | solution.py:368
  100.0 1.2 collective-permute-done.14
  101.2 1.9 %collective-permute-start.15 = (bf16[96,128]{1,0:T(8,128)(2,1)S(1)}, bf16[96,128]{1,0:T(8,128)(2,1)S(1)}, u32[]{:S(2)}, u32[]{:S(2)}) collective-permute-start(bf16[96,128]{1,0:T(8,128)(2,1)S(1)} %add_convert_fusion.3), channel_id=1, source_target_pairs={{0,16},{8,24},{16,0},{24,8},{32,48},{40,56},{48,32},{56,40},{64,80... | collective-permute-start | bytes 73736 | tf_op jit(solution)/shard_map/ppermute | solution.py:368
  103.1 2.6 %collective-permute-done.15 = bf16[96,128]{1,0:T(8,128)(2,1)S(1)} collective-permute-done((bf16[96,128]{1,0:T(8,128)(2,1)S(1)}, bf16[96,128]{1,0:T(8,128)(2,1)S(1)}, u32[]{:S(2)}, u32[]{:S(2)}) %collective-permute-start.15) | collective-permute-done | bytes 24608 | tf_op jit(solution)/shard_map/ppermute | solution.py:368
  105.8 1.9 %collective-permute-start.16 = (bf16[96,128]{1,0:T(8,128)(2,1)S(1)}, bf16[96,128]{1,0:T(8,128)(2,1)S(1)}, u32[]{:S(2)}, u32[]{:S(2)}) collective-permute-start(bf16[96,128]{1,0:T(8,128)(2,1)S(1)} %add_convert_fusion.2), channel_id=1, source_target_pairs={{0,32},{8,40},{16,48},{24,56},{32,0},{40,8},{48,16},{56,24},{64,96... | collective-permute-start | bytes 73736 | tf_op jit(solution)/shard_map/ppermute | solution.py:368
  107.7 3.5 %collective-permute-done.16 = bf16[96,128]{1,0:T(8,128)(2,1)S(1)} collective-permute-done((bf16[96,128]{1,0:T(8,128)(2,1)S(1)}, bf16[96,128]{1,0:T(8,128)(2,1)S(1)}, u32[]{:S(2)}, u32[]{:S(2)}) %collective-permute-start.16) | collective-permute-done | bytes 24608 | tf_op jit(solution)/shard_map/ppermute | solution.py:368
  111.3 2.3 %collective-permute-start.17 = (bf16[96,128]{1,0:T(8,128)(2,1)S(1)}, bf16[96,128]{1,0:T(8,128)(2,1)S(1)}, u32[]{:S(2)}, u32[]{:S(2)}) collective-permute-start(bf16[96,128]{1,0:T(8,128)(2,1)S(1)} %add_convert_fusion.1), channel_id=1, source_target_pairs={{0,64},{8,72},{16,80},{24,88},{32,96},{40,104},{48,112},{56,120},{... | collective-permute-start | bytes 73736 | tf_op jit(solution)/shard_map/ppermute | solution.py:368
  113.6 6.4 %collective-permute-done.17 = bf16[96,128]{1,0:T(8,128)(2,1)S(1)} collective-permute-done((bf16[96,128]{1,0:T(8,128)(2,1)S(1)}, bf16[96,128]{1,0:T(8,128)(2,1)S(1)}, u32[]{:S(2)}, u32[]{:S(2)}) %collective-permute-start.17) | collective-permute-done | bytes 24608 | tf_op jit(solution)/shard_map/ppermute | solution.py:368
  120.0 7.4 %collective-permute-start.18 = (bf16[96,128]{1,0:T(8,128)(2,1)S(1)}, bf16[96,128]{1,0:T(8,128)(2,1)S(1)}, u32[]{:S(2)}, u32[]{:S(2)}) collective-permute-start(bf16[96,128]{1,0:T(8,128)(2,1)S(1)} %add_convert_fusion), channel_id=1, source_target_pairs={{0,128},{8,136},{16,144},{24,152},{32,160},{40,168},{48,176},{56,1... | collective-permute-start | bytes 73736 | tf_op jit(solution)/shard_map/ppermute | solution.py:368
  127.4 6.2 %collective-permute-done.18 = bf16[96,128]{1,0:T(8,128)(2,1)S(1)} collective-permute-done((bf16[96,128]{1,0:T(8,128)(2,1)S(1)}, bf16[96,128]{1,0:T(8,128)(2,1)S(1)}, u32[]{:S(2)}, u32[]{:S(2)}) %collective-permute-start.18) | collective-permute-done | bytes 24608 | tf_op jit(solution)/shard_map/ppermute | solution.py:368
  133.6 10.9 %collective-permute-start.19 = (f32[96,128]{1,0:T(8,128)S(1)}, f32[96,128]{1,0:T(8,128)S(1)}, u32[]{:S(2)}, u32[]{:S(2)}) collective-permute-start(f32[96,128]{1,0:T(8,128)S(1)} %convert_add_fusion.mine), channel_id=1, source_target_pairs={{0,8},{8,0},{16,24},{24,16},{32,40},{40,32},{48,56},{56,48},{64,72... | collective-permute-start | bytes 147464 | tf_op jit(solution)/shard_map/ppermute | solution.py:368
  144.5 2.5 %shard_map.75 = bf16[8,64,256]{2,1,0:T(8,128)(2,1)S(1)} custom-call(bf16[10,128,128]{2,1,0:T(8,128)(2,1)S(1)} %collective-permute-done.10.below, bf16[10,128,128]{2,1,0:T(8,128)(2,1)S(1)} %get-tuple-element.47.low, bf16[10,128,128]{2,1,0:T(8,128)(2,1)S(1)} %get-tuple-element.46.high, bf16[10,128,128]{2,1,0:T(8,128)(2,1)S(1)} %collective-permute-done.11.above, ...), custom_call_target="tpu_custom_call" | custom-call | flops 536870912 | bytes 2097152 | tf_op jit(solution)/shard_map/pallas_call | solution.py:20
  147.3 0.8 reshape.31
  148.1 1.0 shard_map.77
  (47 shorter events, 2.0 us)
Async XLA Ops:
  0.6 19.8 %copy-start.10 = (bf16[8,1,64,128]{3,2,1,0:T(8,128)(2,1)S(1)}, bf16[8,1,64,128]{3,2,1,0:T(8,128)(2,1)}, u32[]{:S(2)}) copy-start(bf16[8,1,64,128]{3,2,1,0:T(8,128)(2,1)} %param.7) | copy-start | bytes 393220
  0.6 19.9 %copy-start.5 = (bf16[3,3,3,8,32]{4,3,2,1,0:T(8,128)(2,1)S(1)}, bf16[3,3,3,8,32]{4,3,2,1,0:T(8,128)(2,1)}, u32[]{:S(2)}) copy-start(bf16[3,3,3,8,32]{4,3,2,1,0:T(8,128)(2,1)} %param.6) | copy-start | bytes 41476
  1.8 27.0 %copy-start.2 = (bf16[3,3,3,32,16]{3,4,2,1,0:T(8,128)(2,1)S(1)}, bf16[3,3,3,32,16]{3,4,2,1,0:T(8,128)(2,1)}, u32[]{:S(2)}) copy-start(bf16[3,3,3,32,16]{3,4,2,1,0:T(8,128)(2,1)} %param.5) | copy-start | bytes 82948
  1.8 6.3 %collective-permute-start.1 = (bf16[7,2,16,256]{3,2,1,0:T(8,128)(2,1)S(1)}, bf16[7,2,16,256]{3,2,1,0:T(8,128)(2,1)S(1)}, u32[]{:S(2)}, u32[]{:S(2)}) collective-permute-start(bf16[7,2,16,256]{3,2,1,0:T(8,128)(2,1)S(1)} %slice.27), channel_id=1, source_target_pairs={{1,0},{2,1},{3,2},{4,3},{5,4},{6,5},{7,6},{9,8},{10,9},{11,10},{12... | collective-permute-start | bytes 344072 | tf_op jit(solution)/shard_map/ppermute | solution.py:359
  3.3 6.4 %collective-permute-start = (bf16[7,2,16,256]{3,2,0,1:T(8,128)(2,1)S(1)}, bf16[7,2,16,256]{3,2,0,1:T(8,128)(2,1)S(1)}, u32[]{:S(2)}, u32[]{:S(2)}) collective-permute-start(bf16[7,2,16,256]{3,2,0,1:T(8,128)(2,1)S(1)} %slice.32), channel_id=1, source_target_pairs={{0,1},{1,2},{2,3},{3,4},{4,5},{5,6},{6,7},{8,9},{9,10},{10,11},{11... | collective-permute-start | bytes 344072 | tf_op jit(solution)/shard_map/ppermute | solution.py:358
  8.1 20.7 %copy-start.3 = (bf16[7,2,16,256]{3,2,1,0:T(8,128)(2,1)}, bf16[7,2,16,256]{3,2,1,0:T(8,128)(2,1)S(1)}, u32[]{:S(2)}) copy-start(bf16[7,2,16,256]{3,2,1,0:T(8,128)(2,1)S(1)} %collective-permute-done.1.bottom) | copy-start | bytes 344068
  9.7 20.5 %collective-permute-start.2 = (bf16[30,16,256]{2,1,0:T(8,128)(2,1)S(1)}, bf16[30,16,256]{2,1,0:T(8,128)(2,1)S(1)}, u32[]{:S(2)}, u32[]{:S(2)}) collective-permute-start(bf16[30,16,256]{2,1,0:T(8,128)(2,1)S(1)} %pad_maximum_fusion), channel_id=1, source_target_pairs={{0,8},{8,16},{16,24},{24,32},{32,40},{40,48},{48,56},{56,64},{64,7... | collective-permute-start | bytes 737288 | tf_op jit(solution)/shard_map/ppermute | solution.py:358
  15.2 15.6 %collective-permute-start.3 = (bf16[30,16,256]{2,1,0:T(8,128)(2,1)S(1)}, bf16[30,16,256]{2,1,0:T(8,128)(2,1)S(1)}, u32[]{:S(2)}, u32[]{:S(2)}) collective-permute-start(bf16[30,16,256]{2,1,0:T(8,128)(2,1)S(1)} %pad_maximum_fusion.1), channel_id=1, source_target_pairs={{8,0},{16,8},{24,16},{32,24},{40,32},{48,40},{56,48},{64,56},{72,6... | collective-permute-start | bytes 737288 | tf_op jit(solution)/shard_map/ppermute | solution.py:359
  21.3 22.1 %all-to-all-start = ((bf16[8,8,2432]{2,1,0:T(8,128)(2,1)}), bf16[8,8,2432]{2,1,0:T(8,128)(2,1)}, u32[]{:S(2)}, u32[]{:S(2)}) async-start(bf16[8,8,2432]{2,1,0:T(8,128)(2,1)} %shard_map.69), calls=%async_computation | async-start | bytes 622592 | tf_op jit(solution)/shard_map/all_to_all | solution.py:364
  29.4 0.8 copy-start
  30.2 0.7 copy-start.6
  30.9 0.7 copy-start.8
  31.6 0.9 copy-start.4
  32.5 0.9 copy-start.7
  33.4 0.9 copy-start.9
  37.6 6.6 %collective-permute-start.5 = (bf16[14,32,128]{2,1,0:T(8,128)(2,1)}, bf16[14,32,128]{2,1,0:T(8,128)(2,1)S(1)}, u32[]{:S(2)}, u32[]{:S(2)}) collective-permute-start(bf16[14,32,128]{2,1,0:T(8,128)(2,1)} %get-tuple-element.32.own), channel_id=1, source_target_pairs={{8,0},{16,8},{24,16},{32,24},{40,32},{48,40},{56,48},{64,56},{72,6... | collective-permute-start | bytes 344072 | tf_op jit(solution)/shard_map/ppermute | solution.py:359
  39.5 6.0 %collective-permute-start.4 = (bf16[14,32,128]{2,1,0:T(8,128)(2,1)}, bf16[14,32,128]{2,1,0:T(8,128)(2,1)S(1)}, u32[]{:S(2)}, u32[]{:S(2)}) collective-permute-start(bf16[14,32,128]{2,1,0:T(8,128)(2,1)} %get-tuple-element.32.own), channel_id=1, source_target_pairs={{0,8},{8,16},{16,24},{24,32},{32,40},{40,48},{48,56},{56,64},{64,7... | collective-permute-start | bytes 344072 | tf_op jit(solution)/shard_map/ppermute | solution.py:358
  47.9 6.8 %collective-permute-start.6 = (bf16[10,32,128]{2,1,0:T(8,128)(2,1)S(1)}, bf16[10,32,128]{2,1,0:T(8,128)(2,1)S(1)}, u32[]{:S(2)}, u32[]{:S(2)}) collective-permute-start(bf16[10,32,128]{2,1,0:T(8,128)(2,1)S(1)} %get-tuple-element.34), channel_id=1, source_target_pairs={{0,8},{8,16},{16,24},{24,32},{32,40},{40,48},{48,56},{56,64},{64,7... | collective-permute-start | bytes 245768 | tf_op jit(solution)/shard_map/ppermute | solution.py:358
  52.1 5.8 %collective-permute-start.7 = (bf16[10,32,128]{2,1,0:T(8,128)(2,1)S(1)}, bf16[10,32,128]{2,1,0:T(8,128)(2,1)S(1)}, u32[]{:S(2)}, u32[]{:S(2)}) collective-permute-start(bf16[10,32,128]{2,1,0:T(8,128)(2,1)S(1)} %get-tuple-element.36), channel_id=1, source_target_pairs={{8,0},{16,8},{24,16},{32,24},{40,32},{48,40},{56,48},{64,56},{72,6... | collective-permute-start | bytes 245768 | tf_op jit(solution)/shard_map/ppermute | solution.py:359
  57.9 86.7 %copy-start.1 = (bf16[128,2048]{1,0:T(8,128)(2,1)S(1)}, bf16[128,2048]{1,0:T(8,128)(2,1)}, u32[]{:S(2)}) copy-start(bf16[128,2048]{1,0:T(8,128)(2,1)} %copy-done) | copy-start | bytes 1572868
  58.8 13.3 %collective-permute-start.10 = (bf16[10,128,128]{2,1,0:T(8,128)(2,1)S(1)}, bf16[10,128,128]{2,1,0:T(8,128)(2,1)S(1)}, u32[]{:S(2)}, u32[]{:S(2)}) collective-permute-start(bf16[10,128,128]{2,1,0:T(8,128)(2,1)S(1)} %get-tuple-element.46.high), channel_id=1, source_target_pairs={{0,8},{8,16},{16,24},{24,32},{32,40},{40,48},{48,56},{56,64},{64,7... | collective-permute-start | bytes 983048 | tf_op jit(solution)/shard_map/ppermute | solution.py:358
  60.7 11.4 %collective-permute-start.11 = (bf16[10,128,128]{2,1,0:T(8,128)(2,1)S(1)}, bf16[10,128,128]{2,1,0:T(8,128)(2,1)S(1)}, u32[]{:S(2)}, u32[]{:S(2)}) collective-permute-start(bf16[10,128,128]{2,1,0:T(8,128)(2,1)S(1)} %get-tuple-element.47.low), channel_id=1, source_target_pairs={{8,0},{16,8},{24,16},{32,24},{40,32},{48,40},{56,48},{64,56},{72,6... | collective-permute-start | bytes 983048 | tf_op jit(solution)/shard_map/ppermute | solution.py:359
  63.2 3.3 %collective-permute-start.8 = (f32[320,128]{1,0:T(8,128)S(1)}, f32[320,128]{1,0:T(8,128)S(1)}, u32[]{:S(2)}, u32[]{:S(2)}) collective-permute-start(f32[320,128]{1,0:T(8,128)S(1)} %get-tuple-element.42), channel_id=1, source_target_pairs={{0,8},{8,0},{16,24},{24,16},{32,40},{40,32},{48,56},{56,48},{64,72... | collective-permute-start | bytes 491528 | tf_op jit(solution)/shard_map/ppermute | solution.py:368
  66.5 5.6 %collective-permute-start.9 = (bf16[192,128]{1,0:T(8,128)(2,1)S(1)}, bf16[192,128]{1,0:T(8,128)(2,1)S(1)}, u32[]{:S(2)}, u32[]{:S(2)}) collective-permute-start(bf16[192,128]{1,0:T(8,128)(2,1)S(1)} %get-tuple-element.44), channel_id=1, source_target_pairs={{0,1},{1,0},{2,3},{3,2},{4,5},{5,4},{6,7},{7,6},{8,9},{9,8},{10,11... | collective-permute-start | bytes 147464 | tf_op jit(solution)/shard_map/ppermute | solution.py:368
  72.1 6.2 %collective-permute-start.12 = (bf16[128,128]{1,0:T(8,128)(2,1)S(1)}, bf16[128,128]{1,0:T(8,128)(2,1)S(1)}, u32[]{:S(2)}, u32[]{:S(2)}) collective-permute-start(bf16[128,128]{1,0:T(8,128)(2,1)S(1)} %get-tuple-element.52), channel_id=1, source_target_pairs={{0,2},{1,3},{2,0},{3,1},{4,6},{5,7},{6,4},{7,5},{8,10},{9,11},{10,... | collective-permute-start | bytes 98312 | tf_op jit(solution)/shard_map/ppermute | solution.py:368
  78.3 6.1 %collective-permute-start.13 = (bf16[96,128]{1,0:T(8,128)(2,1)S(1)}, bf16[96,128]{1,0:T(8,128)(2,1)S(1)}, u32[]{:S(2)}, u32[]{:S(2)}) collective-permute-start(bf16[96,128]{1,0:T(8,128)(2,1)S(1)} %get-tuple-element.54), channel_id=1, source_target_pairs={{0,4},{1,5},{2,6},{3,7},{4,0},{5,1},{6,2},{7,3},{8,12},{9,13},{10,... | collective-permute-start | bytes 73736 | tf_op jit(solution)/shard_map/ppermute | solution.py:368
  84.4 16.8 %collective-permute-start.14 = (bf16[96,128]{1,0:T(8,128)(2,1)S(1)}, bf16[96,128]{1,0:T(8,128)(2,1)S(1)}, u32[]{:S(2)}, u32[]{:S(2)}) collective-permute-start(bf16[96,128]{1,0:T(8,128)(2,1)S(1)} %add_convert_fusion.4), channel_id=1, source_target_pairs={{0,256},{8,264},{16,272},{24,280},{32,288},{40,296},{48,304},{56,3... | collective-permute-start | bytes 73736 | tf_op jit(solution)/shard_map/ppermute | solution.py:368
  101.2 4.6 %collective-permute-start.15 = (bf16[96,128]{1,0:T(8,128)(2,1)S(1)}, bf16[96,128]{1,0:T(8,128)(2,1)S(1)}, u32[]{:S(2)}, u32[]{:S(2)}) collective-permute-start(bf16[96,128]{1,0:T(8,128)(2,1)S(1)} %add_convert_fusion.3), channel_id=1, source_target_pairs={{0,16},{8,24},{16,0},{24,8},{32,48},{40,56},{48,32},{56,40},{64,80... | collective-permute-start | bytes 73736 | tf_op jit(solution)/shard_map/ppermute | solution.py:368
  105.8 5.5 %collective-permute-start.16 = (bf16[96,128]{1,0:T(8,128)(2,1)S(1)}, bf16[96,128]{1,0:T(8,128)(2,1)S(1)}, u32[]{:S(2)}, u32[]{:S(2)}) collective-permute-start(bf16[96,128]{1,0:T(8,128)(2,1)S(1)} %add_convert_fusion.2), channel_id=1, source_target_pairs={{0,32},{8,40},{16,48},{24,56},{32,0},{40,8},{48,16},{56,24},{64,96... | collective-permute-start | bytes 73736 | tf_op jit(solution)/shard_map/ppermute | solution.py:368
  111.3 8.7 %collective-permute-start.17 = (bf16[96,128]{1,0:T(8,128)(2,1)S(1)}, bf16[96,128]{1,0:T(8,128)(2,1)S(1)}, u32[]{:S(2)}, u32[]{:S(2)}) collective-permute-start(bf16[96,128]{1,0:T(8,128)(2,1)S(1)} %add_convert_fusion.1), channel_id=1, source_target_pairs={{0,64},{8,72},{16,80},{24,88},{32,96},{40,104},{48,112},{56,120},{... | collective-permute-start | bytes 73736 | tf_op jit(solution)/shard_map/ppermute | solution.py:368
  120.0 13.5 %collective-permute-start.18 = (bf16[96,128]{1,0:T(8,128)(2,1)S(1)}, bf16[96,128]{1,0:T(8,128)(2,1)S(1)}, u32[]{:S(2)}, u32[]{:S(2)}) collective-permute-start(bf16[96,128]{1,0:T(8,128)(2,1)S(1)} %add_convert_fusion), channel_id=1, source_target_pairs={{0,128},{8,136},{16,144},{24,152},{32,160},{40,168},{48,176},{56,1... | collective-permute-start | bytes 73736 | tf_op jit(solution)/shard_map/ppermute | solution.py:368
  133.6 14.5 %collective-permute-start.19 = (f32[96,128]{1,0:T(8,128)S(1)}, f32[96,128]{1,0:T(8,128)S(1)}, u32[]{:S(2)}, u32[]{:S(2)}) collective-permute-start(f32[96,128]{1,0:T(8,128)S(1)} %convert_add_fusion.mine), channel_id=1, source_target_pairs={{0,8},{8,0},{16,24},{24,16},{32,40},{40,32},{48,56},{56,48},{64,72... | collective-permute-start | bytes 147464 | tf_op jit(solution)/shard_map/ppermute | solution.py:368

commit v4 on v3

--- a/solution.py
+++ b/solution.py
@@ -12,6 +12,17 @@
 F32 = jnp.float32
 BF16 = jnp.bfloat16
 BREADTH = 128
+DEPTH = ("yl", "z", "core")
+GROUP = ("yh", "x")
+NEAR = ("yl", "core", "yh", "x")
+
+
+def axis_count(names):
+    return math.prod(lax.axis_size(name) for name in names)
+
+
+def group_index():
+    return lax.axis_index("yh") * lax.axis_size("x") + lax.axis_index("x")
 
 
 def call(kernel, outs, scratch, args, flops):
@@ -36,6 +47,10 @@
     return lax.dot_general(left, right, (((1,), (1,)), ((), ())), preferred_element_type=F32)
 
 
+def dot_tn(left, right):
+    return lax.dot_general(left, right, (((0,), (0,)), ((), ())), preferred_element_type=F32)
+
+
 def indicator(shape, test):
     row = lax.broadcasted_iota(jnp.int32, shape, 0)
     col = lax.broadcasted_iota(jnp.int32, shape, 1)
@@ -65,44 +80,44 @@
     return indicator((2 * BREADTH, 2 * BREADTH), test)
 
 
-def weights_two(plain, turned, ahead, back):
-    def blocks(source, outs, ins, flip):
-        per = BREADTH // ins
-        total = []
-        for part in range(64 // per):
-            summed = jnp.zeros((outs, BREADTH), F32)
-            for at in range(per):
-                place = part * per + at
-                b, e, a = place // 16, (place // 4) % 4, place % 4
-                if max(a, b, e) > 2:
-                    continue
-                if flip:
-                    a, b, e = 2 - a, 2 - b, 2 - e
-                spread = indicator((ins, BREADTH), lambda row, col: col == row + at * ins)
-                summed = summed + dot(source[a * 9 + b * 3 + e], spread)
-            total.append(summed)
-        return jnp.concatenate(total, axis=1)
-
-    def phases(out, base, outs, ins, row_of):
-        for phase in range(8):
-            deep, high, wide = phase // 4, (phase // 2) % 2, phase % 2
-            move = (high * 16 + wide * 4 + deep) * ins
-            full = pltpu.roll(base, move, 1) if move else base
-            at = row_of(deep, high, wide) * outs
-            out[at : at + outs, :] = full.astype(BF16)
-
-    phases(ahead, blocks(plain, 32, 16, False), 32, 16, lambda d, h, w: d * 4 + h * 2 + w)
-    phases(back, blocks(turned, 16, 32, True), 16, 32, lambda d, h, w: w * 4 + d * 2 + h)
+def weights_two(out, turned, flip):
+    outs, ins = (16, 32) if flip else (32, 16)
+    per = BREADTH // ins
+    total = []
+    for part in range(64 // per):
+        summed = jnp.zeros((outs, BREADTH), F32)
+        for at in range(per):
+            place = part * per + at
+            b, e, a = place // 16, (place // 4) % 4, place % 4
+            if max(a, b, e) > 2:
+                continue
+            if flip:
+                a, b, e = 2 - a, 2 - b, 2 - e
+            spread = indicator((ins, BREADTH), lambda row, col: col == row + at * ins)
+            tap = turned[a * 9 + b * 3 + e]
+            summed = summed + (dot(tap, spread) if flip else dot_tn(tap, spread))
+        total.append(summed)
+    base = jnp.concatenate(total, axis=1)
+    for phase in range(8):
+        deep, high, wide = phase // 4, (phase // 2) % 2, phase % 2
+        move = (high * 16 + wide * 4 + deep) * ins
+        full = pltpu.roll(base, move, 1) if move else base
+        at = (wide * 4 + deep * 2 + high if flip else phase) * outs
+        out[at : at + outs, :] = full.astype(BF16)
+
+
+def weights_ahead(turned, out):
+    weights_two(out, turned, False)
 
 
 def inside(at, rows):
-    return jnp.logical_and(at >= 0, at < rows * lax.axis_size("grp"))
+    return jnp.logical_and(at >= 0, at < rows * axis_count(GROUP))
 
 
 def forward_two(own, below, above, top, bottom, weight, pooled, slope, parts, split):
     split[...] = splitter()
     first = pooled.shape[0] - 6
-    first = first * lax.axis_index("grp") - 3
+    first = first * group_index() - 3
     edge = top.shape[0]
     height = own.shape[0]
 
@@ -226,18 +241,13 @@
     rows = grads.shape[0]
     left = jnp.concatenate([grads[row] for row in range(2, rows - 2)], axis=1)
     full = dot_nt(left, side_by_side(parts, 2, rows - 4, 3))
-    full = jnp.concatenate([full, jnp.zeros((full.shape[0], 160), F32)], axis=1)
-    for half in range(2):
-        for to in range(8):
-            for part in range(4):
-                lane = (half * 4 + part) * BREADTH
-                at = to * 32 + part * 8
-                out[half, at : at + 8, :] = full[to * 8 : to * 8 + 8, lane : lane + BREADTH]
-
-
-def middle_two(below, own, above, slope, parts, three, low, high, keep, send):
+    out[:, :864] = full
+    out[:, 864:] = jnp.zeros((full.shape[0], 160), F32)
+
+
+def middle_two(below, own, above, slope, parts, three, low, high, lines):
     rows = own.shape[0] - 2
-    first = rows * lax.axis_index("grp") - 1
+    first = rows * group_index() - 1
     left = []
     for row in range(rows + 2):
         pool = own[row] + below[row].astype(F32) + above[row].astype(F32)
@@ -274,11 +284,14 @@
         moved = pltpu.roll(two, 96 + off * 16, 1) if off != 2 else two
         rest = jnp.where(slot == off, moved, rest)
     dense.append(rest)
-    second = jnp.bitwise_and(lax.axis_index("depth"), 1) != 0
-    one = jnp.concatenate(dense[:2] + [three[0]], axis=0)
-    two = jnp.concatenate(dense[2:] + [three[1]], axis=0)
-    keep[...] = jnp.where(second, two, one)
-    send[...] = jnp.where(second, one, two)
+    for to in range(32):
+        quarter, group = to // 8, to % 8
+        for part in range(2):
+            lane = (quarter * 2 + part) * BREADTH
+            block = three[group * 8 : group * 8 + 8, lane : lane + BREADTH]
+            lines[to, part * 8 : part * 8 + 8, :] = block
+        for block in range(4):
+            lines[to, 16 + block : 17 + block, :] = dense[block][to : to + 1]
 
 
 def slot_of(b, e, a):
@@ -287,22 +300,8 @@
     return ((b, 3), (b, 7), (3, b))[a]
 
 
-def halved(bit, mine, came, keep, send):
-    count = (mine.shape[0] - 64) // 32
-    total = (mine[...].astype(F32) + came[...].astype(F32)).astype(BF16)
-    keep[:64, :] = total[:64]
-    send[:64, :] = total[:64]
-    group = lax.axis_index("grp")
-    on = jnp.bitwise_and(group, bit) != 0
-    for at in range(count // 2):
-        zero, one = 64 + 64 * at, 96 + 64 * at
-        to = 64 + 32 * at
-        first, second = total[zero : zero + 32], total[one : one + 32]
-        keep[to : to + 32, :] = jnp.where(on, second, first)
-        send[to : to + 32, :] = jnp.where(on, first, second)
-
-
-def backward_two(below, low, high, above, weight, out, parts, shift, join):
+def backward_two(below, low, high, above, turned, out, parts, shift, join, weight):
+    weights_two(weight, turned, True)
     shift[...] = shifter()
     join[...] = joiner()
     for row in range(low.shape[0]):
@@ -329,18 +328,18 @@
         out[row + 1] = joined[64:]
 
 
-def spread_out(scale_two, scale_three, mine, other, two, three):
-    second = jnp.bitwise_and(lax.axis_index("depth"), 1) != 0
-    one, another = mine[...], other[...]
-    lower, upper = jnp.where(second, another, one), jnp.where(second, one, another)
-    flat = jnp.transpose(jnp.concatenate([lower[:64], upper[:64]], axis=0) * scale_two)
-    for tap in range(27):
-        a, b, e = tap // 9, (tap // 3) % 3, tap % 3
-        block, slot = slot_of(b, e, a)
-        two[tap] = flat[slot * 16 : slot * 16 + 16, block * 32 : block * 32 + 32]
+def spread_out(scale_two, scale_three, lines, two, three):
+    for block in range(4):
+        rows = [lines[at, 16 + block : 17 + block, :].astype(F32) for at in range(32)]
+        flat = jnp.transpose(jnp.concatenate(rows * 4, axis=0) * scale_two)
+        for tap in range(27):
+            a, b, e = tap // 9, (tap // 3) % 3, tap % 3
+            where, slot = slot_of(b, e, a)
+            if where == block:
+                two[tap] = flat[slot * 16 : slot * 16 + 16, :32]
     for part in range(7):
-        at = 64 + (part % 4) * 8
-        block = (lower, upper)[part // 4][at : at + 8] * scale_three
+        at = (part // 2) * 8 + group_index()
+        block = lines[at, (part % 2) * 8 : (part % 2) * 8 + 8, :].astype(F32) * scale_three
         for at in range(4):
             tap = part * 4 + at
             if tap < 27:
@@ -349,7 +348,7 @@
 
 
 def shifted(axis, step):
-    count = lax.axis_size(axis)
+    count = axis_count(axis)
     return [(i, i + step) for i in range(count) if 0 <= i + step < count]
 
 
@@ -364,13 +363,17 @@
     return lax.all_to_all(blocks, axis, 0, 0, tiled=True)
 
 
-def traded(block, axis, reach):
-    return lax.ppermute(block, axis, [(i, i ^ reach) for i in range(lax.axis_size(axis))])
+def total_of(blocks):
+    return jnp.sum(blocks.astype(F32), axis=0).astype(BF16)
+
+
+def copied(block, names):
+    return jnp.broadcast_to(block[None], (axis_count(names),) + block.shape)
 
 
 def on_device(inputs, weight_two, weight_three, cotangent):
-    groups = lax.axis_size("grp")
-    slabs = lax.axis_size("depth")
+    groups = axis_count(GROUP)
+    slabs = axis_count(DEPTH)
     chans, planes, height, breadth = inputs.shape
     cells = planes * slabs * height * groups * breadth
     pool_rows = height // 2
@@ -379,7 +382,7 @@
 
     own = jnp.transpose(inputs, (2, 1, 0, 3))
     own, cotangent = lax.optimization_barrier((own, cotangent))
-    top, bottom = neighbours(own[:7], own[height - 7 :], "grp")
+    top, bottom = neighbours(own[:7], own[height - 7 :], GROUP)
 
     (packed,) = call(
         pack,
@@ -388,21 +391,22 @@
         (jnp.transpose(cotangent[:, 0], (1, 0, 2)), weight_three.reshape(27, share, 32)),
         2 * 64 * 1024,
     )
-    arrived = exchange(packed, "grp").reshape(filters, -1)
+    arrived = exchange(packed, GROUP).reshape(filters, -1)
 
     def whole(plane):
         return jnp.concatenate([top[:, plane], own[:, plane], bottom[:, plane]], axis=0)
 
-    below, above = neighbours(whole(0), whole(1), "depth")
-
-    plain = weight_two.reshape(27, 32, 16)
-    ahead, back = call(
-        weights_two,
-        [jax.ShapeDtypeStruct((256, 1024), BF16), jax.ShapeDtypeStruct((128, 2048), BF16)],
+    below, above = neighbours(whole(0), whole(1), DEPTH)
+
+    turned = jnp.transpose(weight_two.reshape(27, 32, 16), (0, 2, 1))
+    (ahead,) = call(
+        weights_ahead,
+        [jax.ShapeDtypeStruct((256, 1024), BF16)],
         [],
-        (plain, jnp.transpose(plain, (0, 2, 1))),
+        (turned,),
         2 * 256 * 1024 * 128,
     )
+    ahead, arrived = lax.optimization_barrier((ahead, arrived))
 
     pooled, slope, parts_two = call(
         forward_two,
@@ -416,7 +420,7 @@
         2 * 14 * 256 * 1024 * 128,
     )
 
-    pool_below, pool_above = neighbours(pooled, pooled, "depth")
+    pool_below, pool_above = neighbours(pooled, pooled, DEPTH)
     shift = pltpu.VMEM((BREADTH, 2 * BREADTH), BF16)
     terms = jax.ShapeDtypeStruct((pool_rows + 2, 32, BREADTH), BF16)
     grads, parts_three, down, same, up = call(
@@ -437,41 +441,28 @@
         2 * 12 * 64 * 864 * 128 * 2,
     )
 
-    terms_below, terms_above = neighbours(down, up, "depth")
+    terms_below, terms_above = neighbours(down, up, DEPTH)
     (local_three,) = call(
         filters_three,
-        [jax.ShapeDtypeStruct((2, groups * 32, BREADTH), F32)],
+        [jax.ShapeDtypeStruct((filters, 1024), F32)],
         [],
         (grads, parts_three),
         2 * 8 * 64 * 864 * 128,
     )
-    halves = jax.ShapeDtypeStruct((64 + groups * 32, BREADTH), F32)
     plane = jax.ShapeDtypeStruct((pool_rows + 2, 128, BREADTH), BF16)
-    low, high, keep, send = call(
+    low, high, lines = call(
         middle_two,
-        [plane, plane, halves, halves],
+        [plane, plane, jax.ShapeDtypeStruct((32, 20, BREADTH), F32)],
         [],
         (terms_below, same, terms_above, slope, parts_two, local_three),
         2 * 8 * 256 * 1024 * 128,
     )
 
-    came = traded(send, "depth", 1)
-    two_below, two_above = neighbours(low, high, "depth")
-    reach = 1
-    while reach < groups:
-        half = jax.ShapeDtypeStruct(((keep.shape[0] - 64) // 2 + 64, BREADTH), BF16)
-        keep, send = call(
-            functools.partial(halved, reach), [half, half], [], (keep, came), 1024 * 1024
-        )
-        if reach == 2:
-            send, two_below, two_above = lax.optimization_barrier((send, two_below, two_above))
-        came = traded(send, "grp", reach)
-        reach *= 2
-    mine = keep.astype(F32) + came.astype(F32)
-    for reach in [slabs // 2] + [2**at for at in range(1, slabs.bit_length() - 2)]:
-        mine = mine.astype(BF16)
-        mine = mine.astype(F32) + traded(mine, "depth", reach).astype(F32)
-    other = traded(mine, "depth", 1)
+    two_below, two_above = neighbours(low, high, DEPTH)
+    lines = lines.astype(BF16).reshape(32, 5, 4, BREADTH)
+    lines = total_of(exchange(lines, NEAR))
+    lines = total_of(exchange(copied(lines, ("z",)), "z"))
+    lines = exchange(copied(lines, NEAR), NEAR).reshape(32, 20, BREADTH)
     two, three = call(
         functools.partial(spread_out, 1.0 / math.sqrt(cells), 1.0 / math.sqrt(cells / 8)),
         [
@@ -479,7 +470,7 @@
             jax.ShapeDtypeStruct((27, share, 32), F32),
         ],
         [],
-        (mine, other),
+        (lines.astype(F32),),
         2 * 64 * 1024,
     )
 
@@ -490,8 +481,9 @@
             pltpu.VMEM((height + 4, 512, BREADTH), BF16),
             shift,
             pltpu.VMEM((2 * BREADTH, 2 * BREADTH), BF16),
+            pltpu.VMEM((128, 2048), BF16),
         ],
-        (two_below, low, high, two_above, back),
+        (two_below, low, high, two_above, turned),
         2 * 8 * 128 * 2048 * 128,
     )
     input_grad = jnp.transpose(
@@ -502,16 +494,17 @@
 
 
 def solution(mesh):
+    parts = jax.sharding.Mesh(mesh.devices.reshape(2, 16, 2, 2, 4), DEPTH + GROUP)
     placed = (
-        P(None, "depth", "grp", None),
+        P(None, DEPTH, GROUP, None),
         P(),
-        P(None, None, None, "grp", None),
-        P("grp", "depth", None, None),
+        P(None, None, None, GROUP, None),
+        P(GROUP, DEPTH, None, None),
     )
     return jax.shard_map(
         on_device,
-        mesh=mesh,
+        mesh=parts,
         in_specs=placed,
-        out_specs=(P(None, "depth", "grp", None), P(), P(None, None, None, "grp", None)),
+        out_specs=(P(None, DEPTH, GROUP, None), P(), P(None, None, None, GROUP, None)),
         check_vma=False,
     )

time: 150 us -> 121 us (0.81)
  starting transfers between devices: 94.8 us -> 52.5 us
  blocking collectives: 0 us -> 26.7 us
  waiting for transfers between devices: 33.8 us -> 23.6 us
  Pallas kernels: 11.8 us -> 10 us
  local copies, waits for them, and re-layouts: 7.5 us -> 5.79 us
    ppermute x10 -> x0, starting transfers between devices: 54.3 us -> none  [traded(): lax.ppermute(block, axis, [(i, i ^ reach) for i in range(lax.axis_size(ax...]
    ppermute x10 -> x0, waiting for transfers between devices: 26.8 us -> none  [traded(): lax.ppermute(block, axis, [(i, i ^ reach) for i in range(lax.axis_size(ax...]
    all_to_all x0 -> x1, blocking collectives: none -> 26.7 us  [exchange(): return lax.all_to_all(blocks, axis, 0, 0, tiled=True)]
    all_to_all x1 -> x3, starting transfers between devices: 7.5 us -> 23 us  [exchange(): return lax.all_to_all(blocks, axis, 0, 0, tiled=True)]
    all_to_all x1 -> x3, waiting for transfers between devices: 0.01 us -> 10.6 us  [exchange(): return lax.all_to_all(blocks, axis, 0, 0, tiled=True)]
    unnamed x23 -> x5, local copies, waits for them, and re-layouts: 6.11 us -> 1.95 us
    ppermute x5, waiting for transfers between devices: 4.07 us -> 8.14 us  [neighbours(): lax.ppermute(first, axis, shifted(axis, -1))]
    ppermute x5, starting transfers between devices: 12.8 us -> 8.97 us  [neighbours(): lax.ppermute(first, axis, shifted(axis, -1))]
  transfers between devices with their start and end apart: 21 -> 13, of which waited for: 14 -> 8; matrix products, arithmetic and copies ran while one was open for 1% -> 2% of each run, Pallas kernels for 5% -> 4%
where the time goes in v4:
time: 121 us; the launch traced here: 120 us
  starting transfers between devices  52.5 us (43%)
  blocking collectives  26.7 us (22%)
  waiting for transfers between devices  23.6 us (20%)
  Pallas kernels  10 us (8%)
  local copies, waits for them, and re-layouts  5.79 us (5%)
    all_to_all x1, blocking collectives, exchange(): return lax.all_to_all(blocks, axis, 0, 0, tiled=True)  26.7 us
    all_to_all x3, starting transfers between devices, exchange(): return lax.all_to_all(blocks, axis, 0, 0, tiled=True)  23 us
    ppermute x5, starting transfers between devices, neighbours(): lax.ppermute(last, axis, shifted(axis, 1))  20.5 us
    all_to_all x3, waiting for transfers between devices, exchange(): return lax.all_to_all(blocks, axis, 0, 0, tiled=True)  10.6 us
    pallas_call x8, Pallas kernels, call(): pl.pallas_call(kernel, out_shape=outs, in_specs=specs, out_specs=[pl.Bloc...  10 us
    ppermute x5, starting transfers between devices, neighbours(): lax.ppermute(first, axis, shifted(axis, -1))  8.97 us
    ppermute x5, waiting for transfers between devices, neighbours(): lax.ppermute(first, axis, shifted(axis, -1))  8.14 us
    ppermute x5, waiting for transfers between devices, neighbours(): lax.ppermute(last, axis, shifted(axis, 1))  4.82 us
  transfers between devices with their start and end apart: 13, of which 8 were waited for; matrix products, arithmetic and copies ran while one was open for 2% of the time, Pallas kernels for 4%

profile of v4, /device:TPU:1, one launch (start us, length us, event | category | flops | bytes accessed | tf_op | source)
XLA Modules:
  0.0 119.8 jit_solution(14197427791730334257)
XLA Ops:
  0.6 1.1 copy.50
  1.7 1.3 %collective-permute-start.1 = (bf16[7,2,16,256]{3,2,1,0:T(8,128)(2,1)S(1)}, bf16[7,2,16,256]{3,2,1,0:T(8,128)(2,1)S(1)}, u32[]{:S(2)}, u32[]{:S(2)}) collective-permute-start(bf16[7,2,16,256]{3,2,1,0:T(8,128)(2,1)S(1)} %slice.27), channel_id=1, source_target_pairs={{1,0},{2,1},{3,2},{4,3},{5,4},{6,5},{7,6},{9,8},{10,9},{11,10},{12... | collective-permute-start | bytes 344072 | tf_op jit(solution)/shard_map/ppermute | solution.py:358
  3.0 1.0 copy.51
  4.0 0.0 copy-start
  4.1 0.0 copy-start.1
  4.1 0.8 copy-done.1
  4.9 0.8 shard_map.68
  5.7 8.4 %all-to-all-start = ((bf16[8,8,2432]{2,1,0:T(8,128)(2,1)}), bf16[8,8,2432]{2,1,0:T(8,128)(2,1)S(1)}, u32[]{:S(2)}, u32[]{:S(2)}) async-start(bf16[8,8,2432]{2,1,0:T(8,128)(2,1)} %shard_map.68), calls=%async_computation | async-start | bytes 622592 | tf_op jit(solution)/shard_map/all_to_all | solution.py:363
  14.1 3.4 %collective-permute-start = (bf16[7,2,16,256]{3,2,0,1:T(8,128)(2,1)S(1)}, bf16[7,2,16,256]{3,2,0,1:T(8,128)(2,1)S(1)}, u32[]{:S(2)}, u32[]{:S(2)}) collective-permute-start(bf16[7,2,16,256]{3,2,0,1:T(8,128)(2,1)S(1)} %slice.32), channel_id=1, source_target_pairs={{0,1},{1,2},{2,3},{3,4},{4,5},{5,6},{6,7},{8,9},{9,10},{10,11},{11... | collective-permute-start | bytes 344072 | tf_op jit(solution)/shard_map/ppermute | solution.py:357
  17.5 0.0 collective-permute-done.1.bottom
  17.6 2.8 %collective-permute-done = bf16[7,2,16,256]{3,2,0,1:T(8,128)(2,1)S(1)} collective-permute-done((bf16[7,2,16,256]{3,2,0,1:T(8,128)(2,1)S(1)}, bf16[7,2,16,256]{3,2,0,1:T(8,128)(2,1)S(1)}, u32[]{:S(2)}, u32[]{:S(2)}) %collective-permute-start) | collective-permute-done | bytes 114720 | tf_op jit(solution)/shard_map/ppermute | solution.py:357
  20.4 4.7 %collective-permute-start.2 = (bf16[30,16,256]{2,1,0:T(8,128)(2,1)S(1)}, bf16[30,16,256]{2,1,0:T(8,128)(2,1)S(1)}, u32[]{:S(2)}, u32[]{:S(2)}) collective-permute-start(bf16[30,16,256]{2,1,0:T(8,128)(2,1)S(1)} %pad_maximum_fusion), channel_id=1, source_target_pairs={{0,8},{8,16},{16,24},{24,32},{32,40},{40,48},{48,56},{56,64},{64,7... | collective-permute-start | bytes 737288 | tf_op jit(solution)/shard_map/ppermute | solution.py:357
  25.2 1.9 %collective-permute-start.3 = (bf16[30,16,256]{2,1,0:T(8,128)(2,1)S(1)}, bf16[30,16,256]{2,1,0:T(8,128)(2,1)S(1)}, u32[]{:S(2)}, u32[]{:S(2)}) collective-permute-start(bf16[30,16,256]{2,1,0:T(8,128)(2,1)S(1)} %pad_maximum_fusion.1), channel_id=1, source_target_pairs={{8,0},{16,8},{24,16},{32,24},{40,32},{48,40},{56,48},{64,56},{72,6... | collective-permute-start | bytes 737288 | tf_op jit(solution)/shard_map/ppermute | solution.py:358
  27.1 0.4 shard_map.67.weight
  27.5 0.0 all-to-all-done
  27.5 0.8 collective-permute-done.2.below
  28.3 4.4 %collective-permute-done.3.above = bf16[30,16,256]{2,1,0:T(8,128)(2,1)S(1)} collective-permute-done((bf16[30,16,256]{2,1,0:T(8,128)(2,1)S(1)}, bf16[30,16,256]{2,1,0:T(8,128)(2,1)S(1)}, u32[]{:S(2)}, u32[]{:S(2)}) %collective-permute-start.3) | collective-permute-done | bytes 245792 | tf_op jit(solution)/shard_map/ppermute | solution.py:358
  32.7 2.5 %shard_map.69 = (bf16[14,32,128]{2,1,0:T(8,128)(2,1)S(1)}, f32[10,256,128]{2,1,0:T(8,128)S(1)}, bf16[30,256,128]{2,1,0:T(8,128)(2,1)S(1)}) custom-call(bf16[16,2,16,256]{3,2,1,0:T(8,128)(2,1)S(1)} %bitcast.39, bf16[30,16,256]{2,1,0:T(8,128)(2,1)S(1)} %collective-permute-done.2.below, bf16[30,16,256]{2,1,0:T(8,128)(2,1)S(1)} %collective-permute-done.3.above, ...), custom_call_target="tpu_custom_call" | custom-call | flops 939524096 | bytes 4898816 | tf_op jit(solution)/shard_map/pallas_call | solution.py:31
  35.2 1.9 %collective-permute-start.5 = (bf16[14,32,128]{2,1,0:T(8,128)(2,1)S(1)}, bf16[14,32,128]{2,1,0:T(8,128)(2,1)S(1)}, u32[]{:S(2)}, u32[]{:S(2)}) collective-permute-start(bf16[14,32,128]{2,1,0:T(8,128)(2,1)S(1)} %get-tuple-element.23.own), channel_id=1, source_target_pairs={{8,0},{16,8},{24,16},{32,24},{40,32},{48,40},{56,48},{64,56},{72,6... | collective-permute-start | bytes 344072 | tf_op jit(solution)/shard_map/ppermute | solution.py:358
  37.2 3.6 %collective-permute-start.4 = (bf16[14,32,128]{2,1,0:T(8,128)(2,1)S(1)}, bf16[14,32,128]{2,1,0:T(8,128)(2,1)S(1)}, u32[]{:S(2)}, u32[]{:S(2)}) collective-permute-start(bf16[14,32,128]{2,1,0:T(8,128)(2,1)S(1)} %get-tuple-element.23.own), channel_id=1, source_target_pairs={{0,8},{8,16},{16,24},{24,32},{32,40},{40,48},{48,56},{56,64},{64,7... | collective-permute-start | bytes 344072 | tf_op jit(solution)/shard_map/ppermute | solution.py:357
  40.8 0.5 collective-permute-done.5.above
  41.3 1.2 %collective-permute-done.4.below = bf16[14,32,128]{2,1,0:T(8,128)(2,1)S(1)} collective-permute-done((bf16[14,32,128]{2,1,0:T(8,128)(2,1)S(1)}, bf16[14,32,128]{2,1,0:T(8,128)(2,1)S(1)}, u32[]{:S(2)}, u32[]{:S(2)}) %collective-permute-start.4) | collective-permute-done | bytes 114720 | tf_op jit(solution)/shard_map/ppermute | solution.py:357
  42.6 1.4 %shard_map.70 = (bf16[12,64,128]{2,1,0:T(8,128)(2,1)S(1)}, bf16[14,288,128]{2,1,0:T(8,128)(2,1)S(1)}, bf16[10,32,128]{2,1,0:T(8,128)(2,1)S(1)}, f32[10,32,128]{2,1,0:T(8,128)S(1)}, bf16[10,32,128]{2,1,0:T(8,128)(2,1)S(1)}) custom-call(bf16[14,32,128]{2,1,0:T(8,128)(2,1)S(1)} %collective-permute-done.4.below, bf16[14,32,128]{2,1,0:T(8,128)(2,1)S(1)} %get-tuple-element.23.own, ...), custom_call_target="tpu_custom_call" | custom-call | flops 339738624 | bytes 2211840 | tf_op jit(solution)/shard_map/pallas_call | solution.py:31
  43.9 4.3 %collective-permute-start.6 = (bf16[10,32,128]{2,1,0:T(8,128)(2,1)S(1)}, bf16[10,32,128]{2,1,0:T(8,128)(2,1)S(1)}, u32[]{:S(2)}, u32[]{:S(2)}) collective-permute-start(bf16[10,32,128]{2,1,0:T(8,128)(2,1)S(1)} %get-tuple-element.25), channel_id=1, source_target_pairs={{0,8},{8,16},{16,24},{24,32},{32,40},{40,48},{48,56},{56,64},{64,7... | collective-permute-start | bytes 245768 | tf_op jit(solution)/shard_map/ppermute | solution.py:357
  48.3 1.9 %collective-permute-start.7 = (bf16[10,32,128]{2,1,0:T(8,128)(2,1)S(1)}, bf16[10,32,128]{2,1,0:T(8,128)(2,1)S(1)}, u32[]{:S(2)}, u32[]{:S(2)}) collective-permute-start(bf16[10,32,128]{2,1,0:T(8,128)(2,1)S(1)} %get-tuple-element.27), channel_id=1, source_target_pairs={{8,0},{16,8},{24,16},{32,24},{40,32},{48,40},{56,48},{64,56},{72,6... | collective-permute-start | bytes 245768 | tf_op jit(solution)/shard_map/ppermute | solution.py:358
  50.2 0.6 shard_map.71.three
  50.9 0.0 collective-permute-done.6.below
  50.9 3.2 %collective-permute-done.7.above = bf16[10,32,128]{2,1,0:T(8,128)(2,1)S(1)} collective-permute-done((bf16[10,32,128]{2,1,0:T(8,128)(2,1)S(1)}, bf16[10,32,128]{2,1,0:T(8,128)(2,1)S(1)}, u32[]{:S(2)}, u32[]{:S(2)}) %collective-permute-start.7) | collective-permute-done | bytes 81952 | tf_op jit(solution)/shard_map/ppermute | solution.py:358
  54.0 0.9 shard_map.72
  55.0 0.1 copy.43
  55.1 26.7 %all_to_all.20 = bf16[32,5,4,128]{3,2,1,0:T(4,128)(2,1)S(1)} all-to-all(bf16[32,5,4,128]{3,2,1,0:T(4,128)(2,1)S(1)} %copy.43), channel_id=1, replica_groups=mesh['yl'=2,'z'=16,'core'=2,'yh'=2,'x'=4] {'yl','core','yh','x'}, dimensions={0} | all-to-all | bytes 327680 | tf_op jit(solution)/shard_map/all_to_all | solution.py:363
  81.8 0.1 reduce_sum.24
  81.9 0.7 broadcast_in_dim.4
  82.6 8.8 %all-to-all-start.2 = ((bf16[16,5,4,128]{3,2,1,0:T(4,128)(2,1)}), bf16[16,5,4,128]{3,2,1,0:T(4,128)(2,1)S(1)}, u32[]{:S(2)}, u32[]{:S(2)}) async-start(bf16[16,5,4,128]{3,2,1,0:T(4,128)(2,1)} %broadcast_in_dim.4), calls=%async_computation.2 | async-start | bytes 163840 | tf_op jit(solution)/shard_map/all_to_all | solution.py:363
  91.4 4.5 %collective-permute-start.8 = (bf16[10,128,128]{2,1,0:T(8,128)(2,1)S(1)}, bf16[10,128,128]{2,1,0:T(8,128)(2,1)S(1)}, u32[]{:S(2)}, u32[]{:S(2)}) collective-permute-start(bf16[10,128,128]{2,1,0:T(8,128)(2,1)S(1)} %get-tuple-element.32.high), channel_id=1, source_target_pairs={{0,8},{8,16},{16,24},{24,32},{32,40},{40,48},{48,56},{56,64},{64,7... | collective-permute-start | bytes 983048 | tf_op jit(solution)/shard_map/ppermute | solution.py:357
  95.9 1.9 %collective-permute-start.9 = (bf16[10,128,128]{2,1,0:T(8,128)(2,1)S(1)}, bf16[10,128,128]{2,1,0:T(8,128)(2,1)S(1)}, u32[]{:S(2)}, u32[]{:S(2)}) collective-permute-start(bf16[10,128,128]{2,1,0:T(8,128)(2,1)S(1)} %get-tuple-element.33.low), channel_id=1, source_target_pairs={{8,0},{16,8},{24,16},{32,24},{40,32},{48,40},{56,48},{64,56},{72,6... | collective-permute-start | bytes 983048 | tf_op jit(solution)/shard_map/ppermute | solution.py:358
  97.8 5.4 %all-to-all-done.2 = bf16[16,5,4,128]{3,2,1,0:T(4,128)(2,1)S(1)} async-done(((bf16[16,5,4,128]{3,2,1,0:T(4,128)(2,1)}), bf16[16,5,4,128]{3,2,1,0:T(4,128)(2,1)S(1)}, u32[]{:S(2)}, u32[]{:S(2)}) %all-to-all-start.2) | async-done | bytes 81952 | tf_op jit(solution)/shard_map/all_to_all | solution.py:363
  103.2 0.1 reduce_sum.25
  103.3 0.7 broadcast_in_dim.5
  104.0 5.9 %all-to-all-start.3 = ((bf16[32,5,4,128]{3,2,1,0:T(4,128)(2,1)}), bf16[32,5,4,128]{3,2,1,0:T(4,128)(2,1)S(1)}, u32[]{:S(2)}, u32[]{:S(2)}) async-start(bf16[32,5,4,128]{3,2,1,0:T(4,128)(2,1)} %broadcast_in_dim.5), calls=%async_computation.3 | async-start | bytes 327680 | tf_op jit(solution)/shard_map/all_to_all | solution.py:363
  109.9 0.0 collective-permute-done.8.below
  109.9 0.0 collective-permute-done.9.above
  109.9 2.6 %shard_map.73 = bf16[8,64,256]{2,1,0:T(8,128)(2,1)S(1)} custom-call(bf16[10,128,128]{2,1,0:T(8,128)(2,1)S(1)} %collective-permute-done.8.below, bf16[10,128,128]{2,1,0:T(8,128)(2,1)S(1)} %get-tuple-element.33.low, bf16[10,128,128]{2,1,0:T(8,128)(2,1)S(1)} %get-tuple-element.32.high, bf16[10,128,128]{2,1,0:T(8,128)(2,1)S(1)} %collective-permute-done.9.above, ...), custom_call_target="tpu_custom_call" | custom-call | flops 536870912 | bytes 1600512 | tf_op jit(solution)/shard_map/pallas_call | solution.py:31
  112.4 0.2 copy.41
  112.7 5.2 %all-to-all-done.3 = bf16[32,5,4,128]{3,2,1,0:T(4,128)(2,1)S(1)} async-done(((bf16[32,5,4,128]{3,2,1,0:T(4,128)(2,1)}), bf16[32,5,4,128]{3,2,1,0:T(4,128)(2,1)S(1)}, u32[]{:S(2)}, u32[]{:S(2)}) %all-to-all-start.3) | async-done | bytes 163872 | tf_op jit(solution)/shard_map/all_to_all | solution.py:363
  118.0 0.2 copy.46.lines
  118.2 0.8 reshape.39
  119.0 0.9 shard_map.74
  (14 shorter events, 0.3 us)
Async XLA Ops:
  1.7 15.8 %collective-permute-start.1 = (bf16[7,2,16,256]{3,2,1,0:T(8,128)(2,1)S(1)}, bf16[7,2,16,256]{3,2,1,0:T(8,128)(2,1)S(1)}, u32[]{:S(2)}, u32[]{:S(2)}) collective-permute-start(bf16[7,2,16,256]{3,2,1,0:T(8,128)(2,1)S(1)} %slice.27), channel_id=1, source_target_pairs={{1,0},{2,1},{3,2},{4,3},{5,4},{6,5},{7,6},{9,8},{10,9},{11,10},{12... | collective-permute-start | bytes 344072 | tf_op jit(solution)/shard_map/ppermute | solution.py:358
  4.0 23.1 %copy-start = (bf16[3,3,3,32,16]{3,4,2,1,0:T(8,128)(2,1)S(1)}, bf16[3,3,3,32,16]{3,4,2,1,0:T(8,128)(2,1)}, u32[]{:S(2)}) copy-start(bf16[3,3,3,32,16]{3,4,2,1,0:T(8,128)(2,1)} %param.5) | copy-start | bytes 82948
  4.1 0.9 copy-start.1
  5.7 21.8 %all-to-all-start = ((bf16[8,8,2432]{2,1,0:T(8,128)(2,1)}), bf16[8,8,2432]{2,1,0:T(8,128)(2,1)S(1)}, u32[]{:S(2)}, u32[]{:S(2)}) async-start(bf16[8,8,2432]{2,1,0:T(8,128)(2,1)} %shard_map.68), calls=%async_computation | async-start | bytes 622592 | tf_op jit(solution)/shard_map/all_to_all | solution.py:363
  14.1 6.3 %collective-permute-start = (bf16[7,2,16,256]{3,2,0,1:T(8,128)(2,1)S(1)}, bf16[7,2,16,256]{3,2,0,1:T(8,128)(2,1)S(1)}, u32[]{:S(2)}, u32[]{:S(2)}) collective-permute-start(bf16[7,2,16,256]{3,2,0,1:T(8,128)(2,1)S(1)} %slice.32), channel_id=1, source_target_pairs={{0,1},{1,2},{2,3},{3,4},{4,5},{5,6},{6,7},{8,9},{9,10},{10,11},{11... | collective-permute-start | bytes 344072 | tf_op jit(solution)/shard_map/ppermute | solution.py:357
  20.4 7.8 %collective-permute-start.2 = (bf16[30,16,256]{2,1,0:T(8,128)(2,1)S(1)}, bf16[30,16,256]{2,1,0:T(8,128)(2,1)S(1)}, u32[]{:S(2)}, u32[]{:S(2)}) collective-permute-start(bf16[30,16,256]{2,1,0:T(8,128)(2,1)S(1)} %pad_maximum_fusion), channel_id=1, source_target_pairs={{0,8},{8,16},{16,24},{24,32},{32,40},{40,48},{48,56},{56,64},{64,7... | collective-permute-start | bytes 737288 | tf_op jit(solution)/shard_map/ppermute | solution.py:357
  25.2 7.5 %collective-permute-start.3 = (bf16[30,16,256]{2,1,0:T(8,128)(2,1)S(1)}, bf16[30,16,256]{2,1,0:T(8,128)(2,1)S(1)}, u32[]{:S(2)}, u32[]{:S(2)}) collective-permute-start(bf16[30,16,256]{2,1,0:T(8,128)(2,1)S(1)} %pad_maximum_fusion.1), channel_id=1, source_target_pairs={{8,0},{16,8},{24,16},{32,24},{40,32},{48,40},{56,48},{64,56},{72,6... | collective-permute-start | bytes 737288 | tf_op jit(solution)/shard_map/ppermute | solution.py:358
  35.2 6.1 %collective-permute-start.5 = (bf16[14,32,128]{2,1,0:T(8,128)(2,1)S(1)}, bf16[14,32,128]{2,1,0:T(8,128)(2,1)S(1)}, u32[]{:S(2)}, u32[]{:S(2)}) collective-permute-start(bf16[14,32,128]{2,1,0:T(8,128)(2,1)S(1)} %get-tuple-element.23.own), channel_id=1, source_target_pairs={{8,0},{16,8},{24,16},{32,24},{40,32},{48,40},{56,48},{64,56},{72,6... | collective-permute-start | bytes 344072 | tf_op jit(solution)/shard_map/ppermute | solution.py:358
  37.2 5.4 %collective-permute-start.4 = (bf16[14,32,128]{2,1,0:T(8,128)(2,1)S(1)}, bf16[14,32,128]{2,1,0:T(8,128)(2,1)S(1)}, u32[]{:S(2)}, u32[]{:S(2)}) collective-permute-start(bf16[14,32,128]{2,1,0:T(8,128)(2,1)S(1)} %get-tuple-element.23.own), channel_id=1, source_target_pairs={{0,8},{8,16},{16,24},{24,32},{32,40},{40,48},{48,56},{56,64},{64,7... | collective-permute-start | bytes 344072 | tf_op jit(solution)/shard_map/ppermute | solution.py:357
  43.9 6.9 %collective-permute-start.6 = (bf16[10,32,128]{2,1,0:T(8,128)(2,1)S(1)}, bf16[10,32,128]{2,1,0:T(8,128)(2,1)S(1)}, u32[]{:S(2)}, u32[]{:S(2)}) collective-permute-start(bf16[10,32,128]{2,1,0:T(8,128)(2,1)S(1)} %get-tuple-element.25), channel_id=1, source_target_pairs={{0,8},{8,16},{16,24},{24,32},{32,40},{40,48},{48,56},{56,64},{64,7... | collective-permute-start | bytes 245768 | tf_op jit(solution)/shard_map/ppermute | solution.py:357
  48.3 5.8 %collective-permute-start.7 = (bf16[10,32,128]{2,1,0:T(8,128)(2,1)S(1)}, bf16[10,32,128]{2,1,0:T(8,128)(2,1)S(1)}, u32[]{:S(2)}, u32[]{:S(2)}) collective-permute-start(bf16[10,32,128]{2,1,0:T(8,128)(2,1)S(1)} %get-tuple-element.27), channel_id=1, source_target_pairs={{8,0},{16,8},{24,16},{32,24},{40,32},{48,40},{56,48},{64,56},{72,6... | collective-permute-start | bytes 245768 | tf_op jit(solution)/shard_map/ppermute | solution.py:358
  82.6 20.6 %all-to-all-start.2 = ((bf16[16,5,4,128]{3,2,1,0:T(4,128)(2,1)}), bf16[16,5,4,128]{3,2,1,0:T(4,128)(2,1)S(1)}, u32[]{:S(2)}, u32[]{:S(2)}) async-start(bf16[16,5,4,128]{3,2,1,0:T(4,128)(2,1)} %broadcast_in_dim.4), calls=%async_computation.2 | async-start | bytes 163840 | tf_op jit(solution)/shard_map/all_to_all | solution.py:363
  91.4 18.4 %collective-permute-start.8 = (bf16[10,128,128]{2,1,0:T(8,128)(2,1)S(1)}, bf16[10,128,128]{2,1,0:T(8,128)(2,1)S(1)}, u32[]{:S(2)}, u32[]{:S(2)}) collective-permute-start(bf16[10,128,128]{2,1,0:T(8,128)(2,1)S(1)} %get-tuple-element.32.high), channel_id=1, source_target_pairs={{0,8},{8,16},{16,24},{24,32},{32,40},{40,48},{48,56},{56,64},{64,7... | collective-permute-start | bytes 983048 | tf_op jit(solution)/shard_map/ppermute | solution.py:357
  95.9 14.0 %collective-permute-start.9 = (bf16[10,128,128]{2,1,0:T(8,128)(2,1)S(1)}, bf16[10,128,128]{2,1,0:T(8,128)(2,1)S(1)}, u32[]{:S(2)}, u32[]{:S(2)}) collective-permute-start(bf16[10,128,128]{2,1,0:T(8,128)(2,1)S(1)} %get-tuple-element.33.low), channel_id=1, source_target_pairs={{8,0},{16,8},{24,16},{32,24},{40,32},{48,40},{56,48},{64,56},{72,6... | collective-permute-start | bytes 983048 | tf_op jit(solution)/shard_map/ppermute | solution.py:358
  104.0 13.9 %all-to-all-start.3 = ((bf16[32,5,4,128]{3,2,1,0:T(4,128)(2,1)}), bf16[32,5,4,128]{3,2,1,0:T(4,128)(2,1)S(1)}, u32[]{:S(2)}, u32[]{:S(2)}) async-start(bf16[32,5,4,128]{3,2,1,0:T(4,128)(2,1)} %broadcast_in_dim.5), calls=%async_computation.3 | async-start | bytes 327680 | tf_op jit(solution)/shard_map/all_to_all | solution.py:363

commit v5 on v4

--- a/solution.py
+++ b/solution.py
@@ -114,12 +114,35 @@
     return jnp.logical_and(at >= 0, at < rows * axis_count(GROUP))
 
 
-def forward_two(own, below, above, top, bottom, weight, pooled, slope, parts, split):
+def edges(own, top, bottom, near, far):
+    core = lax.axis_index("core")
+    at = 0
+    for ref in (top, own, bottom):
+        for row in range(ref.shape[0]):
+            near[at] = ref[row, 1 - core]
+            far[at] = ref[row, core]
+            at += 1
+
+
+def in_order(near, far):
+    lower = lax.axis_index("core") == 0
+
+    def below(*at):
+        return lax.select(lower, far[at], near[at])
+
+    def above(*at):
+        return lax.select(lower, near[at], far[at])
+
+    return below, above
+
+
+def forward_two(own, near, far, top, bottom, weight, pooled, slope, parts, split):
     split[...] = splitter()
     first = pooled.shape[0] - 6
     first = first * group_index() - 3
     edge = top.shape[0]
     height = own.shape[0]
+    below, above = in_order(near, far)
 
     def place(row, many, block):
         cells = dot(block, split[...]).astype(BF16).reshape(many, 64, 4 * BREADTH)
@@ -131,7 +154,7 @@
         for row in range(0, ref.shape[0], 4):
             block = []
             for at in range(row, min(row + 4, ref.shape[0])):
-                block += [below[to + at], ref[at, 0], ref[at, 1], above[to + at]]
+                block += [below(to + at), ref[at, 0], ref[at, 1], above(to + at)]
             place(to + row, len(block) // 4, jnp.concatenate(block, axis=0))
 
     rows = pooled.shape[0]
@@ -152,15 +175,14 @@
             slope[row - 1] = rate[:, BREADTH:]
 
 
-def place_shifted(refs, parts, shift, chans):
-    span = len(refs) * chans
-    rows = refs[0].shape[0]
+def place_shifted(planes, rows, parts, shift, chans):
+    span = len(planes) * chans
     step = 256 // chans
-    for plane, ref in enumerate(refs):
+    for plane, taken in enumerate(planes):
         at = plane * chans
         for row in range(0, rows, step):
             many = min(step, rows - row)
-            block = ref[row : row + many]
+            block = taken(slice(row, row + many))
             moved = dot(block.reshape(many * chans, BREADTH), shift[...]).astype(BF16)
             moved = moved.reshape(many, chans, 2 * BREADTH)
             parts[row : row + many, at : at + chans, :] = moved[:, :, :BREADTH]
@@ -200,10 +222,12 @@
             out[to, :, lane : lane + BREADTH] = blocks[part]
 
 
-def middle_three(below, own, above, arrived, grads, parts, down, same, up, shift, around, turned):
+def middle_three(near, own, far, arrived, grads, parts, to_near, same, to_far, shift, around, turned):
     shift[...] = shifter()
-    place_shifted((below, own, above), parts, shift, 32)
+    below, above = in_order(near, far)
+    place_shifted((below, own.__getitem__, above), own.shape[0], parts, shift, 32)
     rows = grads.shape[0]
+    lower = lax.axis_index("core") == 0
     span = rows * BREADTH
     weight = arrived[:, span:]
     for row in range(0, rows, 4):
@@ -227,14 +251,15 @@
             pair = jnp.where(lane < 64, tap(at), tap(at + 1))
             turned[to : to + 32, at * 64 : at * 64 + 128] = pair.astype(BF16)
         turned[to : to + 32, 512:576] = tap(8)[:, :64].astype(BF16)
-    place_shifted((grads,), around, shift, 64)
+    place_shifted((grads.__getitem__,), rows, around, shift, 64)
     for row in range(0, rows - 2, 2):
         pool = dot(turned[...], side_by_side(around, row, 2, 3))
         for off in range(2):
             half = pool[:, off * BREADTH : (off + 1) * BREADTH]
-            up[row + off] = half[:32].astype(BF16)
+            up, down = half[:32], half[64:]
             same[row + off] = half[32:64]
-            down[row + off] = half[64:].astype(BF16)
+            to_near[row + off] = lax.select(lower, up, down).astype(BF16)
+            to_far[row + off] = lax.select(lower, down, up).astype(BF16)
 
 
 def filters_three(grads, parts, out):
@@ -245,12 +270,12 @@
     out[:, 864:] = jnp.zeros((full.shape[0], 160), F32)
 
 
-def middle_two(below, own, above, slope, parts, three, low, high, lines):
+def middle_two(near, own, far, slope, parts, three, low, high, lines):
     rows = own.shape[0] - 2
     first = rows * group_index() - 1
     left = []
     for row in range(rows + 2):
-        pool = own[row] + below[row].astype(F32) + above[row].astype(F32)
+        pool = own[row] + near[row].astype(F32) + far[row].astype(F32)
         pool = jnp.where(inside(first + row, rows), pool, 0.0) * 0.125
         full = pool[None] * slope[row].reshape(8, 32, BREADTH)
         full = full.astype(BF16).reshape(256, BREADTH)
@@ -359,6 +384,16 @@
     )
 
 
+def paired(near, far):
+    count = axis_count(DEPTH)
+    across = [(i, i + 1) for i in range(1, count - 1, 2)]
+    across += [(i + 1, i) for i in range(1, count - 1, 2)]
+    return (
+        lax.ppermute(near, DEPTH, [(i, i ^ 1) for i in range(count)]),
+        lax.ppermute(far, DEPTH, across),
+    )
+
+
 def exchange(blocks, axis):
     return lax.all_to_all(blocks, axis, 0, 0, tiled=True)
 
@@ -391,12 +426,11 @@
         (jnp.transpose(cotangent[:, 0], (1, 0, 2)), weight_three.reshape(27, share, 32)),
         2 * 64 * 1024,
     )
+    packed, bottom = lax.optimization_barrier((packed, bottom))
     arrived = exchange(packed, GROUP).reshape(filters, -1)
 
-    def whole(plane):
-        return jnp.concatenate([top[:, plane], own[:, plane], bottom[:, plane]], axis=0)
-
-    below, above = neighbours(whole(0), whole(1), DEPTH)
+    plane = jax.ShapeDtypeStruct((height + 14, chans, breadth), BF16)
+    near, far = paired(*call(edges, [plane, plane], [], (own, top, bottom), 1024 * 1024))
 
     turned = jnp.transpose(weight_two.reshape(27, 32, 16), (0, 2, 1))
     (ahead,) = call(
@@ -416,14 +450,14 @@
             jax.ShapeDtypeStruct((height + 14, 256, BREADTH), BF16),
         ],
         [pltpu.VMEM((2 * BREADTH, 4 * BREADTH), BF16)],
-        (own, below, above, top, bottom, ahead),
+        (own, near, far, top, bottom, ahead),
         2 * 14 * 256 * 1024 * 128,
     )
 
-    pool_below, pool_above = neighbours(pooled, pooled, DEPTH)
+    pool_near, pool_far = paired(pooled, pooled)
     shift = pltpu.VMEM((BREADTH, 2 * BREADTH), BF16)
     terms = jax.ShapeDtypeStruct((pool_rows + 2, 32, BREADTH), BF16)
-    grads, parts_three, down, same, up = call(
+    grads, parts_three, to_near, same, to_far = call(
         middle_three,
         [
             jax.ShapeDtypeStruct((pool_rows + 4, filters, BREADTH), BF16),
@@ -437,11 +471,11 @@
             pltpu.VMEM((pool_rows + 4, 3 * filters, BREADTH), BF16),
             pltpu.VMEM((96, 9 * filters), BF16),
         ],
-        (pool_below, pooled, pool_above, arrived),
+        (pool_near, pooled, pool_far, arrived),
         2 * 12 * 64 * 864 * 128 * 2,
     )
 
-    terms_below, terms_above = neighbours(down, up, DEPTH)
+    terms_near, terms_far = paired(to_near, to_far)
     (local_three,) = call(
         filters_three,
         [jax.ShapeDtypeStruct((filters, 1024), F32)],
@@ -454,7 +488,7 @@
         middle_two,
         [plane, plane, jax.ShapeDtypeStruct((32, 20, BREADTH), F32)],
         [],
-        (terms_below, same, terms_above, slope, parts_two, local_three),
+        (terms_near, same, terms_far, slope, parts_two, local_three),
         2 * 8 * 256 * 1024 * 128,
     )
 

time: 121 us -> 112 us (0.926)
  waiting for transfers between devices: 23.6 us -> 19.1 us
  starting transfers between devices: 52.5 us -> 48.3 us
    ppermute x0 -> x6, starting transfers between devices: none -> 16.3 us  [the longest x3 8.43 us: paired(): lax.ppermute(near, DEPTH, [(i, i ^ 1) for i in range(count)])]
    ppermute x5 -> x2, starting transfers between devices: 20.5 us -> 9.04 us  [neighbours(): lax.ppermute(last, axis, shifted(axis, 1))]
    ppermute x5 -> x2, waiting for transfers between devices: 8.14 us -> 0.01 us  [neighbours(): lax.ppermute(first, axis, shifted(axis, -1))]
    ppermute x0 -> x6, waiting for transfers between devices: none -> 7.87 us  [the longest x3 7.86 us: paired(): lax.ppermute(far, DEPTH, across)]
    ppermute x5 -> x2, starting transfers between devices: 8.97 us -> 3.21 us  [neighbours(): lax.ppermute(first, axis, shifted(axis, -1))]
    ppermute x5 -> x2, waiting for transfers between devices: 4.82 us -> 0.01 us  [neighbours(): lax.ppermute(last, axis, shifted(axis, 1))]
    all_to_all x3, starting transfers between devices: 23 us -> 19.7 us  [exchange(): return lax.all_to_all(blocks, axis, 0, 0, tiled=True)]
    pallas_call x8 -> x9, Pallas kernels: 10 us -> 10.1 us  [call(): pl.pallas_call(kernel, out_shape=outs, in_specs=specs, out_specs=[pl.Bloc...]
  transfers between devices with their start and end apart: 13 -> 13, of which waited for: 8 -> 6; matrix products, arithmetic and copies ran while one was open for 2% -> 2% of each run, Pallas kernels for 4% -> 4%
where the time goes in v5:
time: 112 us; the launch traced here: 111 us
  starting transfers between devices  48.3 us (43%)
  blocking collectives  27 us (24%)
  waiting for transfers between devices  19.1 us (17%)
  Pallas kernels  10.1 us (9%)
  local copies, waits for them, and re-layouts  5.72 us (5%)
    all_to_all x1, blocking collectives, exchange(): return lax.all_to_all(blocks, axis, 0, 0, tiled=True)  27 us
    all_to_all x3, starting transfers between devices, exchange(): return lax.all_to_all(blocks, axis, 0, 0, tiled=True)  19.7 us
    all_to_all x3, waiting for transfers between devices, exchange(): return lax.all_to_all(blocks, axis, 0, 0, tiled=True)  11.3 us
    pallas_call x9, Pallas kernels, call(): pl.pallas_call(kernel, out_shape=outs, in_specs=specs, out_specs=[pl.Bloc...  10.1 us
    ppermute x2, starting transfers between devices, neighbours(): lax.ppermute(last, axis, shifted(axis, 1))  9.04 us
    ppermute x3, starting transfers between devices, paired(): lax.ppermute(near, DEPTH, [(i, i ^ 1) for i in range(count)])  8.43 us
    ppermute x3, starting transfers between devices, paired(): lax.ppermute(far, DEPTH, across)  7.9 us
    ppermute x3, waiting for transfers between devices, paired(): lax.ppermute(far, DEPTH, across)  7.86 us
  transfers between devices with their start and end apart: 13, of which 6 were waited for; matrix products, arithmetic and copies ran while one was open for 2% of the time, Pallas kernels for 4%

profile of v5, /device:TPU:1, one launch (start us, length us, event | category | flops | bytes accessed | tf_op | source)
XLA Modules:
  0.0 111.3 jit_solution(11404624905971122114)
XLA Ops:
  0.6 0.0 copy-start
  0.6 1.1 %copy.40 = bf16[16,2,16,256]{3,0,1,2:T(8,128)(2,1)S(1)} copy(bf16[16,2,16,256]{3,2,1,0:T(8,128)(2,1)} %param.4) | data formatting | bytes 524288 | tf_op args[0]
  1.8 1.3 %collective-permute-start.1 = (bf16[7,2,16,256]{3,2,1,0:T(8,128)(2,1)S(1)}, bf16[7,2,16,256]{3,2,1,0:T(8,128)(2,1)S(1)}, u32[]{:S(2)}, u32[]{:S(2)}) collective-permute-start(bf16[7,2,16,256]{3,2,1,0:T(8,128)(2,1)S(1)} %get-tuple-element.45), channel_id=1, source_target_pairs={{1,0},{2,1},{3,2},{4,3},{5,4},{6,5},{7,6},{9,8},{10,9},{11,10},{12... | collective-permute-start | bytes 344072 | tf_op jit(solution)/shard_map/ppermute | solution.py:383
  3.1 4.6 %collective-permute-start = (bf16[7,2,16,256]{3,2,1,0:T(8,128)(2,1)S(1)}, bf16[7,2,16,256]{3,2,1,0:T(8,128)(2,1)S(1)}, u32[]{:S(2)}, u32[]{:S(2)}) collective-permute-start(bf16[7,2,16,256]{3,2,1,0:T(8,128)(2,1)S(1)} %get-tuple-element.46), channel_id=1, source_target_pairs={{0,1},{1,2},{2,3},{3,4},{4,5},{5,6},{6,7},{8,9},{9,10},{10,11},{11... | collective-permute-start | bytes 344072 | tf_op jit(solution)/shard_map/ppermute | solution.py:382
  7.7 1.0 copy.41
  8.7 0.0 copy-start.1
  8.7 0.8 copy-done.1
  9.5 0.8 shard_map.67
  10.3 0.0 collective-permute-done.1.bottom
  10.3 7.6 %all-to-all-start = ((bf16[8,8,2432]{2,1,0:T(8,128)(2,1)}), bf16[8,8,2432]{2,1,0:T(8,128)(2,1)S(1)}, u32[]{:S(2)}, u32[]{:S(2)}) async-start(bf16[8,8,2432]{2,1,0:T(8,128)(2,1)} %shard_map.67), calls=%async_computation | async-start | bytes 622592 | tf_op jit(solution)/shard_map/all_to_all | solution.py:398
  17.9 0.0 collective-permute-done.top
  18.0 4.6 %collective-permute-start.2 = (bf16[30,16,256]{2,1,0:T(8,128)(2,1)S(1)}, bf16[30,16,256]{2,1,0:T(8,128)(2,1)S(1)}, u32[]{:S(2)}, u32[]{:S(2)}) collective-permute-start(bf16[30,16,256]{2,1,0:T(8,128)(2,1)S(1)} %get-tuple-element.27), channel_id=1, source_target_pairs={{0,8},{8,0},{16,24},{24,16},{32,40},{40,32},{48,56},{56,48},{64,72... | collective-permute-start | bytes 737288 | tf_op jit(solution)/shard_map/ppermute | solution.py:392
  22.6 2.3 %collective-permute-start.3 = (bf16[30,16,256]{2,1,0:T(8,128)(2,1)S(1)}, bf16[30,16,256]{2,1,0:T(8,128)(2,1)S(1)}, u32[]{:S(2)}, u32[]{:S(2)}) collective-permute-start(bf16[30,16,256]{2,1,0:T(8,128)(2,1)S(1)} %get-tuple-element.28), channel_id=1, source_target_pairs={{8,16},{24,32},{40,48},{56,64},{72,80},{88,96},{104,112},{120,128}... | collective-permute-start | bytes 737288 | tf_op jit(solution)/shard_map/ppermute | solution.py:393
  24.9 0.4 shard_map.69.weight
  25.2 0.6 all-to-all-done
  25.9 0.0 collective-permute-done.2.near
  25.9 4.2 %collective-permute-done.3.far = bf16[30,16,256]{2,1,0:T(8,128)(2,1)S(1)} collective-permute-done((bf16[30,16,256]{2,1,0:T(8,128)(2,1)S(1)}, bf16[30,16,256]{2,1,0:T(8,128)(2,1)S(1)}, u32[]{:S(2)}, u32[]{:S(2)}) %collective-permute-start.3) | collective-permute-done | bytes 245792 | tf_op jit(solution)/shard_map/ppermute | solution.py:393
  30.1 2.5 %shard_map.70 = (bf16[14,32,128]{2,1,0:T(8,128)(2,1)S(1)}, f32[10,256,128]{2,1,0:T(8,128)S(1)}, bf16[30,256,128]{2,1,0:T(8,128)(2,1)S(1)}) custom-call(bf16[16,2,16,256]{3,2,1,0:T(8,128)(2,1)S(1)} %bitcast.26, bf16[30,16,256]{2,1,0:T(8,128)(2,1)S(1)} %collective-permute-done.2.near, bf16[30,16,256]{2,1,0:T(8,128)(2,1)S(1)} %collective-permute-done.3.far, ...), custom_call_target="tpu_custom_call" | custom-call | flops 939524096 | bytes 4898816 | tf_op jit(solution)/shard_map/pallas_call | solution.py:31
  32.6 2.3 %collective-permute-start.5 = (bf16[14,32,128]{2,1,0:T(8,128)(2,1)S(1)}, bf16[14,32,128]{2,1,0:T(8,128)(2,1)S(1)}, u32[]{:S(2)}, u32[]{:S(2)}) collective-permute-start(bf16[14,32,128]{2,1,0:T(8,128)(2,1)S(1)} %get-tuple-element.31.own), channel_id=1, source_target_pairs={{8,16},{24,32},{40,48},{56,64},{72,80},{88,96},{104,112},{120,128}... | collective-permute-start | bytes 344072 | tf_op jit(solution)/shard_map/ppermute | solution.py:393
  34.9 1.9 %collective-permute-start.4 = (bf16[14,32,128]{2,1,0:T(8,128)(2,1)S(1)}, bf16[14,32,128]{2,1,0:T(8,128)(2,1)S(1)}, u32[]{:S(2)}, u32[]{:S(2)}) collective-permute-start(bf16[14,32,128]{2,1,0:T(8,128)(2,1)S(1)} %get-tuple-element.31.own), channel_id=1, source_target_pairs={{0,8},{8,0},{16,24},{24,16},{32,40},{40,32},{48,56},{56,48},{64,72... | collective-permute-start | bytes 344072 | tf_op jit(solution)/shard_map/ppermute | solution.py:392
  36.9 1.9 %collective-permute-done.5.far = bf16[14,32,128]{2,1,0:T(8,128)(2,1)S(1)} collective-permute-done((bf16[14,32,128]{2,1,0:T(8,128)(2,1)S(1)}, bf16[14,32,128]{2,1,0:T(8,128)(2,1)S(1)}, u32[]{:S(2)}, u32[]{:S(2)}) %collective-permute-start.5) | collective-permute-done | bytes 114720 | tf_op jit(solution)/shard_map/ppermute | solution.py:393
  38.8 0.0 collective-permute-done.4.near
  38.8 1.3 %shard_map.71 = (bf16[12,64,128]{2,1,0:T(8,128)(2,1)S(1)}, bf16[14,288,128]{2,1,0:T(8,128)(2,1)S(1)}, bf16[10,32,128]{2,1,0:T(8,128)(2,1)S(1)}, f32[10,32,128]{2,1,0:T(8,128)S(1)}, bf16[10,32,128]{2,1,0:T(8,128)(2,1)S(1)}) custom-call(bf16[14,32,128]{2,1,0:T(8,128)(2,1)S(1)} %collective-permute-done.4.near, bf16[14,32,128]{2,1,0:T(8,128)(2,1)S(1)} %get-tuple-element.31.own, ...), custom_call_target="tpu_custom_call" | custom-call | flops 339738624 | bytes 2211840 | tf_op jit(solution)/shard_map/pallas_call | solution.py:31
  40.1 1.9 %collective-permute-start.6 = (bf16[10,32,128]{2,1,0:T(8,128)(2,1)S(1)}, bf16[10,32,128]{2,1,0:T(8,128)(2,1)S(1)}, u32[]{:S(2)}, u32[]{:S(2)}) collective-permute-start(bf16[10,32,128]{2,1,0:T(8,128)(2,1)S(1)} %get-tuple-element.33), channel_id=1, source_target_pairs={{0,8},{8,0},{16,24},{24,16},{32,40},{40,32},{48,56},{56,48},{64,72... | collective-permute-start | bytes 245768 | tf_op jit(solution)/shard_map/ppermute | solution.py:392
  42.0 3.3 %collective-permute-start.7 = (bf16[10,32,128]{2,1,0:T(8,128)(2,1)S(1)}, bf16[10,32,128]{2,1,0:T(8,128)(2,1)S(1)}, u32[]{:S(2)}, u32[]{:S(2)}) collective-permute-start(bf16[10,32,128]{2,1,0:T(8,128)(2,1)S(1)} %get-tuple-element.35), channel_id=1, source_target_pairs={{8,16},{24,32},{40,48},{56,64},{72,80},{88,96},{104,112},{120,128}... | collective-permute-start | bytes 245768 | tf_op jit(solution)/shard_map/ppermute | solution.py:393
  45.3 0.6 shard_map.72.three
  46.0 0.0 collective-permute-done.6.near
  46.0 1.8 %collective-permute-done.7.far = bf16[10,32,128]{2,1,0:T(8,128)(2,1)S(1)} collective-permute-done((bf16[10,32,128]{2,1,0:T(8,128)(2,1)S(1)}, bf16[10,32,128]{2,1,0:T(8,128)(2,1)S(1)}, u32[]{:S(2)}, u32[]{:S(2)}) %collective-permute-start.7) | collective-permute-done | bytes 81952 | tf_op jit(solution)/shard_map/ppermute | solution.py:393
  47.8 0.9 shard_map.73
  48.8 0.1 copy.33
  48.9 27.0 %all_to_all.20 = bf16[32,5,4,128]{3,2,1,0:T(4,128)(2,1)S(1)} all-to-all(bf16[32,5,4,128]{3,2,1,0:T(4,128)(2,1)S(1)} %copy.33), channel_id=1, replica_groups=mesh['yl'=2,'z'=16,'core'=2,'yh'=2,'x'=4] {'yl','core','yh','x'}, dimensions={0} | all-to-all | bytes 327680 | tf_op jit(solution)/shard_map/all_to_all | solution.py:398
  75.8 0.1 reduce_sum.24
  75.9 0.7 broadcast_in_dim.4
  76.6 6.3 %all-to-all-start.2 = ((bf16[16,5,4,128]{3,2,1,0:T(4,128)(2,1)}), bf16[16,5,4,128]{3,2,1,0:T(4,128)(2,1)S(1)}, u32[]{:S(2)}, u32[]{:S(2)}) async-start(bf16[16,5,4,128]{3,2,1,0:T(4,128)(2,1)} %broadcast_in_dim.4), calls=%async_computation.2 | async-start | bytes 163840 | tf_op jit(solution)/shard_map/all_to_all | solution.py:398
  82.9 4.5 %collective-permute-start.8 = (bf16[10,128,128]{2,1,0:T(8,128)(2,1)S(1)}, bf16[10,128,128]{2,1,0:T(8,128)(2,1)S(1)}, u32[]{:S(2)}, u32[]{:S(2)}) collective-permute-start(bf16[10,128,128]{2,1,0:T(8,128)(2,1)S(1)} %get-tuple-element.40.high), channel_id=1, source_target_pairs={{0,8},{8,16},{16,24},{24,32},{32,40},{40,48},{48,56},{56,64},{64,7... | collective-permute-start | bytes 983048 | tf_op jit(solution)/shard_map/ppermute | solution.py:382
  87.3 1.9 %collective-permute-start.9 = (bf16[10,128,128]{2,1,0:T(8,128)(2,1)S(1)}, bf16[10,128,128]{2,1,0:T(8,128)(2,1)S(1)}, u32[]{:S(2)}, u32[]{:S(2)}) collective-permute-start(bf16[10,128,128]{2,1,0:T(8,128)(2,1)S(1)} %get-tuple-element.41.low), channel_id=1, source_target_pairs={{8,0},{16,8},{24,16},{32,24},{40,32},{48,40},{56,48},{64,56},{72,6... | collective-permute-start | bytes 983048 | tf_op jit(solution)/shard_map/ppermute | solution.py:383
  89.3 5.4 %all-to-all-done.2 = bf16[16,5,4,128]{3,2,1,0:T(4,128)(2,1)S(1)} async-done(((bf16[16,5,4,128]{3,2,1,0:T(4,128)(2,1)}), bf16[16,5,4,128]{3,2,1,0:T(4,128)(2,1)S(1)}, u32[]{:S(2)}, u32[]{:S(2)}) %all-to-all-start.2) | async-done | bytes 81952 | tf_op jit(solution)/shard_map/all_to_all | solution.py:398
  94.7 0.1 reduce_sum.25
  94.7 0.7 broadcast_in_dim.5
  95.5 5.9 %all-to-all-start.3 = ((bf16[32,5,4,128]{3,2,1,0:T(4,128)(2,1)}), bf16[32,5,4,128]{3,2,1,0:T(4,128)(2,1)S(1)}, u32[]{:S(2)}, u32[]{:S(2)}) async-start(bf16[32,5,4,128]{3,2,1,0:T(4,128)(2,1)} %broadcast_in_dim.5), calls=%async_computation.3 | async-start | bytes 327680 | tf_op jit(solution)/shard_map/all_to_all | solution.py:398
  101.3 0.0 collective-permute-done.8.below
  101.3 0.0 collective-permute-done.9.above
  101.3 2.6 %shard_map.74 = bf16[8,64,256]{2,1,0:T(8,128)(2,1)S(1)} custom-call(bf16[10,128,128]{2,1,0:T(8,128)(2,1)S(1)} %collective-permute-done.8.below, bf16[10,128,128]{2,1,0:T(8,128)(2,1)S(1)} %get-tuple-element.41.low, bf16[10,128,128]{2,1,0:T(8,128)(2,1)S(1)} %get-tuple-element.40.high, bf16[10,128,128]{2,1,0:T(8,128)(2,1)S(1)} %collective-permute-done.9.above, ...), custom_call_target="tpu_custom_call" | custom-call | flops 536870912 | bytes 1600512 | tf_op jit(solution)/shard_map/pallas_call | solution.py:31
  103.9 0.2 copy.31
  104.2 5.2 %all-to-all-done.3 = bf16[32,5,4,128]{3,2,1,0:T(4,128)(2,1)S(1)} async-done(((bf16[32,5,4,128]{3,2,1,0:T(4,128)(2,1)}), bf16[32,5,4,128]{3,2,1,0:T(4,128)(2,1)S(1)}, u32[]{:S(2)}, u32[]{:S(2)}) %all-to-all-start.3) | async-done | bytes 163872 | tf_op jit(solution)/shard_map/all_to_all | solution.py:398
  109.4 0.2 copy.36.lines
  109.6 0.8 reshape.39
  110.4 0.9 shard_map.75
  (7 shorter events, 0.2 us)
Async XLA Ops:
  0.6 24.2 %copy-start = (bf16[3,3,3,32,16]{3,4,2,1,0:T(8,128)(2,1)S(1)}, bf16[3,3,3,32,16]{3,4,2,1,0:T(8,128)(2,1)}, u32[]{:S(2)}) copy-start(bf16[3,3,3,32,16]{3,4,2,1,0:T(8,128)(2,1)} %param.5) | copy-start | bytes 82948
  1.8 8.5 %collective-permute-start.1 = (bf16[7,2,16,256]{3,2,1,0:T(8,128)(2,1)S(1)}, bf16[7,2,16,256]{3,2,1,0:T(8,128)(2,1)S(1)}, u32[]{:S(2)}, u32[]{:S(2)}) collective-permute-start(bf16[7,2,16,256]{3,2,1,0:T(8,128)(2,1)S(1)} %get-tuple-element.45), channel_id=1, source_target_pairs={{1,0},{2,1},{3,2},{4,3},{5,4},{6,5},{7,6},{9,8},{10,9},{11,10},{12... | collective-permute-start | bytes 344072 | tf_op jit(solution)/shard_map/ppermute | solution.py:383
  3.1 14.8 %collective-permute-start = (bf16[7,2,16,256]{3,2,1,0:T(8,128)(2,1)S(1)}, bf16[7,2,16,256]{3,2,1,0:T(8,128)(2,1)S(1)}, u32[]{:S(2)}, u32[]{:S(2)}) collective-permute-start(bf16[7,2,16,256]{3,2,1,0:T(8,128)(2,1)S(1)} %get-tuple-element.46), channel_id=1, source_target_pairs={{0,1},{1,2},{2,3},{3,4},{4,5},{5,6},{6,7},{8,9},{9,10},{10,11},{11... | collective-permute-start | bytes 344072 | tf_op jit(solution)/shard_map/ppermute | solution.py:382
  8.7 0.8 copy-start.1
  10.3 15.6 %all-to-all-start = ((bf16[8,8,2432]{2,1,0:T(8,128)(2,1)}), bf16[8,8,2432]{2,1,0:T(8,128)(2,1)S(1)}, u32[]{:S(2)}, u32[]{:S(2)}) async-start(bf16[8,8,2432]{2,1,0:T(8,128)(2,1)} %shard_map.67), calls=%async_computation | async-start | bytes 622592 | tf_op jit(solution)/shard_map/all_to_all | solution.py:398
  18.0 7.9 %collective-permute-start.2 = (bf16[30,16,256]{2,1,0:T(8,128)(2,1)S(1)}, bf16[30,16,256]{2,1,0:T(8,128)(2,1)S(1)}, u32[]{:S(2)}, u32[]{:S(2)}) collective-permute-start(bf16[30,16,256]{2,1,0:T(8,128)(2,1)S(1)} %get-tuple-element.27), channel_id=1, source_target_pairs={{0,8},{8,0},{16,24},{24,16},{32,40},{40,32},{48,56},{56,48},{64,72... | collective-permute-start | bytes 737288 | tf_op jit(solution)/shard_map/ppermute | solution.py:392
  22.6 7.5 %collective-permute-start.3 = (bf16[30,16,256]{2,1,0:T(8,128)(2,1)S(1)}, bf16[30,16,256]{2,1,0:T(8,128)(2,1)S(1)}, u32[]{:S(2)}, u32[]{:S(2)}) collective-permute-start(bf16[30,16,256]{2,1,0:T(8,128)(2,1)S(1)} %get-tuple-element.28), channel_id=1, source_target_pairs={{8,16},{24,32},{40,48},{56,64},{72,80},{88,96},{104,112},{120,128}... | collective-permute-start | bytes 737288 | tf_op jit(solution)/shard_map/ppermute | solution.py:393
  32.6 6.1 %collective-permute-start.5 = (bf16[14,32,128]{2,1,0:T(8,128)(2,1)S(1)}, bf16[14,32,128]{2,1,0:T(8,128)(2,1)S(1)}, u32[]{:S(2)}, u32[]{:S(2)}) collective-permute-start(bf16[14,32,128]{2,1,0:T(8,128)(2,1)S(1)} %get-tuple-element.31.own), channel_id=1, source_target_pairs={{8,16},{24,32},{40,48},{56,64},{72,80},{88,96},{104,112},{120,128}... | collective-permute-start | bytes 344072 | tf_op jit(solution)/shard_map/ppermute | solution.py:393
  34.9 3.8 %collective-permute-start.4 = (bf16[14,32,128]{2,1,0:T(8,128)(2,1)S(1)}, bf16[14,32,128]{2,1,0:T(8,128)(2,1)S(1)}, u32[]{:S(2)}, u32[]{:S(2)}) collective-permute-start(bf16[14,32,128]{2,1,0:T(8,128)(2,1)S(1)} %get-tuple-element.31.own), channel_id=1, source_target_pairs={{0,8},{8,0},{16,24},{24,16},{32,40},{40,32},{48,56},{56,48},{64,72... | collective-permute-start | bytes 344072 | tf_op jit(solution)/shard_map/ppermute | solution.py:392
  40.1 5.9 %collective-permute-start.6 = (bf16[10,32,128]{2,1,0:T(8,128)(2,1)S(1)}, bf16[10,32,128]{2,1,0:T(8,128)(2,1)S(1)}, u32[]{:S(2)}, u32[]{:S(2)}) collective-permute-start(bf16[10,32,128]{2,1,0:T(8,128)(2,1)S(1)} %get-tuple-element.33), channel_id=1, source_target_pairs={{0,8},{8,0},{16,24},{24,16},{32,40},{40,32},{48,56},{56,48},{64,72... | collective-permute-start | bytes 245768 | tf_op jit(solution)/shard_map/ppermute | solution.py:392
  42.0 5.8 %collective-permute-start.7 = (bf16[10,32,128]{2,1,0:T(8,128)(2,1)S(1)}, bf16[10,32,128]{2,1,0:T(8,128)(2,1)S(1)}, u32[]{:S(2)}, u32[]{:S(2)}) collective-permute-start(bf16[10,32,128]{2,1,0:T(8,128)(2,1)S(1)} %get-tuple-element.35), channel_id=1, source_target_pairs={{8,16},{24,32},{40,48},{56,64},{72,80},{88,96},{104,112},{120,128}... | collective-permute-start | bytes 245768 | tf_op jit(solution)/shard_map/ppermute | solution.py:393
  76.6 18.1 %all-to-all-start.2 = ((bf16[16,5,4,128]{3,2,1,0:T(4,128)(2,1)}), bf16[16,5,4,128]{3,2,1,0:T(4,128)(2,1)S(1)}, u32[]{:S(2)}, u32[]{:S(2)}) async-start(bf16[16,5,4,128]{3,2,1,0:T(4,128)(2,1)} %broadcast_in_dim.4), calls=%async_computation.2 | async-start | bytes 163840 | tf_op jit(solution)/shard_map/all_to_all | solution.py:398
  82.9 18.4 %collective-permute-start.8 = (bf16[10,128,128]{2,1,0:T(8,128)(2,1)S(1)}, bf16[10,128,128]{2,1,0:T(8,128)(2,1)S(1)}, u32[]{:S(2)}, u32[]{:S(2)}) collective-permute-start(bf16[10,128,128]{2,1,0:T(8,128)(2,1)S(1)} %get-tuple-element.40.high), channel_id=1, source_target_pairs={{0,8},{8,16},{16,24},{24,32},{32,40},{40,48},{48,56},{56,64},{64,7... | collective-permute-start | bytes 983048 | tf_op jit(solution)/shard_map/ppermute | solution.py:382
  87.3 14.0 %collective-permute-start.9 = (bf16[10,128,128]{2,1,0:T(8,128)(2,1)S(1)}, bf16[10,128,128]{2,1,0:T(8,128)(2,1)S(1)}, u32[]{:S(2)}, u32[]{:S(2)}) collective-permute-start(bf16[10,128,128]{2,1,0:T(8,128)(2,1)S(1)} %get-tuple-element.41.low), channel_id=1, source_target_pairs={{8,0},{16,8},{24,16},{32,24},{40,32},{48,40},{56,48},{64,56},{72,6... | collective-permute-start | bytes 983048 | tf_op jit(solution)/shard_map/ppermute | solution.py:383
  95.5 13.9 %all-to-all-start.3 = ((bf16[32,5,4,128]{3,2,1,0:T(4,128)(2,1)}), bf16[32,5,4,128]{3,2,1,0:T(4,128)(2,1)S(1)}, u32[]{:S(2)}, u32[]{:S(2)}) async-start(bf16[32,5,4,128]{3,2,1,0:T(4,128)(2,1)} %broadcast_in_dim.5), calls=%async_computation.3 | async-start | bytes 327680 | tf_op jit(solution)/shard_map/all_to_all | solution.py:398

commit v6 on v5

--- a/solution.py
+++ b/solution.py
@@ -114,18 +114,30 @@
     return jnp.logical_and(at >= 0, at < rows * axis_count(GROUP))
 
 
-def edges(own, top, bottom, near, far):
+def sides(own, near, far):
+    odd = lax.rem(lax.axis_index("x"), 2)
+    rest = own.shape[0] - near.shape[0]
+    for row in range(near.shape[0]):
+        near[row] = own[row + rest * (1 - odd)]
+        far[row] = own[row + rest * odd]
+
+
+def edges(own, near_rows, far_rows, near, far):
     core = lax.axis_index("core")
-    at = 0
-    for ref in (top, own, bottom):
-        for row in range(ref.shape[0]):
-            near[at] = ref[row, 1 - core]
-            far[at] = ref[row, core]
-            at += 1
-
-
-def in_order(near, far):
-    lower = lax.axis_index("core") == 0
+    top, bottom = in_order(near_rows, far_rows, "x")
+    count, height = near_rows.shape[0], own.shape[0]
+    for row in range(count):
+        near[row] = top(row, 1 - core)
+        far[row] = top(row, core)
+        near[count + height + row] = bottom(row, 1 - core)
+        far[count + height + row] = bottom(row, core)
+    for row in range(height):
+        near[count + row] = own[row, 1 - core]
+        far[count + row] = own[row, core]
+
+
+def in_order(near, far, name="core"):
+    lower = lax.rem(lax.axis_index(name), 2) == 0
 
     def below(*at):
         return lax.select(lower, far[at], near[at])
@@ -136,13 +148,14 @@
     return below, above
 
 
-def forward_two(own, near, far, top, bottom, weight, pooled, slope, parts, split):
+def forward_two(own, near, far, near_rows, far_rows, weight, pooled, slope, parts, split):
     split[...] = splitter()
     first = pooled.shape[0] - 6
     first = first * group_index() - 3
-    edge = top.shape[0]
+    edge = near_rows.shape[0]
     height = own.shape[0]
     below, above = in_order(near, far)
+    top, bottom = in_order(near_rows, far_rows, "x")
 
     def place(row, many, block):
         cells = dot(block, split[...]).astype(BF16).reshape(many, 64, 4 * BREADTH)
@@ -150,11 +163,15 @@
             to = part * 64
             parts[row : row + many, to : to + 64, :] = cells[:, :, part * BREADTH : (part + 1) * BREADTH]
 
-    for ref, to in ((top, 0), (own, edge), (bottom, edge + height)):
-        for row in range(0, ref.shape[0], 4):
+    for taken, to, many in ((top, 0, edge), (own, edge, height), (bottom, edge + height, edge)):
+        for row in range(0, many, 4):
             block = []
-            for at in range(row, min(row + 4, ref.shape[0])):
-                block += [below(to + at), ref[at, 0], ref[at, 1], above(to + at)]
+            for at in range(row, min(row + 4, many)):
+                if taken is own:
+                    both = [own[at, 0], own[at, 1]]
+                else:
+                    both = [taken(at, 0), taken(at, 1)]
+                block += [below(to + at)] + both + [above(to + at)]
             place(to + row, len(block) // 4, jnp.concatenate(block, axis=0))
 
     rows = pooled.shape[0]
@@ -355,7 +372,7 @@
 
 def spread_out(scale_two, scale_three, lines, two, three):
     for block in range(4):
-        rows = [lines[at, 16 + block : 17 + block, :].astype(F32) for at in range(32)]
+        rows = [lines[at, 4].astype(F32)[block : block + 1] for at in range(32)]
         flat = jnp.transpose(jnp.concatenate(rows * 4, axis=0) * scale_two)
         for tap in range(27):
             a, b, e = tap // 9, (tap // 3) % 3, tap % 3
@@ -364,7 +381,9 @@
                 two[tap] = flat[slot * 16 : slot * 16 + 16, :32]
     for part in range(7):
         at = (part // 2) * 8 + group_index()
-        block = lines[at, (part % 2) * 8 : (part % 2) * 8 + 8, :].astype(F32) * scale_three
+        first = (part % 2) * 2
+        block = [lines[at, first].astype(F32), lines[at, first + 1].astype(F32)]
+        block = jnp.concatenate(block, axis=0) * scale_three
         for at in range(4):
             tap = part * 4 + at
             if tap < 27:
@@ -384,13 +403,13 @@
     )
 
 
-def paired(near, far):
-    count = axis_count(DEPTH)
+def paired(near, far, names=DEPTH):
+    count = axis_count(names)
     across = [(i, i + 1) for i in range(1, count - 1, 2)]
     across += [(i + 1, i) for i in range(1, count - 1, 2)]
     return (
-        lax.ppermute(near, DEPTH, [(i, i ^ 1) for i in range(count)]),
-        lax.ppermute(far, DEPTH, across),
+        lax.ppermute(near, names, [(i, i ^ 1) for i in range(count)]),
+        lax.ppermute(far, names, across),
     )
 
 
@@ -417,7 +436,8 @@
 
     own = jnp.transpose(inputs, (2, 1, 0, 3))
     own, cotangent = lax.optimization_barrier((own, cotangent))
-    top, bottom = neighbours(own[:7], own[height - 7 :], GROUP)
+    rows = jax.ShapeDtypeStruct((7, planes, chans, breadth), BF16)
+    near_rows, far_rows = paired(*call(sides, [rows, rows], [], (own,), 1024), GROUP)
 
     (packed,) = call(
         pack,
@@ -426,11 +446,11 @@
         (jnp.transpose(cotangent[:, 0], (1, 0, 2)), weight_three.reshape(27, share, 32)),
         2 * 64 * 1024,
     )
-    packed, bottom = lax.optimization_barrier((packed, bottom))
+    packed, near_rows = lax.optimization_barrier((packed, near_rows))
     arrived = exchange(packed, GROUP).reshape(filters, -1)
 
     plane = jax.ShapeDtypeStruct((height + 14, chans, breadth), BF16)
-    near, far = paired(*call(edges, [plane, plane], [], (own, top, bottom), 1024 * 1024))
+    near, far = paired(*call(edges, [plane, plane], [], (own, near_rows, far_rows), 1024 * 1024))
 
     turned = jnp.transpose(weight_two.reshape(27, 32, 16), (0, 2, 1))
     (ahead,) = call(
@@ -450,7 +470,7 @@
             jax.ShapeDtypeStruct((height + 14, 256, BREADTH), BF16),
         ],
         [pltpu.VMEM((2 * BREADTH, 4 * BREADTH), BF16)],
-        (own, near, far, top, bottom, ahead),
+        (own, near, far, near_rows, far_rows, ahead),
         2 * 14 * 256 * 1024 * 128,
     )
 
@@ -496,7 +516,7 @@
     lines = lines.astype(BF16).reshape(32, 5, 4, BREADTH)
     lines = total_of(exchange(lines, NEAR))
     lines = total_of(exchange(copied(lines, ("z",)), "z"))
-    lines = exchange(copied(lines, NEAR), NEAR).reshape(32, 20, BREADTH)
+    lines = exchange(copied(lines, NEAR), NEAR)
     two, three = call(
         functools.partial(spread_out, 1.0 / math.sqrt(cells), 1.0 / math.sqrt(cells / 8)),
         [
@@ -504,7 +524,7 @@
             jax.ShapeDtypeStruct((27, share, 32), F32),
         ],
         [],
-        (lines.astype(F32),),
+        (lines,),
         2 * 64 * 1024,
     )
 

time: 112 us -> 109 us (0.973)
  starting transfers between devices: 48.3 us -> 46.3 us
    ppermute x2 -> x1, starting transfers between devices: 9.04 us -> 4.46 us  [neighbours(): lax.ppermute(last, axis, shifted(axis, 1))]
    ppermute x6 -> x8, starting transfers between devices: 16.3 us -> 20.6 us  [the longest x4 13.3 us: paired(): lax.ppermute(near, names, [(i, i ^ 1) for i in range(count)])]
    ppermute x6 -> x8, waiting for transfers between devices: 7.87 us -> 9.74 us  [the longest x4 9.73 us: paired(): lax.ppermute(far, names, across)]
    all_to_all x3, waiting for transfers between devices: 11.3 us -> 9.82 us  [exchange(): return lax.all_to_all(blocks, axis, 0, 0, tiled=True)]
    ppermute x2 -> x1, starting transfers between devices: 3.21 us -> 1.92 us  [neighbours(): lax.ppermute(first, axis, shifted(axis, -1))]
    pallas_call x9 -> x10, Pallas kernels: 10.1 us -> 10.1 us  [call(): pl.pallas_call(kernel, out_shape=outs, in_specs=specs, out_specs=[pl.Bloc...]
  transfers between devices with their start and end apart: 13 -> 13, of which waited for: 6 -> 5; matrix products, arithmetic and copies ran while one was open for 2% -> 3% of each run, Pallas kernels for 4% -> 4%
where the time goes in v6:
time: 109 us; the launch traced here: 108 us
  starting transfers between devices  46.3 us (42%)
  blocking collectives  26 us (24%)
  waiting for transfers between devices  19.6 us (18%)
  Pallas kernels  10.1 us (9%)
  local copies, waits for them, and re-layouts  5.48 us (5%)
    all_to_all x1, blocking collectives, exchange(): return lax.all_to_all(blocks, axis, 0, 0, tiled=True)  26 us
    all_to_all x3, starting transfers between devices, exchange(): return lax.all_to_all(blocks, axis, 0, 0, tiled=True)  19.3 us
    ppermute x4, starting transfers between devices, paired(): lax.ppermute(near, names, [(i, i ^ 1) for i in range(count)])  13.3 us
    pallas_call x10, Pallas kernels, call(): pl.pallas_call(kernel, out_shape=outs, in_specs=specs, out_specs=[pl.Bloc...  10.1 us
    all_to_all x3, waiting for transfers between devices, exchange(): return lax.all_to_all(blocks, axis, 0, 0, tiled=True)  9.82 us
    ppermute x4, waiting for transfers between devices, paired(): lax.ppermute(far, names, across)  9.73 us
    ppermute x4, starting transfers between devices, paired(): lax.ppermute(far, names, across)  7.32 us
    ppermute x1, starting transfers between devices, neighbours(): lax.ppermute(last, axis, shifted(axis, 1))  4.46 us
  transfers between devices with their start and end apart: 13, of which 5 were waited for; matrix products, arithmetic and copies ran while one was open for 3% of the time, Pallas kernels for 4%

profile of v6, /device:TPU:1, one launch (start us, length us, event | category | flops | bytes accessed | tf_op | source)
XLA Modules:
  0.0 108.5 jit_solution(6472615490340622244)
XLA Ops:
  0.6 0.0 copy-start
  0.6 1.1 %copy.33 = bf16[16,2,16,256]{3,0,1,2:T(8,128)(2,1)S(1)} copy(bf16[16,2,16,256]{3,2,1,0:T(8,128)(2,1)} %param.4) | data formatting | bytes 524288 | tf_op args[0]
  1.8 3.9 %collective-permute-start = (bf16[7,2,16,256]{3,2,1,0:T(8,128)(2,1)S(1)}, bf16[7,2,16,256]{3,2,1,0:T(8,128)(2,1)S(1)}, u32[]{:S(2)}, u32[]{:S(2)}) collective-permute-start(bf16[7,2,16,256]{3,2,1,0:T(8,128)(2,1)S(1)} %get-tuple-element.28), channel_id=1, source_target_pairs={{0,1},{1,0},{2,3},{3,2},{4,5},{5,4},{6,7},{7,6},{8,9},{9,8},{10,11... | collective-permute-start | bytes 344072 | tf_op jit(solution)/shard_map/ppermute | solution.py:411
  5.8 0.7 collective-permute-start.1
  6.4 1.0 copy.34
  7.4 0.0 copy-start.1
  7.5 0.8 copy-done.1
  8.3 0.8 shard_map.67
  9.1 0.0 collective-permute-done.near_rows
  9.1 7.8 %all-to-all-start = ((bf16[8,8,2432]{2,1,0:T(8,128)(2,1)}), bf16[8,8,2432]{2,1,0:T(8,128)(2,1)S(1)}, u32[]{:S(2)}, u32[]{:S(2)}) async-start(bf16[8,8,2432]{2,1,0:T(8,128)(2,1)} %shard_map.67), calls=%async_computation | async-start | bytes 622592 | tf_op jit(solution)/shard_map/all_to_all | solution.py:417
  16.9 0.0 collective-permute-done.1.far_rows
  17.0 5.5 %collective-permute-start.2 = (bf16[30,16,256]{2,1,0:T(8,128)(2,1)S(1)}, bf16[30,16,256]{2,1,0:T(8,128)(2,1)S(1)}, u32[]{:S(2)}, u32[]{:S(2)}) collective-permute-start(bf16[30,16,256]{2,1,0:T(8,128)(2,1)S(1)} %get-tuple-element.31), channel_id=1, source_target_pairs={{0,8},{8,0},{16,24},{24,16},{32,40},{40,32},{48,56},{56,48},{64,72... | collective-permute-start | bytes 737288 | tf_op jit(solution)/shard_map/ppermute | solution.py:411
  22.5 1.9 %collective-permute-start.3 = (bf16[30,16,256]{2,1,0:T(8,128)(2,1)S(1)}, bf16[30,16,256]{2,1,0:T(8,128)(2,1)S(1)}, u32[]{:S(2)}, u32[]{:S(2)}) collective-permute-start(bf16[30,16,256]{2,1,0:T(8,128)(2,1)S(1)} %get-tuple-element.32), channel_id=1, source_target_pairs={{8,16},{24,32},{40,48},{56,64},{72,80},{88,96},{104,112},{120,128}... | collective-permute-start | bytes 737288 | tf_op jit(solution)/shard_map/ppermute | solution.py:412
  24.4 0.0 copy-done
  24.4 0.4 shard_map.70.weight
  24.8 0.0 all-to-all-done
  24.8 0.0 collective-permute-done.2.near
  24.8 5.2 %collective-permute-done.3.far = bf16[30,16,256]{2,1,0:T(8,128)(2,1)S(1)} collective-permute-done((bf16[30,16,256]{2,1,0:T(8,128)(2,1)S(1)}, bf16[30,16,256]{2,1,0:T(8,128)(2,1)S(1)}, u32[]{:S(2)}, u32[]{:S(2)}) %collective-permute-start.3) | collective-permute-done | bytes 245792 | tf_op jit(solution)/shard_map/ppermute | solution.py:412
  30.0 2.5 %shard_map.71 = (bf16[14,32,128]{2,1,0:T(8,128)(2,1)S(1)}, f32[10,256,128]{2,1,0:T(8,128)S(1)}, bf16[30,256,128]{2,1,0:T(8,128)(2,1)S(1)}) custom-call(bf16[16,2,16,256]{3,2,1,0:T(8,128)(2,1)S(1)} %bitcast.23, bf16[30,16,256]{2,1,0:T(8,128)(2,1)S(1)} %collective-permute-done.2.near, bf16[30,16,256]{2,1,0:T(8,128)(2,1)S(1)} %collective-permute-done.3.far, ...), custom_call_target="tpu_custom_call" | custom-call | flops 939524096 | bytes 4898816 | tf_op jit(solution)/shard_map/pallas_call | solution.py:31
  32.5 1.9 %collective-permute-start.5 = (bf16[14,32,128]{2,1,0:T(8,128)(2,1)S(1)}, bf16[14,32,128]{2,1,0:T(8,128)(2,1)S(1)}, u32[]{:S(2)}, u32[]{:S(2)}) collective-permute-start(bf16[14,32,128]{2,1,0:T(8,128)(2,1)S(1)} %get-tuple-element.35.own), channel_id=1, source_target_pairs={{8,16},{24,32},{40,48},{56,64},{72,80},{88,96},{104,112},{120,128}... | collective-permute-start | bytes 344072 | tf_op jit(solution)/shard_map/ppermute | solution.py:412
  34.5 1.9 %collective-permute-start.4 = (bf16[14,32,128]{2,1,0:T(8,128)(2,1)S(1)}, bf16[14,32,128]{2,1,0:T(8,128)(2,1)S(1)}, u32[]{:S(2)}, u32[]{:S(2)}) collective-permute-start(bf16[14,32,128]{2,1,0:T(8,128)(2,1)S(1)} %get-tuple-element.35.own), channel_id=1, source_target_pairs={{0,8},{8,0},{16,24},{24,16},{32,40},{40,32},{48,56},{56,48},{64,72... | collective-permute-start | bytes 344072 | tf_op jit(solution)/shard_map/ppermute | solution.py:411
  36.4 2.3 %collective-permute-done.5.far = bf16[14,32,128]{2,1,0:T(8,128)(2,1)S(1)} collective-permute-done((bf16[14,32,128]{2,1,0:T(8,128)(2,1)S(1)}, bf16[14,32,128]{2,1,0:T(8,128)(2,1)S(1)}, u32[]{:S(2)}, u32[]{:S(2)}) %collective-permute-start.5) | collective-permute-done | bytes 114720 | tf_op jit(solution)/shard_map/ppermute | solution.py:412
  38.7 0.0 collective-permute-done.4.near
  38.7 1.3 %shard_map.72 = (bf16[12,64,128]{2,1,0:T(8,128)(2,1)S(1)}, bf16[14,288,128]{2,1,0:T(8,128)(2,1)S(1)}, bf16[10,32,128]{2,1,0:T(8,128)(2,1)S(1)}, f32[10,32,128]{2,1,0:T(8,128)S(1)}, bf16[10,32,128]{2,1,0:T(8,128)(2,1)S(1)}) custom-call(bf16[14,32,128]{2,1,0:T(8,128)(2,1)S(1)} %collective-permute-done.4.near, bf16[14,32,128]{2,1,0:T(8,128)(2,1)S(1)} %get-tuple-element.35.own, ...), custom_call_target="tpu_custom_call" | custom-call | flops 339738624 | bytes 2211840 | tf_op jit(solution)/shard_map/pallas_call | solution.py:31
  40.0 1.9 %collective-permute-start.6 = (bf16[10,32,128]{2,1,0:T(8,128)(2,1)S(1)}, bf16[10,32,128]{2,1,0:T(8,128)(2,1)S(1)}, u32[]{:S(2)}, u32[]{:S(2)}) collective-permute-start(bf16[10,32,128]{2,1,0:T(8,128)(2,1)S(1)} %get-tuple-element.37), channel_id=1, source_target_pairs={{0,8},{8,0},{16,24},{24,16},{32,40},{40,32},{48,56},{56,48},{64,72... | collective-permute-start | bytes 245768 | tf_op jit(solution)/shard_map/ppermute | solution.py:411
  41.9 2.8 %collective-permute-start.7 = (bf16[10,32,128]{2,1,0:T(8,128)(2,1)S(1)}, bf16[10,32,128]{2,1,0:T(8,128)(2,1)S(1)}, u32[]{:S(2)}, u32[]{:S(2)}) collective-permute-start(bf16[10,32,128]{2,1,0:T(8,128)(2,1)S(1)} %get-tuple-element.39), channel_id=1, source_target_pairs={{8,16},{24,32},{40,48},{56,64},{72,80},{88,96},{104,112},{120,128}... | collective-permute-start | bytes 245768 | tf_op jit(solution)/shard_map/ppermute | solution.py:412
  44.7 0.6 shard_map.73.three
  45.4 0.0 collective-permute-done.6.near
  45.4 2.3 %collective-permute-done.7.far = bf16[10,32,128]{2,1,0:T(8,128)(2,1)S(1)} collective-permute-done((bf16[10,32,128]{2,1,0:T(8,128)(2,1)S(1)}, bf16[10,32,128]{2,1,0:T(8,128)(2,1)S(1)}, u32[]{:S(2)}, u32[]{:S(2)}) %collective-permute-start.7) | collective-permute-done | bytes 81952 | tf_op jit(solution)/shard_map/ppermute | solution.py:412
  47.7 0.9 shard_map.74
  48.7 0.1 copy.28
  48.8 26.0 %all_to_all.20 = bf16[32,5,4,128]{3,2,1,0:T(4,128)(2,1)S(1)} all-to-all(bf16[32,5,4,128]{3,2,1,0:T(4,128)(2,1)S(1)} %copy.28), channel_id=1, replica_groups=mesh['yl'=2,'z'=16,'core'=2,'yh'=2,'x'=4] {'yl','core','yh','x'}, dimensions={0} | all-to-all | bytes 327680 | tf_op jit(solution)/shard_map/all_to_all | solution.py:417
  74.7 0.1 reduce_sum.24
  74.8 0.7 broadcast_in_dim.4
  75.5 5.6 %all-to-all-start.2 = ((bf16[16,5,4,128]{3,2,1,0:T(4,128)(2,1)}), bf16[16,5,4,128]{3,2,1,0:T(4,128)(2,1)S(1)}, u32[]{:S(2)}, u32[]{:S(2)}) async-start(bf16[16,5,4,128]{3,2,1,0:T(4,128)(2,1)} %broadcast_in_dim.4), calls=%async_computation.2 | async-start | bytes 163840 | tf_op jit(solution)/shard_map/all_to_all | solution.py:417
  81.1 4.5 %collective-permute-start.8 = (bf16[10,128,128]{2,1,0:T(8,128)(2,1)S(1)}, bf16[10,128,128]{2,1,0:T(8,128)(2,1)S(1)}, u32[]{:S(2)}, u32[]{:S(2)}) collective-permute-start(bf16[10,128,128]{2,1,0:T(8,128)(2,1)S(1)} %get-tuple-element.44.high), channel_id=1, source_target_pairs={{0,8},{8,16},{16,24},{24,32},{32,40},{40,48},{48,56},{56,64},{64,7... | collective-permute-start | bytes 983048 | tf_op jit(solution)/shard_map/ppermute | solution.py:401
  85.6 1.9 %collective-permute-start.9 = (bf16[10,128,128]{2,1,0:T(8,128)(2,1)S(1)}, bf16[10,128,128]{2,1,0:T(8,128)(2,1)S(1)}, u32[]{:S(2)}, u32[]{:S(2)}) collective-permute-start(bf16[10,128,128]{2,1,0:T(8,128)(2,1)S(1)} %get-tuple-element.45.low), channel_id=1, source_target_pairs={{8,0},{16,8},{24,16},{32,24},{40,32},{48,40},{56,48},{64,56},{72,6... | collective-permute-start | bytes 983048 | tf_op jit(solution)/shard_map/ppermute | solution.py:402
  87.5 5.4 %all-to-all-done.2 = bf16[16,5,4,128]{3,2,1,0:T(4,128)(2,1)S(1)} async-done(((bf16[16,5,4,128]{3,2,1,0:T(4,128)(2,1)}), bf16[16,5,4,128]{3,2,1,0:T(4,128)(2,1)S(1)}, u32[]{:S(2)}, u32[]{:S(2)}) %all-to-all-start.2) | async-done | bytes 81952 | tf_op jit(solution)/shard_map/all_to_all | solution.py:417
  92.9 0.1 reduce_sum.25
  93.0 0.7 broadcast_in_dim.5
  93.7 5.9 %all-to-all-start.3 = ((bf16[32,5,4,128]{3,2,1,0:T(4,128)(2,1)}), bf16[32,5,4,128]{3,2,1,0:T(4,128)(2,1)S(1)}, u32[]{:S(2)}, u32[]{:S(2)}) async-start(bf16[32,5,4,128]{3,2,1,0:T(4,128)(2,1)} %broadcast_in_dim.5), calls=%async_computation.3 | async-start | bytes 327680 | tf_op jit(solution)/shard_map/all_to_all | solution.py:417
  99.5 0.0 collective-permute-done.8.below
  99.5 0.0 collective-permute-done.9.above
  99.6 2.6 %shard_map.75 = bf16[8,64,256]{2,1,0:T(8,128)(2,1)S(1)} custom-call(bf16[10,128,128]{2,1,0:T(8,128)(2,1)S(1)} %collective-permute-done.8.below, bf16[10,128,128]{2,1,0:T(8,128)(2,1)S(1)} %get-tuple-element.45.low, bf16[10,128,128]{2,1,0:T(8,128)(2,1)S(1)} %get-tuple-element.44.high, bf16[10,128,128]{2,1,0:T(8,128)(2,1)S(1)} %collective-permute-done.9.above, ...), custom_call_target="tpu_custom_call" | custom-call | flops 536870912 | bytes 1600512 | tf_op jit(solution)/shard_map/pallas_call | solution.py:31
  102.1 0.2 copy.26
  102.4 0.8 reshape.36
  103.2 4.4 %all-to-all-done.3.lines = bf16[32,5,4,128]{3,2,1,0:T(4,128)(2,1)S(1)} async-done(((bf16[32,5,4,128]{3,2,1,0:T(4,128)(2,1)}), bf16[32,5,4,128]{3,2,1,0:T(4,128)(2,1)S(1)}, u32[]{:S(2)}, u32[]{:S(2)}) %all-to-all-start.3) | async-done | bytes 163872 | tf_op jit(solution)/shard_map/all_to_all | solution.py:417
  107.6 0.9 shard_map.76
  (4 shorter events, 0.1 us)
Async XLA Ops:
  0.6 23.8 %copy-start = (bf16[3,3,3,32,16]{3,4,2,1,0:T(8,128)(2,1)S(1)}, bf16[3,3,3,32,16]{3,4,2,1,0:T(8,128)(2,1)}, u32[]{:S(2)}) copy-start(bf16[3,3,3,32,16]{3,4,2,1,0:T(8,128)(2,1)} %param.5) | copy-start | bytes 82948
  1.8 7.3 %collective-permute-start = (bf16[7,2,16,256]{3,2,1,0:T(8,128)(2,1)S(1)}, bf16[7,2,16,256]{3,2,1,0:T(8,128)(2,1)S(1)}, u32[]{:S(2)}, u32[]{:S(2)}) collective-permute-start(bf16[7,2,16,256]{3,2,1,0:T(8,128)(2,1)S(1)} %get-tuple-element.28), channel_id=1, source_target_pairs={{0,1},{1,0},{2,3},{3,2},{4,5},{5,4},{6,7},{7,6},{8,9},{9,8},{10,11... | collective-permute-start | bytes 344072 | tf_op jit(solution)/shard_map/ppermute | solution.py:411
  5.8 11.1 %collective-permute-start.1 = (bf16[7,2,16,256]{3,2,1,0:T(8,128)(2,1)S(1)}, bf16[7,2,16,256]{3,2,1,0:T(8,128)(2,1)S(1)}, u32[]{:S(2)}, u32[]{:S(2)}) collective-permute-start(bf16[7,2,16,256]{3,2,1,0:T(8,128)(2,1)S(1)} %get-tuple-element.30), channel_id=1, source_target_pairs={{1,2},{3,4},{5,6},{2,1},{4,3},{6,5},{9,10},{11,12},{13,14},{10,9},... | collective-permute-start | bytes 344072 | tf_op jit(solution)/shard_map/ppermute | solution.py:412
  7.4 0.8 copy-start.1
  9.1 15.7 %all-to-all-start = ((bf16[8,8,2432]{2,1,0:T(8,128)(2,1)}), bf16[8,8,2432]{2,1,0:T(8,128)(2,1)S(1)}, u32[]{:S(2)}, u32[]{:S(2)}) async-start(bf16[8,8,2432]{2,1,0:T(8,128)(2,1)} %shard_map.67), calls=%async_computation | async-start | bytes 622592 | tf_op jit(solution)/shard_map/all_to_all | solution.py:417
  17.0 7.9 %collective-permute-start.2 = (bf16[30,16,256]{2,1,0:T(8,128)(2,1)S(1)}, bf16[30,16,256]{2,1,0:T(8,128)(2,1)S(1)}, u32[]{:S(2)}, u32[]{:S(2)}) collective-permute-start(bf16[30,16,256]{2,1,0:T(8,128)(2,1)S(1)} %get-tuple-element.31), channel_id=1, source_target_pairs={{0,8},{8,0},{16,24},{24,16},{32,40},{40,32},{48,56},{56,48},{64,72... | collective-permute-start | bytes 737288 | tf_op jit(solution)/shard_map/ppermute | solution.py:411
  22.5 7.5 %collective-permute-start.3 = (bf16[30,16,256]{2,1,0:T(8,128)(2,1)S(1)}, bf16[30,16,256]{2,1,0:T(8,128)(2,1)S(1)}, u32[]{:S(2)}, u32[]{:S(2)}) collective-permute-start(bf16[30,16,256]{2,1,0:T(8,128)(2,1)S(1)} %get-tuple-element.32), channel_id=1, source_target_pairs={{8,16},{24,32},{40,48},{56,64},{72,80},{88,96},{104,112},{120,128}... | collective-permute-start | bytes 737288 | tf_op jit(solution)/shard_map/ppermute | solution.py:412
  32.5 6.1 %collective-permute-start.5 = (bf16[14,32,128]{2,1,0:T(8,128)(2,1)S(1)}, bf16[14,32,128]{2,1,0:T(8,128)(2,1)S(1)}, u32[]{:S(2)}, u32[]{:S(2)}) collective-permute-start(bf16[14,32,128]{2,1,0:T(8,128)(2,1)S(1)} %get-tuple-element.35.own), channel_id=1, source_target_pairs={{8,16},{24,32},{40,48},{56,64},{72,80},{88,96},{104,112},{120,128}... | collective-permute-start | bytes 344072 | tf_op jit(solution)/shard_map/ppermute | solution.py:412
  34.5 4.2 %collective-permute-start.4 = (bf16[14,32,128]{2,1,0:T(8,128)(2,1)S(1)}, bf16[14,32,128]{2,1,0:T(8,128)(2,1)S(1)}, u32[]{:S(2)}, u32[]{:S(2)}) collective-permute-start(bf16[14,32,128]{2,1,0:T(8,128)(2,1)S(1)} %get-tuple-element.35.own), channel_id=1, source_target_pairs={{0,8},{8,0},{16,24},{24,16},{32,40},{40,32},{48,56},{56,48},{64,72... | collective-permute-start | bytes 344072 | tf_op jit(solution)/shard_map/ppermute | solution.py:411
  40.0 5.4 %collective-permute-start.6 = (bf16[10,32,128]{2,1,0:T(8,128)(2,1)S(1)}, bf16[10,32,128]{2,1,0:T(8,128)(2,1)S(1)}, u32[]{:S(2)}, u32[]{:S(2)}) collective-permute-start(bf16[10,32,128]{2,1,0:T(8,128)(2,1)S(1)} %get-tuple-element.37), channel_id=1, source_target_pairs={{0,8},{8,0},{16,24},{24,16},{32,40},{40,32},{48,56},{56,48},{64,72... | collective-permute-start | bytes 245768 | tf_op jit(solution)/shard_map/ppermute | solution.py:411
  41.9 5.8 %collective-permute-start.7 = (bf16[10,32,128]{2,1,0:T(8,128)(2,1)S(1)}, bf16[10,32,128]{2,1,0:T(8,128)(2,1)S(1)}, u32[]{:S(2)}, u32[]{:S(2)}) collective-permute-start(bf16[10,32,128]{2,1,0:T(8,128)(2,1)S(1)} %get-tuple-element.39), channel_id=1, source_target_pairs={{8,16},{24,32},{40,48},{56,64},{72,80},{88,96},{104,112},{120,128}... | collective-permute-start | bytes 245768 | tf_op jit(solution)/shard_map/ppermute | solution.py:412
  75.5 17.4 %all-to-all-start.2 = ((bf16[16,5,4,128]{3,2,1,0:T(4,128)(2,1)}), bf16[16,5,4,128]{3,2,1,0:T(4,128)(2,1)S(1)}, u32[]{:S(2)}, u32[]{:S(2)}) async-start(bf16[16,5,4,128]{3,2,1,0:T(4,128)(2,1)} %broadcast_in_dim.4), calls=%async_computation.2 | async-start | bytes 163840 | tf_op jit(solution)/shard_map/all_to_all | solution.py:417
  81.1 18.4 %collective-permute-start.8 = (bf16[10,128,128]{2,1,0:T(8,128)(2,1)S(1)}, bf16[10,128,128]{2,1,0:T(8,128)(2,1)S(1)}, u32[]{:S(2)}, u32[]{:S(2)}) collective-permute-start(bf16[10,128,128]{2,1,0:T(8,128)(2,1)S(1)} %get-tuple-element.44.high), channel_id=1, source_target_pairs={{0,8},{8,16},{16,24},{24,32},{32,40},{40,48},{48,56},{56,64},{64,7... | collective-permute-start | bytes 983048 | tf_op jit(solution)/shard_map/ppermute | solution.py:401
  85.6 14.0 %collective-permute-start.9 = (bf16[10,128,128]{2,1,0:T(8,128)(2,1)S(1)}, bf16[10,128,128]{2,1,0:T(8,128)(2,1)S(1)}, u32[]{:S(2)}, u32[]{:S(2)}) collective-permute-start(bf16[10,128,128]{2,1,0:T(8,128)(2,1)S(1)} %get-tuple-element.45.low), channel_id=1, source_target_pairs={{8,0},{16,8},{24,16},{32,24},{40,32},{48,40},{56,48},{64,56},{72,6... | collective-permute-start | bytes 983048 | tf_op jit(solution)/shard_map/ppermute | solution.py:402
  93.7 13.9 %all-to-all-start.3 = ((bf16[32,5,4,128]{3,2,1,0:T(4,128)(2,1)}), bf16[32,5,4,128]{3,2,1,0:T(4,128)(2,1)S(1)}, u32[]{:S(2)}, u32[]{:S(2)}) async-start(bf16[32,5,4,128]{3,2,1,0:T(4,128)(2,1)} %broadcast_in_dim.5), calls=%async_computation.3 | async-start | bytes 327680 | tf_op jit(solution)/shard_map/all_to_all | solution.py:417

commit v7 on v6

--- a/solution.py
+++ b/solution.py
@@ -25,8 +25,9 @@
     return lax.axis_index("yh") * lax.axis_size("x") + lax.axis_index("x")
 
 
-def call(kernel, outs, scratch, args, flops):
-    specs = [pl.BlockSpec(memory_space=pltpu.VMEM)] * len(args)
+def call(kernel, outs, scratch, args, flops, outside=0, room=16):
+    specs = [pl.BlockSpec(memory_space=pl.ANY)] * outside
+    specs += [pl.BlockSpec(memory_space=pltpu.VMEM)] * (len(args) - outside)
     moved = sum(math.prod(a.shape) * a.dtype.itemsize for a in list(args) + list(outs))
     return pl.pallas_call(
         kernel,
@@ -34,7 +35,7 @@
         in_specs=specs,
         out_specs=[pl.BlockSpec(memory_space=pltpu.VMEM)] * len(outs),
         scratch_shapes=scratch,
-        compiler_params=pltpu.CompilerParams(vmem_limit_bytes=16 * 1024 * 1024),
+        compiler_params=pltpu.CompilerParams(vmem_limit_bytes=room * 1024 * 1024),
         cost_estimate=pl.CostEstimate(flops=flops, bytes_accessed=moved, transcendentals=0),
     )(*args)
 
@@ -215,10 +216,27 @@
     )
 
 
-def pack(cot, taps, out):
+def pack(taps_in, cot_in, out, taps, rows_in, done):
+    copies = [
+        pltpu.make_async_copy(cot_in, rows_in, done.at[0]),
+        pltpu.make_async_copy(taps_in, taps, done.at[1]),
+    ]
+    for copy in copies:
+        copy.start()
+    copies[0].wait()
     count, share, width = out.shape
+    cot = jnp.swapaxes(rows_in[...].astype(F32), 0, 1).astype(BF16)
     rows = cot.shape[0] // count
     extra = (width - 896) // BREADTH - rows
+    for to in range(count):
+        for row in range(rows + extra):
+            at = rows * to - extra // 2 + row
+            lane = row * BREADTH
+            if 0 <= at < cot.shape[0]:
+                out[to, :, lane : lane + BREADTH] = cot[at]
+            else:
+                out[to, :, lane : lane + BREADTH] = jnp.zeros((share, BREADTH), BF16)
+    copies[1].wait()
     blocks = []
     for part in range(7):
         piece = []
@@ -227,13 +245,6 @@
             piece.append(taps[at].astype(F32) if tap < 27 else jnp.zeros((share, 32), F32))
         blocks.append(jnp.concatenate(piece, axis=1).astype(BF16))
     for to in range(count):
-        for row in range(rows + extra):
-            at = rows * to - extra // 2 + row
-            lane = row * BREADTH
-            if 0 <= at < cot.shape[0]:
-                out[to, :, lane : lane + BREADTH] = cot[at]
-            else:
-                out[to, :, lane : lane + BREADTH] = jnp.zeros((share, BREADTH), BF16)
         for part in range(7):
             lane = (rows + extra + part) * BREADTH
             out[to, :, lane : lane + BREADTH] = blocks[part]
@@ -328,12 +339,15 @@
     dense.append(rest)
     for to in range(32):
         quarter, group = to // 8, to % 8
-        for part in range(2):
-            lane = (quarter * 2 + part) * BREADTH
-            block = three[group * 8 : group * 8 + 8, lane : lane + BREADTH]
-            lines[to, part * 8 : part * 8 + 8, :] = block
+        row = 0
+        while row < 14:
+            part, off = divmod(quarter * 14 + row, 8)
+            many = min(8 - off, 14 - row)
+            at, lane = group * 8 + off, part * BREADTH
+            lines[to, row : row + many, :] = three[at : at + many, lane : lane + BREADTH]
+            row += many
         for block in range(4):
-            lines[to, 16 + block : 17 + block, :] = dense[block][to : to + 1]
+            lines[to, 14 + block : 15 + block, :] = dense[block][to : to + 1]
 
 
 def slot_of(b, e, a):
@@ -372,17 +386,17 @@
 
 def spread_out(scale_two, scale_three, lines, two, three):
     for block in range(4):
-        rows = [lines[at, 4].astype(F32)[block : block + 1] for at in range(32)]
+        pair, off = divmod(block, 2)
+        rows = [lines[at, 7 + pair].astype(F32)[off : off + 1] for at in range(32)]
         flat = jnp.transpose(jnp.concatenate(rows * 4, axis=0) * scale_two)
         for tap in range(27):
             a, b, e = tap // 9, (tap // 3) % 3, tap % 3
             where, slot = slot_of(b, e, a)
             if where == block:
                 two[tap] = flat[slot * 16 : slot * 16 + 16, :32]
+    pairs = [lines[at * 8 + group_index(), pair] for at in range(4) for pair in range(7)]
     for part in range(7):
-        at = (part // 2) * 8 + group_index()
-        first = (part % 2) * 2
-        block = [lines[at, first].astype(F32), lines[at, first + 1].astype(F32)]
+        block = [pair.astype(F32) for pair in pairs[part * 4 : part * 4 + 4]]
         block = jnp.concatenate(block, axis=0) * scale_three
         for at in range(4):
             tap = part * 4 + at
@@ -442,9 +456,15 @@
     (packed,) = call(
         pack,
         [jax.ShapeDtypeStruct((groups, share, (pool_rows + 4) * BREADTH + 896), BF16)],
-        [],
-        (jnp.transpose(cotangent[:, 0], (1, 0, 2)), weight_three.reshape(27, share, 32)),
+        [
+            pltpu.VMEM((27, share, 32), BF16),
+            pltpu.VMEM((share, pool_rows * groups, BREADTH), BF16),
+            pltpu.SemaphoreType.DMA((2,)),
+        ],
+        (weight_three.reshape(27, share, 32), cotangent[:, 0]),
         2 * 64 * 1024,
+        outside=2,
+        room=56,
     )
     packed, near_rows = lax.optimization_barrier((packed, near_rows))
     arrived = exchange(packed, GROUP).reshape(filters, -1)
@@ -506,14 +526,14 @@
     plane = jax.ShapeDtypeStruct((pool_rows + 2, 128, BREADTH), BF16)
     low, high, lines = call(
         middle_two,
-        [plane, plane, jax.ShapeDtypeStruct((32, 20, BREADTH), F32)],
+        [plane, plane, jax.ShapeDtypeStruct((32, 18, BREADTH), F32)],
         [],
         (terms_near, same, terms_far, slope, parts_two, local_three),
         2 * 8 * 256 * 1024 * 128,
     )
 
     two_below, two_above = neighbours(low, high, DEPTH)
-    lines = lines.astype(BF16).reshape(32, 5, 4, BREADTH)
+    lines = lines.astype(BF16).reshape(32, 9, 2, BREADTH)
     lines = total_of(exchange(lines, NEAR))
     lines = total_of(exchange(copied(lines, ("z",)), "z"))
     lines = exchange(copied(lines, NEAR), NEAR)

time: 109 us -> 108 us (level)
  local copies, waits for them, and re-layouts: 5.48 us -> 3.75 us
  transfers between devices with their start and end apart: 13 -> 13, of which waited for: 5 -> 5; matrix products, arithmetic and copies ran while one was open for 3% -> 2% of each run, Pallas kernels for 4% -> 5%
where the time goes in v7:
time: 108 us; the launch traced here: 107 us
  starting transfers between devices  46.2 us (43%)
  blocking collectives  25.8 us (24%)
  waiting for transfers between devices  19.3 us (18%)
  Pallas kernels  11.1 us (10%)
  local copies, waits for them, and re-layouts  3.75 us (3%)
    all_to_all x1, blocking collectives, exchange(): return lax.all_to_all(blocks, axis, 0, 0, tiled=True)  25.8 us
    all_to_all x3, starting transfers between devices, exchange(): return lax.all_to_all(blocks, axis, 0, 0, tiled=True)  19.2 us
    ppermute x4, starting transfers between devices, paired(): lax.ppermute(near, names, [(i, i ^ 1) for i in range(count)])  13.3 us
    pallas_call x10, Pallas kernels, call(): pl.pallas_call(kernel, out_shape=outs, in_specs=specs, out_specs=[pl.Bloc...  11.1 us
    ppermute x4, waiting for transfers between devices, paired(): lax.ppermute(far, names, across)  9.72 us
    all_to_all x3, waiting for transfers between devices, exchange(): return lax.all_to_all(blocks, axis, 0, 0, tiled=True)  9.56 us
    ppermute x4, starting transfers between devices, paired(): lax.ppermute(far, names, across)  7.32 us
    ppermute x1, starting transfers between devices, neighbours(): lax.ppermute(last, axis, shifted(axis, 1))  4.44 us
  transfers between devices with their start and end apart: 13, of which 5 were waited for; matrix products, arithmetic and copies ran while one was open for 2% of the time, Pallas kernels for 5%

profile of v7, /device:TPU:1, one launch (start us, length us, event | category | flops | bytes accessed | tf_op | source)
XLA Modules:
  0.0 107.3 jit_solution(18318347595740384258)
XLA Ops:
  0.6 0.0 copy-start
  0.6 1.1 %copy.27 = bf16[16,2,16,256]{3,0,1,2:T(8,128)(2,1)S(1)} copy(bf16[16,2,16,256]{3,2,1,0:T(8,128)(2,1)} %param.4) | data formatting | bytes 524288 | tf_op args[0]
  1.8 3.9 %collective-permute-start = (bf16[7,2,16,256]{3,2,1,0:T(8,128)(2,1)S(1)}, bf16[7,2,16,256]{3,2,1,0:T(8,128)(2,1)S(1)}, u32[]{:S(2)}, u32[]{:S(2)}) collective-permute-start(bf16[7,2,16,256]{3,2,1,0:T(8,128)(2,1)S(1)} %get-tuple-element.28), channel_id=1, source_target_pairs={{0,1},{1,0},{2,3},{3,2},{4,5},{5,4},{6,7},{7,6},{8,9},{9,8},{10,11... | collective-permute-start | bytes 344072 | tf_op jit(solution)/shard_map/ppermute | solution.py:425
  5.8 0.7 collective-permute-start.1
  6.4 1.8 %shard_map.67 = bf16[8,8,2432]{2,1,0:T(8,128)(2,1)} custom-call(bf16[27,8,32]{2,1,0:T(8,128)(2,1)} %bitcast.26, bf16[8,64,128]{2,1,0:T(8,128)(2,1)} %bitcast.25), custom_call_target="tpu_custom_call" | custom-call | flops 131072 | bytes 456192 | tf_op jit(solution)/shard_map/pallas_call | solution.py:32
  8.2 0.0 collective-permute-done.near_rows
  8.3 7.8 %all-to-all-start = ((bf16[8,8,2432]{2,1,0:T(8,128)(2,1)}), bf16[8,8,2432]{2,1,0:T(8,128)(2,1)S(1)}, u32[]{:S(2)}, u32[]{:S(2)}) async-start(bf16[8,8,2432]{2,1,0:T(8,128)(2,1)} %shard_map.67), calls=%async_computation | async-start | bytes 622592 | tf_op jit(solution)/shard_map/all_to_all | solution.py:431
  16.1 0.0 collective-permute-done.1.far_rows
  16.2 5.5 %collective-permute-start.2 = (bf16[30,16,256]{2,1,0:T(8,128)(2,1)S(1)}, bf16[30,16,256]{2,1,0:T(8,128)(2,1)S(1)}, u32[]{:S(2)}, u32[]{:S(2)}) collective-permute-start(bf16[30,16,256]{2,1,0:T(8,128)(2,1)S(1)} %get-tuple-element.31), channel_id=1, source_target_pairs={{0,8},{8,0},{16,24},{24,16},{32,40},{40,32},{48,56},{56,48},{64,72... | collective-permute-start | bytes 737288 | tf_op jit(solution)/shard_map/ppermute | solution.py:425
  21.7 1.9 %collective-permute-start.3 = (bf16[30,16,256]{2,1,0:T(8,128)(2,1)S(1)}, bf16[30,16,256]{2,1,0:T(8,128)(2,1)S(1)}, u32[]{:S(2)}, u32[]{:S(2)}) collective-permute-start(bf16[30,16,256]{2,1,0:T(8,128)(2,1)S(1)} %get-tuple-element.32), channel_id=1, source_target_pairs={{8,16},{24,32},{40,48},{56,64},{72,80},{88,96},{104,112},{120,128}... | collective-permute-start | bytes 737288 | tf_op jit(solution)/shard_map/ppermute | solution.py:426
  23.6 0.0 copy-done
  23.6 0.4 shard_map.70.weight
  24.0 0.0 all-to-all-done
  24.0 0.0 collective-permute-done.2.near
  24.0 5.2 %collective-permute-done.3.far = bf16[30,16,256]{2,1,0:T(8,128)(2,1)S(1)} collective-permute-done((bf16[30,16,256]{2,1,0:T(8,128)(2,1)S(1)}, bf16[30,16,256]{2,1,0:T(8,128)(2,1)S(1)}, u32[]{:S(2)}, u32[]{:S(2)}) %collective-permute-start.3) | collective-permute-done | bytes 245792 | tf_op jit(solution)/shard_map/ppermute | solution.py:426
  29.2 2.5 %shard_map.71 = (bf16[14,32,128]{2,1,0:T(8,128)(2,1)S(1)}, f32[10,256,128]{2,1,0:T(8,128)S(1)}, bf16[30,256,128]{2,1,0:T(8,128)(2,1)S(1)}) custom-call(bf16[16,2,16,256]{3,2,1,0:T(8,128)(2,1)S(1)} %bitcast.19, bf16[30,16,256]{2,1,0:T(8,128)(2,1)S(1)} %collective-permute-done.2.near, bf16[30,16,256]{2,1,0:T(8,128)(2,1)S(1)} %collective-permute-done.3.far, ...), custom_call_target="tpu_custom_call" | custom-call | flops 939524096 | bytes 4898816 | tf_op jit(solution)/shard_map/pallas_call | solution.py:32
  31.8 1.9 %collective-permute-start.5 = (bf16[14,32,128]{2,1,0:T(8,128)(2,1)S(1)}, bf16[14,32,128]{2,1,0:T(8,128)(2,1)S(1)}, u32[]{:S(2)}, u32[]{:S(2)}) collective-permute-start(bf16[14,32,128]{2,1,0:T(8,128)(2,1)S(1)} %get-tuple-element.35.own), channel_id=1, source_target_pairs={{8,16},{24,32},{40,48},{56,64},{72,80},{88,96},{104,112},{120,128}... | collective-permute-start | bytes 344072 | tf_op jit(solution)/shard_map/ppermute | solution.py:426
  33.7 1.9 %collective-permute-start.4 = (bf16[14,32,128]{2,1,0:T(8,128)(2,1)S(1)}, bf16[14,32,128]{2,1,0:T(8,128)(2,1)S(1)}, u32[]{:S(2)}, u32[]{:S(2)}) collective-permute-start(bf16[14,32,128]{2,1,0:T(8,128)(2,1)S(1)} %get-tuple-element.35.own), channel_id=1, source_target_pairs={{0,8},{8,0},{16,24},{24,16},{32,40},{40,32},{48,56},{56,48},{64,72... | collective-permute-start | bytes 344072 | tf_op jit(solution)/shard_map/ppermute | solution.py:425
  35.6 2.3 %collective-permute-done.5.far = bf16[14,32,128]{2,1,0:T(8,128)(2,1)S(1)} collective-permute-done((bf16[14,32,128]{2,1,0:T(8,128)(2,1)S(1)}, bf16[14,32,128]{2,1,0:T(8,128)(2,1)S(1)}, u32[]{:S(2)}, u32[]{:S(2)}) %collective-permute-start.5) | collective-permute-done | bytes 114720 | tf_op jit(solution)/shard_map/ppermute | solution.py:426
  37.9 0.0 collective-permute-done.4.near
  37.9 1.3 %shard_map.72 = (bf16[12,64,128]{2,1,0:T(8,128)(2,1)S(1)}, bf16[14,288,128]{2,1,0:T(8,128)(2,1)S(1)}, bf16[10,32,128]{2,1,0:T(8,128)(2,1)S(1)}, f32[10,32,128]{2,1,0:T(8,128)S(1)}, bf16[10,32,128]{2,1,0:T(8,128)(2,1)S(1)}) custom-call(bf16[14,32,128]{2,1,0:T(8,128)(2,1)S(1)} %collective-permute-done.4.near, bf16[14,32,128]{2,1,0:T(8,128)(2,1)S(1)} %get-tuple-element.35.own, ...), custom_call_target="tpu_custom_call" | custom-call | flops 339738624 | bytes 2211840 | tf_op jit(solution)/shard_map/pallas_call | solution.py:32
  39.2 1.9 %collective-permute-start.6 = (bf16[10,32,128]{2,1,0:T(8,128)(2,1)S(1)}, bf16[10,32,128]{2,1,0:T(8,128)(2,1)S(1)}, u32[]{:S(2)}, u32[]{:S(2)}) collective-permute-start(bf16[10,32,128]{2,1,0:T(8,128)(2,1)S(1)} %get-tuple-element.37), channel_id=1, source_target_pairs={{0,8},{8,0},{16,24},{24,16},{32,40},{40,32},{48,56},{56,48},{64,72... | collective-permute-start | bytes 245768 | tf_op jit(solution)/shard_map/ppermute | solution.py:425
  41.1 2.8 %collective-permute-start.7 = (bf16[10,32,128]{2,1,0:T(8,128)(2,1)S(1)}, bf16[10,32,128]{2,1,0:T(8,128)(2,1)S(1)}, u32[]{:S(2)}, u32[]{:S(2)}) collective-permute-start(bf16[10,32,128]{2,1,0:T(8,128)(2,1)S(1)} %get-tuple-element.39), channel_id=1, source_target_pairs={{8,16},{24,32},{40,48},{56,64},{72,80},{88,96},{104,112},{120,128}... | collective-permute-start | bytes 245768 | tf_op jit(solution)/shard_map/ppermute | solution.py:426
  43.9 0.6 shard_map.73.three
  44.6 0.0 collective-permute-done.6.near
  44.6 2.3 %collective-permute-done.7.far = bf16[10,32,128]{2,1,0:T(8,128)(2,1)S(1)} collective-permute-done((bf16[10,32,128]{2,1,0:T(8,128)(2,1)S(1)}, bf16[10,32,128]{2,1,0:T(8,128)(2,1)S(1)}, u32[]{:S(2)}, u32[]{:S(2)}) %collective-permute-start.7) | collective-permute-done | bytes 81952 | tf_op jit(solution)/shard_map/ppermute | solution.py:426
  46.9 0.9 shard_map.74
  47.9 0.1 copy.23
  48.0 25.8 %all_to_all.20 = bf16[32,9,2,128]{3,2,1,0:T(2,128)(2,1)S(1)} all-to-all(bf16[32,9,2,128]{3,2,1,0:T(2,128)(2,1)S(1)} %copy.23), channel_id=1, replica_groups=mesh['yl'=2,'z'=16,'core'=2,'yh'=2,'x'=4] {'yl','core','yh','x'}, dimensions={0} | all-to-all | bytes 294912 | tf_op jit(solution)/shard_map/all_to_all | solution.py:431
  73.8 0.1 reduce_sum.24
  74.0 0.7 broadcast_in_dim.4
  74.7 5.6 %all-to-all-start.2 = ((bf16[16,9,2,128]{3,2,1,0:T(2,128)(2,1)}), bf16[16,9,2,128]{3,2,1,0:T(2,128)(2,1)S(1)}, u32[]{:S(2)}, u32[]{:S(2)}) async-start(bf16[16,9,2,128]{3,2,1,0:T(2,128)(2,1)} %broadcast_in_dim.4), calls=%async_computation.2 | async-start | bytes 147456 | tf_op jit(solution)/shard_map/all_to_all | solution.py:431
  80.2 4.4 %collective-permute-start.8 = (bf16[10,128,128]{2,1,0:T(8,128)(2,1)S(1)}, bf16[10,128,128]{2,1,0:T(8,128)(2,1)S(1)}, u32[]{:S(2)}, u32[]{:S(2)}) collective-permute-start(bf16[10,128,128]{2,1,0:T(8,128)(2,1)S(1)} %get-tuple-element.44.high), channel_id=1, source_target_pairs={{0,8},{8,16},{16,24},{24,32},{32,40},{40,48},{48,56},{56,64},{64,7... | collective-permute-start | bytes 983048 | tf_op jit(solution)/shard_map/ppermute | solution.py:415
  84.7 1.9 %collective-permute-start.9 = (bf16[10,128,128]{2,1,0:T(8,128)(2,1)S(1)}, bf16[10,128,128]{2,1,0:T(8,128)(2,1)S(1)}, u32[]{:S(2)}, u32[]{:S(2)}) collective-permute-start(bf16[10,128,128]{2,1,0:T(8,128)(2,1)S(1)} %get-tuple-element.45.low), channel_id=1, source_target_pairs={{8,0},{16,8},{24,16},{32,24},{40,32},{48,40},{56,48},{64,56},{72,6... | collective-permute-start | bytes 983048 | tf_op jit(solution)/shard_map/ppermute | solution.py:416
  86.6 5.3 %all-to-all-done.2 = bf16[16,9,2,128]{3,2,1,0:T(2,128)(2,1)S(1)} async-done(((bf16[16,9,2,128]{3,2,1,0:T(2,128)(2,1)}), bf16[16,9,2,128]{3,2,1,0:T(2,128)(2,1)S(1)}, u32[]{:S(2)}, u32[]{:S(2)}) %all-to-all-start.2) | async-done | bytes 73760 | tf_op jit(solution)/shard_map/all_to_all | solution.py:431
  92.0 0.1 reduce_sum.25
  92.0 0.7 broadcast_in_dim.5
  92.8 5.8 %all-to-all-start.3 = ((bf16[32,9,2,128]{3,2,1,0:T(2,128)(2,1)}), bf16[32,9,2,128]{3,2,1,0:T(2,128)(2,1)S(1)}, u32[]{:S(2)}, u32[]{:S(2)}) async-start(bf16[32,9,2,128]{3,2,1,0:T(2,128)(2,1)} %broadcast_in_dim.5), calls=%async_computation.3 | async-start | bytes 294912 | tf_op jit(solution)/shard_map/all_to_all | solution.py:431
  98.6 0.0 collective-permute-done.8.below
  98.6 0.0 collective-permute-done.9.above
  98.6 2.6 %shard_map.75 = bf16[8,64,256]{2,1,0:T(8,128)(2,1)S(1)} custom-call(bf16[10,128,128]{2,1,0:T(8,128)(2,1)S(1)} %collective-permute-done.8.below, bf16[10,128,128]{2,1,0:T(8,128)(2,1)S(1)} %get-tuple-element.45.low, bf16[10,128,128]{2,1,0:T(8,128)(2,1)S(1)} %get-tuple-element.44.high, bf16[10,128,128]{2,1,0:T(8,128)(2,1)S(1)} %collective-permute-done.9.above, ...), custom_call_target="tpu_custom_call" | custom-call | flops 536870912 | bytes 1600512 | tf_op jit(solution)/shard_map/pallas_call | solution.py:32
  101.2 0.2 copy.21
  101.4 0.8 reshape.36
  102.2 4.2 %all-to-all-done.3.lines = bf16[32,9,2,128]{3,2,1,0:T(2,128)(2,1)S(1)} async-done(((bf16[32,9,2,128]{3,2,1,0:T(2,128)(2,1)}), bf16[32,9,2,128]{3,2,1,0:T(2,128)(2,1)S(1)}, u32[]{:S(2)}, u32[]{:S(2)}) %all-to-all-start.3) | async-done | bytes 147488 | tf_op jit(solution)/shard_map/all_to_all | solution.py:431
  106.5 0.9 shard_map.76
  (4 shorter events, 0.1 us)
Async XLA Ops:
  0.6 23.0 %copy-start = (bf16[3,3,3,32,16]{3,4,2,1,0:T(8,128)(2,1)S(1)}, bf16[3,3,3,32,16]{3,4,2,1,0:T(8,128)(2,1)}, u32[]{:S(2)}) copy-start(bf16[3,3,3,32,16]{3,4,2,1,0:T(8,128)(2,1)} %param.5) | copy-start | bytes 82948
  1.8 6.4 %collective-permute-start = (bf16[7,2,16,256]{3,2,1,0:T(8,128)(2,1)S(1)}, bf16[7,2,16,256]{3,2,1,0:T(8,128)(2,1)S(1)}, u32[]{:S(2)}, u32[]{:S(2)}) collective-permute-start(bf16[7,2,16,256]{3,2,1,0:T(8,128)(2,1)S(1)} %get-tuple-element.28), channel_id=1, source_target_pairs={{0,1},{1,0},{2,3},{3,2},{4,5},{5,4},{6,7},{7,6},{8,9},{9,8},{10,11... | collective-permute-start | bytes 344072 | tf_op jit(solution)/shard_map/ppermute | solution.py:425
  5.8 10.3 %collective-permute-start.1 = (bf16[7,2,16,256]{3,2,1,0:T(8,128)(2,1)S(1)}, bf16[7,2,16,256]{3,2,1,0:T(8,128)(2,1)S(1)}, u32[]{:S(2)}, u32[]{:S(2)}) collective-permute-start(bf16[7,2,16,256]{3,2,1,0:T(8,128)(2,1)S(1)} %get-tuple-element.30), channel_id=1, source_target_pairs={{1,2},{3,4},{5,6},{2,1},{4,3},{6,5},{9,10},{11,12},{13,14},{10,9},... | collective-permute-start | bytes 344072 | tf_op jit(solution)/shard_map/ppermute | solution.py:426
  8.3 15.7 %all-to-all-start = ((bf16[8,8,2432]{2,1,0:T(8,128)(2,1)}), bf16[8,8,2432]{2,1,0:T(8,128)(2,1)S(1)}, u32[]{:S(2)}, u32[]{:S(2)}) async-start(bf16[8,8,2432]{2,1,0:T(8,128)(2,1)} %shard_map.67), calls=%async_computation | async-start | bytes 622592 | tf_op jit(solution)/shard_map/all_to_all | solution.py:431
  16.2 7.9 %collective-permute-start.2 = (bf16[30,16,256]{2,1,0:T(8,128)(2,1)S(1)}, bf16[30,16,256]{2,1,0:T(8,128)(2,1)S(1)}, u32[]{:S(2)}, u32[]{:S(2)}) collective-permute-start(bf16[30,16,256]{2,1,0:T(8,128)(2,1)S(1)} %get-tuple-element.31), channel_id=1, source_target_pairs={{0,8},{8,0},{16,24},{24,16},{32,40},{40,32},{48,56},{56,48},{64,72... | collective-permute-start | bytes 737288 | tf_op jit(solution)/shard_map/ppermute | solution.py:425
  21.7 7.5 %collective-permute-start.3 = (bf16[30,16,256]{2,1,0:T(8,128)(2,1)S(1)}, bf16[30,16,256]{2,1,0:T(8,128)(2,1)S(1)}, u32[]{:S(2)}, u32[]{:S(2)}) collective-permute-start(bf16[30,16,256]{2,1,0:T(8,128)(2,1)S(1)} %get-tuple-element.32), channel_id=1, source_target_pairs={{8,16},{24,32},{40,48},{56,64},{72,80},{88,96},{104,112},{120,128}... | collective-permute-start | bytes 737288 | tf_op jit(solution)/shard_map/ppermute | solution.py:426
  31.8 6.1 %collective-permute-start.5 = (bf16[14,32,128]{2,1,0:T(8,128)(2,1)S(1)}, bf16[14,32,128]{2,1,0:T(8,128)(2,1)S(1)}, u32[]{:S(2)}, u32[]{:S(2)}) collective-permute-start(bf16[14,32,128]{2,1,0:T(8,128)(2,1)S(1)} %get-tuple-element.35.own), channel_id=1, source_target_pairs={{8,16},{24,32},{40,48},{56,64},{72,80},{88,96},{104,112},{120,128}... | collective-permute-start | bytes 344072 | tf_op jit(solution)/shard_map/ppermute | solution.py:426
  33.7 4.2 %collective-permute-start.4 = (bf16[14,32,128]{2,1,0:T(8,128)(2,1)S(1)}, bf16[14,32,128]{2,1,0:T(8,128)(2,1)S(1)}, u32[]{:S(2)}, u32[]{:S(2)}) collective-permute-start(bf16[14,32,128]{2,1,0:T(8,128)(2,1)S(1)} %get-tuple-element.35.own), channel_id=1, source_target_pairs={{0,8},{8,0},{16,24},{24,16},{32,40},{40,32},{48,56},{56,48},{64,72... | collective-permute-start | bytes 344072 | tf_op jit(solution)/shard_map/ppermute | solution.py:425
  39.2 5.4 %collective-permute-start.6 = (bf16[10,32,128]{2,1,0:T(8,128)(2,1)S(1)}, bf16[10,32,128]{2,1,0:T(8,128)(2,1)S(1)}, u32[]{:S(2)}, u32[]{:S(2)}) collective-permute-start(bf16[10,32,128]{2,1,0:T(8,128)(2,1)S(1)} %get-tuple-element.37), channel_id=1, source_target_pairs={{0,8},{8,0},{16,24},{24,16},{32,40},{40,32},{48,56},{56,48},{64,72... | collective-permute-start | bytes 245768 | tf_op jit(solution)/shard_map/ppermute | solution.py:425
  41.1 5.8 %collective-permute-start.7 = (bf16[10,32,128]{2,1,0:T(8,128)(2,1)S(1)}, bf16[10,32,128]{2,1,0:T(8,128)(2,1)S(1)}, u32[]{:S(2)}, u32[]{:S(2)}) collective-permute-start(bf16[10,32,128]{2,1,0:T(8,128)(2,1)S(1)} %get-tuple-element.39), channel_id=1, source_target_pairs={{8,16},{24,32},{40,48},{56,64},{72,80},{88,96},{104,112},{120,128}... | collective-permute-start | bytes 245768 | tf_op jit(solution)/shard_map/ppermute | solution.py:426
  74.7 17.3 %all-to-all-start.2 = ((bf16[16,9,2,128]{3,2,1,0:T(2,128)(2,1)}), bf16[16,9,2,128]{3,2,1,0:T(2,128)(2,1)S(1)}, u32[]{:S(2)}, u32[]{:S(2)}) async-start(bf16[16,9,2,128]{3,2,1,0:T(2,128)(2,1)} %broadcast_in_dim.4), calls=%async_computation.2 | async-start | bytes 147456 | tf_op jit(solution)/shard_map/all_to_all | solution.py:431
  80.2 18.3 %collective-permute-start.8 = (bf16[10,128,128]{2,1,0:T(8,128)(2,1)S(1)}, bf16[10,128,128]{2,1,0:T(8,128)(2,1)S(1)}, u32[]{:S(2)}, u32[]{:S(2)}) collective-permute-start(bf16[10,128,128]{2,1,0:T(8,128)(2,1)S(1)} %get-tuple-element.44.high), channel_id=1, source_target_pairs={{0,8},{8,16},{16,24},{24,32},{32,40},{40,48},{48,56},{56,64},{64,7... | collective-permute-start | bytes 983048 | tf_op jit(solution)/shard_map/ppermute | solution.py:415
  84.7 13.9 %collective-permute-start.9 = (bf16[10,128,128]{2,1,0:T(8,128)(2,1)S(1)}, bf16[10,128,128]{2,1,0:T(8,128)(2,1)S(1)}, u32[]{:S(2)}, u32[]{:S(2)}) collective-permute-start(bf16[10,128,128]{2,1,0:T(8,128)(2,1)S(1)} %get-tuple-element.45.low), channel_id=1, source_target_pairs={{8,0},{16,8},{24,16},{32,24},{40,32},{48,40},{56,48},{64,56},{72,6... | collective-permute-start | bytes 983048 | tf_op jit(solution)/shard_map/ppermute | solution.py:416
  92.8 13.7 %all-to-all-start.3 = ((bf16[32,9,2,128]{3,2,1,0:T(2,128)(2,1)}), bf16[32,9,2,128]{3,2,1,0:T(2,128)(2,1)S(1)}, u32[]{:S(2)}, u32[]{:S(2)}) async-start(bf16[32,9,2,128]{3,2,1,0:T(2,128)(2,1)} %broadcast_in_dim.5), calls=%async_computation.3 | async-start | bytes 294912 | tf_op jit(solution)/shard_map/all_to_all | solution.py:431

commit v8 on v7

--- a/solution.py
+++ b/solution.py
@@ -123,7 +123,7 @@
         far[row] = own[row + rest * odd]
 
 
-def edges(own, near_rows, far_rows, near, far):
+def edges(own, near_rows, far_rows, far, near):
     core = lax.axis_index("core")
     top, bottom = in_order(near_rows, far_rows, "x")
     count, height = near_rows.shape[0], own.shape[0]
@@ -149,7 +149,7 @@
     return below, above
 
 
-def forward_two(own, near, far, near_rows, far_rows, weight, pooled, slope, parts, split):
+def forward_two(own, far, near, near_rows, far_rows, weight, pooled, slope, parts, split):
     split[...] = splitter()
     first = pooled.shape[0] - 6
     first = first * group_index() - 3
@@ -250,7 +250,7 @@
             out[to, :, lane : lane + BREADTH] = blocks[part]
 
 
-def middle_three(near, own, far, arrived, grads, parts, to_near, same, to_far, shift, around, turned):
+def middle_three(near, own, far, arrived, grads, parts, to_far, same, to_near, shift, around, turned):
     shift[...] = shifter()
     below, above = in_order(near, far)
     place_shifted((below, own.__getitem__, above), own.shape[0], parts, shift, 32)
@@ -421,10 +421,9 @@
     count = axis_count(names)
     across = [(i, i + 1) for i in range(1, count - 1, 2)]
     across += [(i + 1, i) for i in range(1, count - 1, 2)]
-    return (
-        lax.ppermute(near, names, [(i, i ^ 1) for i in range(count)]),
-        lax.ppermute(far, names, across),
-    )
+    far = lax.ppermute(far, names, across)
+    near = lax.ppermute(near, names, [(i, i ^ 1) for i in range(count)])
+    return near, far
 
 
 def exchange(blocks, axis):
@@ -470,7 +469,8 @@
     arrived = exchange(packed, GROUP).reshape(filters, -1)
 
     plane = jax.ShapeDtypeStruct((height + 14, chans, breadth), BF16)
-    near, far = paired(*call(edges, [plane, plane], [], (own, near_rows, far_rows), 1024 * 1024))
+    far, near = call(edges, [plane, plane], [], (own, near_rows, far_rows), 1024 * 1024)
+    near, far = paired(near, far)
 
     turned = jnp.transpose(weight_two.reshape(27, 32, 16), (0, 2, 1))
     (ahead,) = call(
@@ -490,14 +490,14 @@
             jax.ShapeDtypeStruct((height + 14, 256, BREADTH), BF16),
         ],
         [pltpu.VMEM((2 * BREADTH, 4 * BREADTH), BF16)],
-        (own, near, far, near_rows, far_rows, ahead),
+        (own, far, near, near_rows, far_rows, ahead),
         2 * 14 * 256 * 1024 * 128,
     )
 
     pool_near, pool_far = paired(pooled, pooled)
     shift = pltpu.VMEM((BREADTH, 2 * BREADTH), BF16)
     terms = jax.ShapeDtypeStruct((pool_rows + 2, 32, BREADTH), BF16)
-    grads, parts_three, to_near, same, to_far = call(
+    grads, parts_three, to_far, same, to_near = call(
         middle_three,
         [
             jax.ShapeDtypeStruct((pool_rows + 4, filters, BREADTH), BF16),
@@ -528,7 +528,7 @@
         middle_two,
         [plane, plane, jax.ShapeDtypeStruct((32, 18, BREADTH), F32)],
         [],
-        (terms_near, same, terms_far, slope, parts_two, local_three),
+        (terms_far, same, terms_near, slope, parts_two, local_three),
         2 * 8 * 256 * 1024 * 128,
     )
 

time: 108 us -> 104 us (0.963)
  waiting for transfers between devices: 19.3 us -> 13.3 us
  starting transfers between devices: 46.2 us -> 50.9 us
  blocking collectives: 25.8 us -> 23.3 us
    ppermute x8, waiting for transfers between devices: 9.73 us -> 3.15 us  [the longest x4 1.81 us: paired(): far = lax.ppermute(far, names, across)]
    ppermute x8, starting transfers between devices: 20.6 us -> 23.7 us  [the longest x4 14 us: paired(): far = lax.ppermute(far, names, across)]
    all_to_all x1, blocking collectives: 25.8 us -> 23.3 us  [exchange(): return lax.all_to_all(blocks, axis, 0, 0, tiled=True)]
    all_to_all x3, starting transfers between devices: 19.2 us -> 20.8 us  [exchange(): return lax.all_to_all(blocks, axis, 0, 0, tiled=True)]
  transfers between devices with their start and end apart: 13 -> 13, of which waited for: 5 -> 7; matrix products, arithmetic and copies ran while one was open for 2% -> 2% of each run, Pallas kernels for 5% -> 5%
where the time goes in v8:
time: 104 us; the launch traced here: 103 us
  starting transfers between devices  50.9 us (49%)
  blocking collectives  23.3 us (22%)
  waiting for transfers between devices  13.3 us (13%)
  Pallas kernels  11.1 us (11%)
  local copies, waits for them, and re-layouts  3.75 us (4%)
    all_to_all x1, blocking collectives, exchange(): return lax.all_to_all(blocks, axis, 0, 0, tiled=True)  23.3 us
    all_to_all x3, starting transfers between devices, exchange(): return lax.all_to_all(blocks, axis, 0, 0, tiled=True)  20.8 us
    ppermute x4, starting transfers between devices, paired(): far = lax.ppermute(far, names, across)  14 us
    pallas_call x10, Pallas kernels, call(): pl.pallas_call(kernel, out_shape=outs, in_specs=specs, out_specs=[pl.Bloc...  11.1 us
    all_to_all x3, waiting for transfers between devices, exchange(): return lax.all_to_all(blocks, axis, 0, 0, tiled=True)  10.1 us
    ppermute x4, starting transfers between devices, paired(): near = lax.ppermute(near, names, [(i, i ^ 1) for i in range(count)])  9.71 us
    ppermute x1, starting transfers between devices, neighbours(): lax.ppermute(last, axis, shifted(axis, 1))  4.44 us
  transfers between devices with their start and end apart: 13, of which 7 were waited for; matrix products, arithmetic and copies ran while one was open for 2% of the time, Pallas kernels for 5%

profile of v8, /device:TPU:1, one launch (start us, length us, event | category | flops | bytes accessed | tf_op | source)
XLA Modules:
  0.0 103.5 jit_solution(4953735408794885537)
XLA Ops:
  0.6 0.0 copy-start
  0.6 1.1 %copy.27 = bf16[16,2,16,256]{3,0,1,2:T(8,128)(2,1)S(1)} copy(bf16[16,2,16,256]{3,2,1,0:T(8,128)(2,1)} %param.4) | data formatting | bytes 524288 | tf_op args[0]
  1.8 3.9 %collective-permute-start = (bf16[7,2,16,256]{3,2,1,0:T(8,128)(2,1)S(1)}, bf16[7,2,16,256]{3,2,1,0:T(8,128)(2,1)S(1)}, u32[]{:S(2)}, u32[]{:S(2)}) collective-permute-start(bf16[7,2,16,256]{3,2,1,0:T(8,128)(2,1)S(1)} %get-tuple-element.28), channel_id=1, source_target_pairs={{0,1},{1,0},{2,3},{3,2},{4,5},{5,4},{6,7},{7,6},{8,9},{9,8},{10,11... | collective-permute-start | bytes 344072 | tf_op jit(solution)/shard_map/ppermute | solution.py:425
  5.8 0.7 collective-permute-start.1
  6.4 1.8 %shard_map.67 = bf16[8,8,2432]{2,1,0:T(8,128)(2,1)} custom-call(bf16[27,8,32]{2,1,0:T(8,128)(2,1)} %bitcast.26, bf16[8,64,128]{2,1,0:T(8,128)(2,1)} %bitcast.25), custom_call_target="tpu_custom_call" | custom-call | flops 131072 | bytes 456192 | tf_op jit(solution)/shard_map/pallas_call | solution.py:32
  8.2 0.0 collective-permute-done.near_rows
  8.3 7.8 %all-to-all-start = ((bf16[8,8,2432]{2,1,0:T(8,128)(2,1)}), bf16[8,8,2432]{2,1,0:T(8,128)(2,1)S(1)}, u32[]{:S(2)}, u32[]{:S(2)}) async-start(bf16[8,8,2432]{2,1,0:T(8,128)(2,1)} %shard_map.67), calls=%async_computation | async-start | bytes 622592 | tf_op jit(solution)/shard_map/all_to_all | solution.py:430
  16.1 0.0 collective-permute-done.1.far_rows
  16.2 4.9 %collective-permute-start.2 = (bf16[30,16,256]{2,1,0:T(8,128)(2,1)S(1)}, bf16[30,16,256]{2,1,0:T(8,128)(2,1)S(1)}, u32[]{:S(2)}, u32[]{:S(2)}) collective-permute-start(bf16[30,16,256]{2,1,0:T(8,128)(2,1)S(1)} %get-tuple-element.31), channel_id=1, source_target_pairs={{8,16},{24,32},{40,48},{56,64},{72,80},{88,96},{104,112},{120,128}... | collective-permute-start | bytes 737288 | tf_op jit(solution)/shard_map/ppermute | solution.py:424
  21.1 1.9 %collective-permute-start.3 = (bf16[30,16,256]{2,1,0:T(8,128)(2,1)S(1)}, bf16[30,16,256]{2,1,0:T(8,128)(2,1)S(1)}, u32[]{:S(2)}, u32[]{:S(2)}) collective-permute-start(bf16[30,16,256]{2,1,0:T(8,128)(2,1)S(1)} %get-tuple-element.32), channel_id=1, source_target_pairs={{0,8},{8,0},{16,24},{24,16},{32,40},{40,32},{48,56},{56,48},{64,72... | collective-permute-start | bytes 737288 | tf_op jit(solution)/shard_map/ppermute | solution.py:425
  23.0 0.0 copy-done
  23.0 0.4 shard_map.70.weight
  23.4 0.6 all-to-all-done
  24.0 1.3 %collective-permute-done.2.far = bf16[30,16,256]{2,1,0:T(8,128)(2,1)S(1)} collective-permute-done((bf16[30,16,256]{2,1,0:T(8,128)(2,1)S(1)}, bf16[30,16,256]{2,1,0:T(8,128)(2,1)S(1)}, u32[]{:S(2)}, u32[]{:S(2)}) %collective-permute-start.2) | collective-permute-done | bytes 245792 | tf_op jit(solution)/shard_map/ppermute | solution.py:424
  25.3 0.0 collective-permute-done.3.near
  25.3 2.5 %shard_map.71 = (bf16[14,32,128]{2,1,0:T(8,128)(2,1)S(1)}, f32[10,256,128]{2,1,0:T(8,128)S(1)}, bf16[30,256,128]{2,1,0:T(8,128)(2,1)S(1)}) custom-call(bf16[16,2,16,256]{3,2,1,0:T(8,128)(2,1)S(1)} %bitcast.19, bf16[30,16,256]{2,1,0:T(8,128)(2,1)S(1)} %collective-permute-done.2.far, bf16[30,16,256]{2,1,0:T(8,128)(2,1)S(1)} %collective-permute-done.3.near, ...), custom_call_target="tpu_custom_call" | custom-call | flops 939524096 | bytes 4898816 | tf_op jit(solution)/shard_map/pallas_call | solution.py:32
  27.8 4.8 %collective-permute-start.5 = (bf16[14,32,128]{2,1,0:T(8,128)(2,1)S(1)}, bf16[14,32,128]{2,1,0:T(8,128)(2,1)S(1)}, u32[]{:S(2)}, u32[]{:S(2)}) collective-permute-start(bf16[14,32,128]{2,1,0:T(8,128)(2,1)S(1)} %get-tuple-element.35.own), channel_id=1, source_target_pairs={{8,16},{24,32},{40,48},{56,64},{72,80},{88,96},{104,112},{120,128}... | collective-permute-start | bytes 344072 | tf_op jit(solution)/shard_map/ppermute | solution.py:424
  32.6 1.9 %collective-permute-start.4 = (bf16[14,32,128]{2,1,0:T(8,128)(2,1)S(1)}, bf16[14,32,128]{2,1,0:T(8,128)(2,1)S(1)}, u32[]{:S(2)}, u32[]{:S(2)}) collective-permute-start(bf16[14,32,128]{2,1,0:T(8,128)(2,1)S(1)} %get-tuple-element.35.own), channel_id=1, source_target_pairs={{0,8},{8,0},{16,24},{24,16},{32,40},{40,32},{48,56},{56,48},{64,72... | collective-permute-start | bytes 344072 | tf_op jit(solution)/shard_map/ppermute | solution.py:425
  34.6 0.5 collective-permute-done.5.far
  35.1 0.8 collective-permute-done.4.near
  35.9 1.3 %shard_map.72 = (bf16[12,64,128]{2,1,0:T(8,128)(2,1)S(1)}, bf16[14,288,128]{2,1,0:T(8,128)(2,1)S(1)}, bf16[10,32,128]{2,1,0:T(8,128)(2,1)S(1)}, f32[10,32,128]{2,1,0:T(8,128)S(1)}, bf16[10,32,128]{2,1,0:T(8,128)(2,1)S(1)}) custom-call(bf16[14,32,128]{2,1,0:T(8,128)(2,1)S(1)} %collective-permute-done.4.near, bf16[14,32,128]{2,1,0:T(8,128)(2,1)S(1)} %get-tuple-element.35.own, ...), custom_call_target="tpu_custom_call" | custom-call | flops 339738624 | bytes 2211840 | tf_op jit(solution)/shard_map/pallas_call | solution.py:32
  37.2 3.6 %collective-permute-start.6 = (bf16[10,32,128]{2,1,0:T(8,128)(2,1)S(1)}, bf16[10,32,128]{2,1,0:T(8,128)(2,1)S(1)}, u32[]{:S(2)}, u32[]{:S(2)}) collective-permute-start(bf16[10,32,128]{2,1,0:T(8,128)(2,1)S(1)} %get-tuple-element.37), channel_id=1, source_target_pairs={{8,16},{24,32},{40,48},{56,64},{72,80},{88,96},{104,112},{120,128}... | collective-permute-start | bytes 245768 | tf_op jit(solution)/shard_map/ppermute | solution.py:424
  40.8 1.9 %collective-permute-start.7 = (bf16[10,32,128]{2,1,0:T(8,128)(2,1)S(1)}, bf16[10,32,128]{2,1,0:T(8,128)(2,1)S(1)}, u32[]{:S(2)}, u32[]{:S(2)}) collective-permute-start(bf16[10,32,128]{2,1,0:T(8,128)(2,1)S(1)} %get-tuple-element.39), channel_id=1, source_target_pairs={{0,8},{8,0},{16,24},{24,16},{32,40},{40,32},{48,56},{56,48},{64,72... | collective-permute-start | bytes 245768 | tf_op jit(solution)/shard_map/ppermute | solution.py:425
  42.7 0.6 shard_map.73.three
  43.4 0.0 collective-permute-done.6.near
  43.4 0.6 collective-permute-done.7.far
  44.0 0.9 shard_map.74
  45.0 0.1 copy.23
  45.1 23.3 %all_to_all.20 = bf16[32,9,2,128]{3,2,1,0:T(2,128)(2,1)S(1)} all-to-all(bf16[32,9,2,128]{3,2,1,0:T(2,128)(2,1)S(1)} %copy.23), channel_id=1, replica_groups=mesh['yl'=2,'z'=16,'core'=2,'yh'=2,'x'=4] {'yl','core','yh','x'}, dimensions={0} | all-to-all | bytes 294912 | tf_op jit(solution)/shard_map/all_to_all | solution.py:430
  68.4 0.1 reduce_sum.24
  68.5 0.7 broadcast_in_dim.4
  69.2 7.2 %all-to-all-start.2 = ((bf16[16,9,2,128]{3,2,1,0:T(2,128)(2,1)}), bf16[16,9,2,128]{3,2,1,0:T(2,128)(2,1)S(1)}, u32[]{:S(2)}, u32[]{:S(2)}) async-start(bf16[16,9,2,128]{3,2,1,0:T(2,128)(2,1)} %broadcast_in_dim.4), calls=%async_computation.2 | async-start | bytes 147456 | tf_op jit(solution)/shard_map/all_to_all | solution.py:430
  76.4 4.4 %collective-permute-start.8 = (bf16[10,128,128]{2,1,0:T(8,128)(2,1)S(1)}, bf16[10,128,128]{2,1,0:T(8,128)(2,1)S(1)}, u32[]{:S(2)}, u32[]{:S(2)}) collective-permute-start(bf16[10,128,128]{2,1,0:T(8,128)(2,1)S(1)} %get-tuple-element.44.high), channel_id=1, source_target_pairs={{0,8},{8,16},{16,24},{24,32},{32,40},{40,48},{48,56},{56,64},{64,7... | collective-permute-start | bytes 983048 | tf_op jit(solution)/shard_map/ppermute | solution.py:415
  80.8 1.9 %collective-permute-start.9 = (bf16[10,128,128]{2,1,0:T(8,128)(2,1)S(1)}, bf16[10,128,128]{2,1,0:T(8,128)(2,1)S(1)}, u32[]{:S(2)}, u32[]{:S(2)}) collective-permute-start(bf16[10,128,128]{2,1,0:T(8,128)(2,1)S(1)} %get-tuple-element.45.low), channel_id=1, source_target_pairs={{8,0},{16,8},{24,16},{32,24},{40,32},{48,40},{56,48},{64,56},{72,6... | collective-permute-start | bytes 983048 | tf_op jit(solution)/shard_map/ppermute | solution.py:416
  82.8 5.3 %all-to-all-done.2 = bf16[16,9,2,128]{3,2,1,0:T(2,128)(2,1)S(1)} async-done(((bf16[16,9,2,128]{3,2,1,0:T(2,128)(2,1)}), bf16[16,9,2,128]{3,2,1,0:T(2,128)(2,1)S(1)}, u32[]{:S(2)}, u32[]{:S(2)}) %all-to-all-start.2) | async-done | bytes 73760 | tf_op jit(solution)/shard_map/all_to_all | solution.py:430
  88.1 0.1 reduce_sum.25
  88.2 0.7 broadcast_in_dim.5
  88.9 5.8 %all-to-all-start.3 = ((bf16[32,9,2,128]{3,2,1,0:T(2,128)(2,1)}), bf16[32,9,2,128]{3,2,1,0:T(2,128)(2,1)S(1)}, u32[]{:S(2)}, u32[]{:S(2)}) async-start(bf16[32,9,2,128]{3,2,1,0:T(2,128)(2,1)} %broadcast_in_dim.5), calls=%async_computation.3 | async-start | bytes 294912 | tf_op jit(solution)/shard_map/all_to_all | solution.py:430
  94.7 0.0 collective-permute-done.8.below
  94.7 0.0 collective-permute-done.9.above
  94.8 2.6 %shard_map.75 = bf16[8,64,256]{2,1,0:T(8,128)(2,1)S(1)} custom-call(bf16[10,128,128]{2,1,0:T(8,128)(2,1)S(1)} %collective-permute-done.8.below, bf16[10,128,128]{2,1,0:T(8,128)(2,1)S(1)} %get-tuple-element.45.low, bf16[10,128,128]{2,1,0:T(8,128)(2,1)S(1)} %get-tuple-element.44.high, bf16[10,128,128]{2,1,0:T(8,128)(2,1)S(1)} %collective-permute-done.9.above, ...), custom_call_target="tpu_custom_call" | custom-call | flops 536870912 | bytes 1600512 | tf_op jit(solution)/shard_map/pallas_call | solution.py:32
  97.3 0.2 copy.21
  97.6 0.8 reshape.36
  98.4 4.2 %all-to-all-done.3.lines = bf16[32,9,2,128]{3,2,1,0:T(2,128)(2,1)S(1)} async-done(((bf16[32,9,2,128]{3,2,1,0:T(2,128)(2,1)}), bf16[32,9,2,128]{3,2,1,0:T(2,128)(2,1)S(1)}, u32[]{:S(2)}, u32[]{:S(2)}) %all-to-all-start.3) | async-done | bytes 147488 | tf_op jit(solution)/shard_map/all_to_all | solution.py:430
  102.6 0.9 shard_map.76
  (4 shorter events, 0.1 us)
Async XLA Ops:
  0.6 22.4 %copy-start = (bf16[3,3,3,32,16]{3,4,2,1,0:T(8,128)(2,1)S(1)}, bf16[3,3,3,32,16]{3,4,2,1,0:T(8,128)(2,1)}, u32[]{:S(2)}) copy-start(bf16[3,3,3,32,16]{3,4,2,1,0:T(8,128)(2,1)} %param.5) | copy-start | bytes 82948
  1.8 6.4 %collective-permute-start = (bf16[7,2,16,256]{3,2,1,0:T(8,128)(2,1)S(1)}, bf16[7,2,16,256]{3,2,1,0:T(8,128)(2,1)S(1)}, u32[]{:S(2)}, u32[]{:S(2)}) collective-permute-start(bf16[7,2,16,256]{3,2,1,0:T(8,128)(2,1)S(1)} %get-tuple-element.28), channel_id=1, source_target_pairs={{0,1},{1,0},{2,3},{3,2},{4,5},{5,4},{6,7},{7,6},{8,9},{9,8},{10,11... | collective-permute-start | bytes 344072 | tf_op jit(solution)/shard_map/ppermute | solution.py:425
  5.8 10.3 %collective-permute-start.1 = (bf16[7,2,16,256]{3,2,1,0:T(8,128)(2,1)S(1)}, bf16[7,2,16,256]{3,2,1,0:T(8,128)(2,1)S(1)}, u32[]{:S(2)}, u32[]{:S(2)}) collective-permute-start(bf16[7,2,16,256]{3,2,1,0:T(8,128)(2,1)S(1)} %get-tuple-element.30), channel_id=1, source_target_pairs={{1,2},{3,4},{5,6},{2,1},{4,3},{6,5},{9,10},{11,12},{13,14},{10,9},... | collective-permute-start | bytes 344072 | tf_op jit(solution)/shard_map/ppermute | solution.py:424
  8.3 15.7 %all-to-all-start = ((bf16[8,8,2432]{2,1,0:T(8,128)(2,1)}), bf16[8,8,2432]{2,1,0:T(8,128)(2,1)S(1)}, u32[]{:S(2)}, u32[]{:S(2)}) async-start(bf16[8,8,2432]{2,1,0:T(8,128)(2,1)} %shard_map.67), calls=%async_computation | async-start | bytes 622592 | tf_op jit(solution)/shard_map/all_to_all | solution.py:430
  16.2 9.1 %collective-permute-start.2 = (bf16[30,16,256]{2,1,0:T(8,128)(2,1)S(1)}, bf16[30,16,256]{2,1,0:T(8,128)(2,1)S(1)}, u32[]{:S(2)}, u32[]{:S(2)}) collective-permute-start(bf16[30,16,256]{2,1,0:T(8,128)(2,1)S(1)} %get-tuple-element.31), channel_id=1, source_target_pairs={{8,16},{24,32},{40,48},{56,64},{72,80},{88,96},{104,112},{120,128}... | collective-permute-start | bytes 737288 | tf_op jit(solution)/shard_map/ppermute | solution.py:424
  21.1 4.2 %collective-permute-start.3 = (bf16[30,16,256]{2,1,0:T(8,128)(2,1)S(1)}, bf16[30,16,256]{2,1,0:T(8,128)(2,1)S(1)}, u32[]{:S(2)}, u32[]{:S(2)}) collective-permute-start(bf16[30,16,256]{2,1,0:T(8,128)(2,1)S(1)} %get-tuple-element.32), channel_id=1, source_target_pairs={{0,8},{8,0},{16,24},{24,16},{32,40},{40,32},{48,56},{56,48},{64,72... | collective-permute-start | bytes 737288 | tf_op jit(solution)/shard_map/ppermute | solution.py:425
  27.8 7.3 %collective-permute-start.5 = (bf16[14,32,128]{2,1,0:T(8,128)(2,1)S(1)}, bf16[14,32,128]{2,1,0:T(8,128)(2,1)S(1)}, u32[]{:S(2)}, u32[]{:S(2)}) collective-permute-start(bf16[14,32,128]{2,1,0:T(8,128)(2,1)S(1)} %get-tuple-element.35.own), channel_id=1, source_target_pairs={{8,16},{24,32},{40,48},{56,64},{72,80},{88,96},{104,112},{120,128}... | collective-permute-start | bytes 344072 | tf_op jit(solution)/shard_map/ppermute | solution.py:424
  32.6 3.2 %collective-permute-start.4 = (bf16[14,32,128]{2,1,0:T(8,128)(2,1)S(1)}, bf16[14,32,128]{2,1,0:T(8,128)(2,1)S(1)}, u32[]{:S(2)}, u32[]{:S(2)}) collective-permute-start(bf16[14,32,128]{2,1,0:T(8,128)(2,1)S(1)} %get-tuple-element.35.own), channel_id=1, source_target_pairs={{0,8},{8,0},{16,24},{24,16},{32,40},{40,32},{48,56},{56,48},{64,72... | collective-permute-start | bytes 344072 | tf_op jit(solution)/shard_map/ppermute | solution.py:425
  37.2 6.2 %collective-permute-start.6 = (bf16[10,32,128]{2,1,0:T(8,128)(2,1)S(1)}, bf16[10,32,128]{2,1,0:T(8,128)(2,1)S(1)}, u32[]{:S(2)}, u32[]{:S(2)}) collective-permute-start(bf16[10,32,128]{2,1,0:T(8,128)(2,1)S(1)} %get-tuple-element.37), channel_id=1, source_target_pairs={{8,16},{24,32},{40,48},{56,64},{72,80},{88,96},{104,112},{120,128}... | collective-permute-start | bytes 245768 | tf_op jit(solution)/shard_map/ppermute | solution.py:424
  40.8 3.2 %collective-permute-start.7 = (bf16[10,32,128]{2,1,0:T(8,128)(2,1)S(1)}, bf16[10,32,128]{2,1,0:T(8,128)(2,1)S(1)}, u32[]{:S(2)}, u32[]{:S(2)}) collective-permute-start(bf16[10,32,128]{2,1,0:T(8,128)(2,1)S(1)} %get-tuple-element.39), channel_id=1, source_target_pairs={{0,8},{8,0},{16,24},{24,16},{32,40},{40,32},{48,56},{56,48},{64,72... | collective-permute-start | bytes 245768 | tf_op jit(solution)/shard_map/ppermute | solution.py:425
  69.2 18.9 %all-to-all-start.2 = ((bf16[16,9,2,128]{3,2,1,0:T(2,128)(2,1)}), bf16[16,9,2,128]{3,2,1,0:T(2,128)(2,1)S(1)}, u32[]{:S(2)}, u32[]{:S(2)}) async-start(bf16[16,9,2,128]{3,2,1,0:T(2,128)(2,1)} %broadcast_in_dim.4), calls=%async_computation.2 | async-start | bytes 147456 | tf_op jit(solution)/shard_map/all_to_all | solution.py:430
  76.4 18.3 %collective-permute-start.8 = (bf16[10,128,128]{2,1,0:T(8,128)(2,1)S(1)}, bf16[10,128,128]{2,1,0:T(8,128)(2,1)S(1)}, u32[]{:S(2)}, u32[]{:S(2)}) collective-permute-start(bf16[10,128,128]{2,1,0:T(8,128)(2,1)S(1)} %get-tuple-element.44.high), channel_id=1, source_target_pairs={{0,8},{8,16},{16,24},{24,32},{32,40},{40,48},{48,56},{56,64},{64,7... | collective-permute-start | bytes 983048 | tf_op jit(solution)/shard_map/ppermute | solution.py:415
  80.8 13.9 %collective-permute-start.9 = (bf16[10,128,128]{2,1,0:T(8,128)(2,1)S(1)}, bf16[10,128,128]{2,1,0:T(8,128)(2,1)S(1)}, u32[]{:S(2)}, u32[]{:S(2)}) collective-permute-start(bf16[10,128,128]{2,1,0:T(8,128)(2,1)S(1)} %get-tuple-element.45.low), channel_id=1, source_target_pairs={{8,0},{16,8},{24,16},{32,24},{40,32},{48,40},{56,48},{64,56},{72,6... | collective-permute-start | bytes 983048 | tf_op jit(solution)/shard_map/ppermute | solution.py:416
  88.9 13.7 %all-to-all-start.3 = ((bf16[32,9,2,128]{3,2,1,0:T(2,128)(2,1)}), bf16[32,9,2,128]{3,2,1,0:T(2,128)(2,1)S(1)}, u32[]{:S(2)}, u32[]{:S(2)}) async-start(bf16[32,9,2,128]{3,2,1,0:T(2,128)(2,1)} %broadcast_in_dim.5), calls=%async_computation.3 | async-start | bytes 294912 | tf_op jit(solution)/shard_map/all_to_all | solution.py:430
